TPU v7x, 512 devices: a whole 4x4x16 slice. The times are simulated.
512 devices in a mesh: context: 64 (over y, z), tensor: 8 (over x, core).
Axes of the slice: x: 4, y: 4, z: 16, core: 2. Of those that a mesh axis runs over, the one named last changes fastest.
Arguments:
- tokens: bfloat16 [8192, 8192], P('context', 'tensor'), may hold values from -6 to 6
- grad_out: bfloat16 [8192, 8192], P('context', 'tensor'), may hold values from -6 to 6
- keep_count: int32 [64], P('context'), may hold values from 1 to 6, as said below
- keep_pos: int32 [64, 6], P('context'), may hold values from 0 to 127, as said below
- router: bfloat16 [64, 6], P('context'), may hold values from 0.19921875 to 1
- gate_weight: bfloat16 [16384, 8192], P(('tensor', 'context')), may hold values from -0.25 to 0.25
- up_weight: bfloat16 [16384, 8192], P(('tensor', 'context')), may hold values from -0.25 to 0.25
- down_weight: bfloat16 [16384, 8192], P(('tensor', 'context')), may hold values from -0.046875 to 0.046875
Outputs:
- grad_tokens: bfloat16 [8192, 8192], P('context', 'tensor')
- grad_gate: bfloat16 [16384, 8192], P(('tensor', 'context'))
- grad_up: bfloat16 [16384, 8192], P(('tensor', 'context'))
- grad_down: bfloat16 [16384, 8192], P(('tensor', 'context'))
- kept_grad: float32 [128, 8192], P(None, 'tensor')
Inputs may be any that keep to these rules, and one draw needn't show every extreme that they name: keep_count sums to 128; the first 12 shards keep exactly 6 rows each, every other shard keeps 1 to 5 rows. `keep_pos`: the 6 positions in one row are distinct; only the first keep_count[c] of row c are used.
All inputs are finite; a program needn't handle non-finite values.
Results may differ from a plain program's by a relative error of at most 0.009.
Values may be sent and summed in bfloat16 or wider, within the bound.
No kernel may reach another device: no remote copies, remote signals or barrier semaphores. Data moves between devices by JAX's collectives and lax.ppermute only.
A program may use at most 128 MiB of HBM per device.

v0:
```python
import jax
import jax.numpy as jnp
from jax import lax
from jax.sharding import PartitionSpec as P

CAP = 2


def compact_index(counts, most_rows, kept_total):
    starts = (jnp.cumsum(counts) - counts).astype(jnp.int32)
    wanted = jnp.arange(kept_total, dtype=jnp.int32)
    owner_shard = jnp.sum((starts[None, :] <= wanted[:, None]).astype(jnp.int32), axis=1) - 1
    offset = wanted - jnp.take(starts, owner_shard)
    return (starts, owner_shard * most_rows + offset)


def body(tokens, grad_out, keep_count, keep_pos, router, gate_weight, up_weight, down_weight):
    tok_dev, part_width = tokens.shape
    most_rows = keep_pos.shape[1]
    ncontext = lax.axis_size("context")
    ntensor = lax.axis_size("tensor")
    kept_total = CAP * ncontext
    row_ids = jnp.arange(most_rows, dtype=jnp.int32)
    live_rows = row_ids < keep_count[0]
    matches = (keep_pos[0][:, None] == jnp.arange(tok_dev, dtype=jnp.int32)[None, :]) & live_rows[
        :, None
    ]
    picker = jnp.where(matches, 1.0, 0.0).astype(jnp.float32)
    picker_low = picker.astype(jnp.bfloat16)
    x_rows = jnp.dot(picker_low, tokens, preferred_element_type=jnp.float32).astype(jnp.bfloat16)
    dy_rows = jnp.dot(picker_low, grad_out, preferred_element_type=jnp.float32).astype(jnp.bfloat16)
    full_x, full_dy = (
        lax.all_gather(x_rows, "tensor", axis=1, tiled=True),
        lax.all_gather(dy_rows, "tensor", axis=1, tiled=True),
    )
    padded_x, padded_dy, padded_router, counts = (
        lax.all_gather(full_x, "context", axis=0, tiled=True),
        lax.all_gather(full_dy, "context", axis=0, tiled=True),
        lax.all_gather(router, "context", axis=0, tiled=True),
        lax.all_gather(keep_count, "context", axis=0, tiled=True),
    )
    starts, source = compact_index(counts, most_rows, kept_total)
    kept_x = jnp.take(padded_x, source, axis=0)
    kept_dy = jnp.take(padded_dy, source, axis=0)
    row_scale = jnp.take(padded_router.reshape(-1), source).astype(jnp.float32)[:, None]
    gate_pre = jnp.einsum("kd,fd->kf", kept_x, gate_weight, preferred_element_type=jnp.float32)
    up_pre = jnp.einsum("kd,fd->kf", kept_x, up_weight, preferred_element_type=jnp.float32)
    sigmoid_gate = jax.nn.sigmoid(gate_pre)
    activated = gate_pre * sigmoid_gate
    hidden = (activated * up_pre).astype(jnp.bfloat16)
    back_proj = jnp.einsum("kd,fd->kf", kept_dy, down_weight, preferred_element_type=jnp.float32)
    hidden_grad = row_scale * back_proj
    gate_grad = (
        hidden_grad * sigmoid_gate * (1.0 + gate_pre * (1.0 - sigmoid_gate)) * up_pre
    ).astype(jnp.bfloat16)
    up_grad = (hidden_grad * activated).astype(jnp.bfloat16)
    scaled_dy = (row_scale * kept_dy.astype(jnp.float32)).astype(jnp.bfloat16)
    grad_down = jnp.einsum(
        "kf,kd->fd", hidden, scaled_dy, preferred_element_type=jnp.float32
    ).astype(jnp.bfloat16)
    grad_gate = jnp.einsum(
        "kf,kd->fd", gate_grad, kept_x, preferred_element_type=jnp.float32
    ).astype(jnp.bfloat16)
    grad_up = jnp.einsum("kf,kd->fd", up_grad, kept_x, preferred_element_type=jnp.float32).astype(
        jnp.bfloat16
    )
    partial_grad = jnp.einsum(
        "kf,fd->kd", gate_grad, gate_weight, preferred_element_type=jnp.float32
    ) + jnp.einsum("kf,fd->kd", up_grad, up_weight, preferred_element_type=jnp.float32)
    arranged = (
        partial_grad.reshape(ncontext, CAP, ntensor, part_width)
        .transpose(0, 2, 1, 3)
        .reshape(ncontext * ntensor * CAP, part_width)
    )
    own_block = lax.psum_scatter(arranged, ("context", "tensor"), scatter_dimension=0, tiled=True)
    summed = lax.all_gather(own_block, "context", axis=0, tiled=True)
    extended = jnp.concatenate([summed, jnp.zeros((most_rows, part_width), jnp.float32)], axis=0)
    start_here = jnp.take(starts, lax.axis_index("context"))
    own_rows = lax.dynamic_slice_in_dim(extended, start_here, most_rows, 0)
    added = jnp.dot(
        picker.T, own_rows, precision=lax.Precision.HIGHEST, preferred_element_type=jnp.float32
    )
    grad_tokens = (grad_out.astype(jnp.float32) + added).astype(jnp.bfloat16)
    return (grad_tokens, grad_gate, grad_up, grad_down, summed)


def solution(mesh):
    placed = (
        P("context", "tensor"),
        P("context", "tensor"),
        P("context"),
        P("context", None),
        P("context", None),
        P(("tensor", "context"), None),
        P(("tensor", "context"), None),
        P(("tensor", "context"), None),
    )
    return jax.shard_map(
        body,
        mesh=mesh,
        in_specs=placed,
        out_specs=(
            P("context", "tensor"),
            P(("tensor", "context"), None),
            P(("tensor", "context"), None),
            P(("tensor", "context"), None),
            P(None, "tensor"),
        ),
        check_vma=False,
    )
```

profile of v0, /device:TPU:6, one launch (start us, length us, event | category | flops | bytes accessed | tf_op | source)
XLA Modules:
  0.0 970.5 jit_solution(6930636405323159802)
XLA Ops:
  7.2 0.0 copy-start
  7.2 0.0 all-gather.7.cloned.1.call-start
  7.9 1.2 convolution_convert_fusion.4
  9.1 16.5 %all_gather.23 = bf16[6,8192]{1,0:T(8,128)(2,1)} all-gather(bf16[6,1024]{1,0:T(8,128)(2,1)S(1)} %convolution_convert_fusion.4), channel_id=1, replica_groups=mesh['context'=64,'tensor'=8] {'tensor'}, dimensions={1}, use_global_device_ids=true | all-gather | bytes 110592 | tf_op jit(solution)/shard_map/all_gather | solution.py:34
  25.6 0.0 all-gather.7.cloned.1.call-update
  25.6 0.0 all-gather.9.cloned.1.call-start
  25.7 1.2 convolution_convert_fusion.3
  26.8 14.1 %all_gather.25 = bf16[6,8192]{1,0:T(8,128)(2,1)} all-gather(bf16[6,1024]{1,0:T(8,128)(2,1)S(1)} %convolution_convert_fusion.3), channel_id=1, replica_groups=mesh['context'=64,'tensor'=8] {'tensor'}, dimensions={1}, use_global_device_ids=true | all-gather | bytes 110592 | tf_op jit(solution)/shard_map/all_gather | solution.py:33
  40.9 0.0 all-gather.9.cloned.1.call-update
  41.0 0.0 all-reduce.5.cloned.1.call-start
  41.0 1.3 dynamic-slice.3
  42.3 0.8 dynamic-update-slice.1
  43.0 31.6 %all-reduce.1 = s32[64]{0:T(128)S(1)} all-reduce(s32[64]{0:T(128)S(1)} %dynamic-update-slice.1), channel_id=1, replica_groups=mesh['context'=64,'tensor'=8] {'context'}, use_global_device_ids=true, to_apply=%add.1 | all-reduce | flops 64 | bytes 512
  74.6 0.1 copy.18
  74.7 0.1 reduce-window.9
  74.8 0.1 reduce
  75.0 0.1 convert_reduce_fusion
  75.1 1.2 gather_fusion
  76.3 71.5 %all-gather = bf16[64,1,6]{2,1,0:T(2,128)(2,1)S(1)} all-gather(bf16[1,1,6]{2,1,0:T(2,128)(2,1)} %bitcast.59), channel_id=1, replica_groups=mesh['context'=64,'tensor'=8] {'context'}, dimensions={0}, use_global_device_ids=true | all-gather | bytes 780 | tf_op jit(solution)/shard_map/all_gather | solution.py:39
  147.8 0.1 reduce.1
  147.9 0.1 reshape.146
  148.1 1.3 gather_fusion.1
  149.4 35.2 %all-gather.7.cloned.1.call-done = bf16[64,6,8192]{2,1,0:T(8,128)(2,1)} async-done(((bf16[1,6,8192]{2,1,0:T(8,128)(2,1)}), bf16[64,6,8192]{2,1,0:T(8,128)(2,1)}) %all-gather.7.cloned.1.call-update) | async-done | bytes 6291472 | tf_op jit(solution)/shard_map/all_gather | solution.py:38
  184.5 9.1 reshape.218
  193.7 7.4 gather_fusion.2
  201.0 138.4 %all-gather.9.cloned.1.call-done = bf16[64,6,8192]{2,1,0:T(8,128)(2,1)} async-done(((bf16[1,6,8192]{2,1,0:T(8,128)(2,1)}), bf16[64,6,8192]{2,1,0:T(8,128)(2,1)}) %all-gather.9.cloned.1.call-update) | async-done | bytes 6291472 | tf_op jit(solution)/shard_map/all_gather | solution.py:37
  339.4 9.1 reshape.220
  348.5 0.0 copy-start.4
  348.5 8.7 gather_fusion.3
  357.2 0.0 copy-done.4
  357.2 0.0 copy-start.2
  357.2 2.6 fusion.34
  359.8 0.0 copy-done
  359.8 0.0 copy-done.2
  359.9 0.0 copy-start.7
  359.9 0.8 fusion.35
  360.7 0.2 copy-done.7
  360.9 0.9 multiply_convert_fusion.3
  361.8 0.7 fusion.36
  362.5 0.7 convolution_add_fusion
  363.3 3.3 copy.20
  366.5 6.0 copy.22
  372.5 6.1 reshape.148
  378.6 0.0 all-reduce.5.cloned.1.call-update
  378.6 0.6 dynamic-slice.2
  379.9 0.0 copy-start.3
  379.9 3.0 convolution_convert_fusion.1
  382.9 0.0 copy-done.3
  382.9 1.3 convolution_convert_fusion.2
  384.2 0.0 copy-start.5
  384.2 0.0 copy-start.6
  384.2 1.6 convolution_convert_fusion
  385.9 477.8 %all-reduce.5.cloned.1.call-done = f32[1024,1024]{1,0:T(8,128)} async-done(((f32[1024,1024]{1,0:T(8,128)}), f32[1024,1024]{1,0:T(8,128)}) %all-reduce.5.cloned.1.call-update) | async-done | bytes 4194320
  863.7 0.8 dynamic-slice_bitcast_fusion
  864.4 97.7 %all-gather.3 = f32[64,2,1024]{2,1,0:T(2,128)S(1)} all-gather(f32[1,2,1024]{2,1,0:T(2,128)S(1)} %dynamic-slice_bitcast_fusion), channel_id=1, replica_groups=mesh['context'=64,'tensor'=8] {'context'}, dimensions={0}, use_global_device_ids=true | all-gather | bytes 532480 | tf_op jit(solution)/shard_map/all_gather | solution.py:76
  962.2 0.4 reshape.222
  962.5 0.0 copy-done.5
  962.6 0.0 copy-done.6
  962.6 0.0 copy-start.1
  962.6 1.4 fusion.1
  964.0 0.0 copy-done.1
  (10 shorter events, 0.1 us)
Async XLA Ops:
  7.2 352.7 %copy-start = (bf16[32,8192]{1,0:T(8,128)(2,1)S(1)}, bf16[32,8192]{1,0:T(8,128)(2,1)}, u32[]{:S(2)}) copy-start(bf16[32,8192]{1,0:T(8,128)(2,1)} %param.15) | copy-start | bytes 1572868
  7.2 177.4 %all-gather.7.cloned.1.call-start = ((), (), s32[]{:S(2)}) async-start(), calls=%async_computation | async-start | bytes 8519680 | tf_op jit(solution)/shard_map/all_gather | solution.py:38
  25.6 313.8 %all-gather.9.cloned.1.call-start = ((), (), s32[]{:S(2)}) async-start(), calls=%async_computation.1 | async-start | bytes 8519680 | tf_op jit(solution)/shard_map/all_gather | solution.py:37
  41.0 822.7 %all-reduce.5.cloned.1.call-start = ((), (), s32[]{:S(2)}) async-start(), calls=%async_computation.2 | async-start | bytes 8388608
  348.5 8.7 copy-start.4
  357.2 2.6 copy-start.2
  359.9 1.0 copy-start.7
  379.9 3.0 copy-start.3
  384.2 578.3 %copy-start.5 = (bf16[128,1024]{1,0:T(8,128)(2,1)S(1)}, bf16[128,1024]{1,0:T(8,128)(2,1)}, u32[]{:S(2)}) copy-start(bf16[128,1024]{1,0:T(8,128)(2,1)} %param.11) | copy-start | bytes 786436
  384.2 578.3 %copy-start.6 = (s32[1,6]{1,0:T(1,128)S(1)}, s32[1,6]{1,0:T(1,128)}, u32[]{:S(2)}) copy-start(s32[1,6]{1,0:T(1,128)} %param.13) | copy-start | bytes 76
  962.6 1.4 copy-start.1
Sparse Core Ops, SparseCore 0:
  25.7 158.7 all-gather.6
  187.5 151.8 all-gather.8
  378.7 484.8 all-reduce.4
where the time goes:
time: 972 us; the launch traced here: 971 us
  waiting for transfers between devices  651 us (67%)
  blocking collectives  231 us (24%)
  local copies, waits for them, and re-layouts  56.4 us (6%)
  matrix products  15.5 us (2%)
  between operations  15.3 us (2%)
    unnamed x4, waiting for transfers between devices  478 us
    all_gather x1, waiting for transfers between devices, body(): lax.all_gather(full_x, 'context', axis=0, tiled=True)  138 us
    all_gather x1, blocking collectives, body(): summed = lax.all_gather(own_block, 'context', axis=0, tiled=True)  97.7 us
    all_gather x1, blocking collectives, body(): lax.all_gather(router, 'context', axis=0, tiled=True)  71.5 us
    all_gather x1, waiting for transfers between devices, body(): lax.all_gather(full_dy, 'context', axis=0, tiled=True)  35.2 us
    unnamed x1, blocking collectives  31.6 us
    unnamed x24, local copies, waits for them, and re-layouts  24.9 us
  transfers between devices with their start and end apart: 3, of which 3 were waited for; matrix products, arithmetic and copies ran while one was open for 3% of the time, Pallas kernels for 0%

commit v1 on v0

v1 whole, which is shorter than its diff:
```python
import jax
import jax.numpy as jnp
from jax import lax
from jax.sharding import Mesh, PartitionSpec as P

NY, NZ, NX, NC = 4, 16, 4, 2
HEAVY = 12
MOST = 6
PLANE = 35
KEPT = 128
BF = jnp.bfloat16
F32 = jnp.float32


def one_hot_rows(hot, rows):
    return jnp.dot(hot.astype(BF), rows, preferred_element_type=F32).astype(BF)


def spread(piece, axes, n):
    return lax.all_to_all(
        jnp.broadcast_to(piece[None], (n,) + piece.shape), axes, 0, 0, tiled=True
    )


def body(tokens, grad_out, keep_count, keep_pos, router, gate_weight, up_weight, down_weight):
    tok_dev, width = tokens.shape
    yi, zi, ci = lax.axis_index("y"), lax.axis_index("z"), lax.axis_index("core")
    shard = yi * NZ + zi

    j8 = jnp.arange(8, dtype=jnp.int32)
    live = j8 < keep_count[0]
    pos8 = jnp.pad(keep_pos[0], (0, 8 - MOST))
    picker = (pos8[:, None] == jnp.arange(tok_dev)[None, :]) & live[:, None]
    lane = jnp.arange(128)[None, :]
    weight8 = jnp.pad(router[0], (0, 8 - MOST)).astype(F32)[:, None]
    meta = jnp.where(lane == 0, weight8, 0.0)
    meta = jnp.where(lane == 1, 1.0, meta)
    meta = jnp.where(lane == 2, shard.astype(F32), meta)
    meta = jnp.where(lane == 3, j8.astype(F32)[:, None], meta)
    meta = jnp.where(live[:, None], meta, 0.0).astype(BF)
    x_rows = jnp.concatenate([one_hot_rows(picker, tokens), meta], axis=1)
    dy_rows = jnp.concatenate([one_hot_rows(picker, grad_out), meta], axis=1)
    column = spread(jnp.concatenate([x_rows, dy_rows], axis=0), "y", NY)

    column = column.reshape(NY, 2, 8, width + 128)
    q = jnp.arange(32)
    qy, qj = q // 8, q % 8
    col_valid = column[:, 0, :, width + 1].reshape(32) > 0.5
    steady = jnp.where(
        zi < HEAVY,
        jnp.where(qy == 0, jnp.where(qj < MOST, qj, 99), jnp.where(qj == 0, 5 + qy, 99)),
        jnp.where(qj == 0, qy, 99),
    )
    extra = col_valid & (qj >= 1) & ((qy > 0) | (zi >= HEAVY))
    nth = jnp.sum((q[None, :] < q[:, None]) & extra[None, :], axis=1)
    p4 = jnp.arange(4)[:, None]
    hot = jnp.where(
        p4 < 3,
        steady[None, :] == 4 * p4 + ((yi - zi) % 4),
        extra[None, :] & (nth[None, :] == yi),
    )
    picked = jnp.concatenate(
        [
            one_hot_rows(hot, column[:, 0].reshape(32, width + 128)),
            one_hot_rows(hot, column[:, 1].reshape(32, width + 128)),
        ],
        axis=0,
    )
    plane = spread(picked, "z", NZ).reshape(NZ, 2, 4, width + 128)

    p_valid = plane[:, 0, :, width + 1].reshape(64) > 0.5
    i64 = jnp.arange(64)
    rank = jnp.sum((i64[None, :] < i64[:, None]) & p_valid[None, :], axis=1)
    hot = (rank[None, :] == jnp.arange(PLANE)[:, None]) & p_valid[None, :]
    px = plane[:, 0].reshape(64, width + 128)
    pd = plane[:, 1].reshape(64, width + 128)
    facts = jnp.einsum(
        "mv,tm->vt", px[:, width : width + 4], hot.astype(BF), preferred_element_type=F32
    ).astype(BF)
    facts = jnp.pad(facts, ((0, 0), (0, 128 - PLANE))).reshape(1, 512)
    packed = jnp.concatenate(
        [
            one_hot_rows(hot, px[:, :width]),
            one_hot_rows(hot, pd[:, :width]),
            jnp.pad(facts, ((0, 1), (0, width - 512))),
        ],
        axis=0,
    )
    everything = spread(packed, ("y", "x"), NY * NX).reshape(NY, NX, 2 * PLANE + 2, width)

    facts = everything[:, 0, 2 * PLANE, :512].reshape(NY, 4, 128)[:, :, :PLANE].astype(F32)
    facts = facts.transpose(1, 0, 2).reshape(4, NY * PLANE)
    valid = facts[1] > 0.5
    key = facts[2] * 8 + facts[3]
    slot = jnp.sum((key[None, :] < key[:, None]) & valid[None, :], axis=1)
    hot = (slot[None, :] == jnp.arange(KEPT)[:, None]) & valid[None, :]
    row_scale = jnp.sum(jnp.where(hot, facts[0][None, :], 0.0), axis=1, keepdims=True)
    start_here = jnp.sum((valid & (facts[2] < shard.astype(F32))).astype(jnp.int32))

    def ordered(part):
        part = part.transpose(0, 2, 1, 3).reshape(NY * PLANE, NX * width)
        return one_hot_rows(hot, part)

    own = jnp.stack(
        [ordered(everything[:, :, :PLANE]), ordered(everything[:, :, PLANE : 2 * PLANE])]
    ).reshape(2, KEPT, NX, 1, width)
    other = lax.ppermute(own, "core", [(0, 1), (1, 0)])
    kept = jnp.concatenate(
        [jnp.where(ci == 0, own, other), jnp.where(ci == 0, other, own)], axis=3
    ).reshape(2, KEPT, NX * NC * width)
    kept_x, kept_dy = kept[0], kept[1]

    gate_pre = jnp.einsum("kd,fd->kf", kept_x, gate_weight, preferred_element_type=F32)
    up_pre = jnp.einsum("kd,fd->kf", kept_x, up_weight, preferred_element_type=F32)
    sigmoid_gate = jax.nn.sigmoid(gate_pre)
    activated = gate_pre * sigmoid_gate
    hidden = (activated * up_pre).astype(BF)
    back_proj = jnp.einsum("kd,fd->kf", kept_dy, down_weight, preferred_element_type=F32)
    hidden_grad = row_scale * back_proj
    gate_grad = (
        hidden_grad * sigmoid_gate * (1.0 + gate_pre * (1.0 - sigmoid_gate)) * up_pre
    ).astype(BF)
    up_grad = (hidden_grad * activated).astype(BF)
    scaled_dy = (row_scale * kept_dy.astype(F32)).astype(BF)

    partial = jnp.einsum("kf,fd->kd", gate_grad, gate_weight, preferred_element_type=F32)
    partial = partial + jnp.einsum("kf,fd->kd", up_grad, up_weight, preferred_element_type=F32)
    partial = partial.reshape(KEPT, NX, NC, width)
    mine = lax.dynamic_index_in_dim(partial, ci, 2, keepdims=False)
    theirs = lax.dynamic_index_in_dim(partial, 1 - ci, 2, keepdims=False).astype(BF)
    came = lax.ppermute(theirs, "core", [(0, 1), (1, 0)])

    grad_down = jnp.einsum("kf,kd->fd", hidden, scaled_dy, preferred_element_type=F32).astype(BF)
    grad_gate = jnp.einsum("kf,kd->fd", gate_grad, kept_x, preferred_element_type=F32).astype(BF)
    grad_up = jnp.einsum("kf,kd->fd", up_grad, kept_x, preferred_element_type=F32).astype(BF)

    chip = (mine + came.astype(F32)).astype(BF)
    chip = chip.reshape(NY, KEPT // NY, NX, width).transpose(0, 2, 1, 3)
    chip = chip.reshape(NY * NX, KEPT // NY, width)
    chip = lax.all_to_all(chip, ("y", "x"), 0, 0, tiled=True)
    quarter = jnp.sum(chip.astype(F32), axis=0).astype(BF)
    rows, cols = KEPT // NY // 4, width // 4
    quarter = quarter.reshape(4, rows, 4, cols).transpose(0, 2, 1, 3).reshape(NZ, rows, cols)
    quarter = lax.all_to_all(quarter, "z", 0, 0, tiled=True)
    block = jnp.sum(quarter.astype(F32), axis=0).astype(BF)
    quarter = spread(block, "z", NZ).reshape(4, 4, rows, cols).transpose(0, 2, 1, 3)
    summed = spread(quarter.reshape(KEPT // NY, width), "y", NY).reshape(KEPT, width)
    summed = summed.astype(F32)

    extended = jnp.concatenate([summed, jnp.zeros((8, width), F32)], axis=0)
    own_rows = lax.dynamic_slice_in_dim(extended, start_here, 8, 0)
    added = jnp.dot(
        picker.astype(F32).T,
        own_rows,
        precision=lax.Precision.HIGHEST,
        preferred_element_type=F32,
    )
    grad_tokens = (grad_out.astype(F32) + added).astype(BF)
    return (grad_tokens, grad_gate, grad_up, grad_down, summed)


def solution(mesh):
    grid = Mesh(mesh.devices.reshape(NY, NZ, NX, NC), ("y", "z", "x", "core"))
    context, tensor = ("y", "z"), ("x", "core")
    units = P(tensor + context, None)
    return jax.shard_map(
        body,
        mesh=grid,
        in_specs=(
            P(context, tensor),
            P(context, tensor),
            P(context),
            P(context, None),
            P(context, None),
            units,
            units,
            units,
        ),
        out_specs=(P(context, tensor), units, units, units, P(None, tensor)),
        check_vma=False,
    )
```

time: 972 us -> 214 us (0.22)
  waiting for transfers between devices: 651 us -> 48.7 us
  blocking collectives: 231 us -> 60.8 us
  starting transfers between devices: 0.12 us -> 34.2 us
  local copies, waits for them, and re-layouts: 56.4 us -> 34.5 us
  between operations: 15.3 us -> 3.69 us
    unnamed x4 -> x0, waiting for transfers between devices: 478 us -> none
    all_gather x4 -> x0, blocking collectives: 200 us -> none  [the longest x1 97.7 us: body(): summed = lax.all_gather(own_block, 'context', axis=0, tiled=True)]
    all_gather x2 -> x0, waiting for transfers between devices: 174 us -> none  [the longest x1 138 us: body(): lax.all_gather(full_x, 'context', axis=0, tiled=True)]
    all_to_all x0 -> x2, blocking collectives: none -> 60.8 us  [spread(): lax.all_to_all(jnp.broadcast_to(piece[None], (n,) + piece.shape), axes, 0...]
    all_to_all x0 -> x5, waiting for transfers between devices: none -> 44.7 us  [the longest x3 22.1 us: spread(): lax.all_to_all(jnp.broadcast_to(piece[None], (n,) + piece.shape), axes, 0...]
    unnamed x1 -> x0, blocking collectives: 31.6 us -> none
    all_to_all x0 -> x5, starting transfers between devices: none -> 30.1 us  [the longest x1 11.8 us: body(): quarter = lax.all_to_all(quarter, 'z', 0, 0, tiled=True)]
    unnamed x24 -> x21, local copies, waits for them, and re-layouts: 24.9 us -> 4.95 us
  transfers between devices with their start and end apart: 3 -> 7, of which waited for: 3 -> 6; matrix products, arithmetic and copies ran while one was open for 3% -> 6% of each run, Pallas kernels for 0% -> 0%
where the time goes in v1:
time: 214 us; the launch traced here: 211 us
  blocking collectives  60.8 us (28%)
  waiting for transfers between devices  48.7 us (23%)
  local copies, waits for them, and re-layouts  34.5 us (16%)
  starting transfers between devices  34.2 us (16%)
  matrix products  18.7 us (9%)
  other arithmetic  10.1 us (5%)
  between operations  3.69 us (2%)
    all_to_all x2, blocking collectives, spread(): lax.all_to_all(jnp.broadcast_to(piece[None], (n,) + piece.shape), axes, 0...  60.8 us
    all_to_all x3, waiting for transfers between devices, spread(): lax.all_to_all(jnp.broadcast_to(piece[None], (n,) + piece.shape), axes, 0...  22.1 us
    all_to_all x1, waiting for transfers between devices, body(): chip = lax.all_to_all(chip, ('y', 'x'), 0, 0, tiled=True)  12.9 us
    all_to_all x1, starting transfers between devices, body(): quarter = lax.all_to_all(quarter, 'z', 0, 0, tiled=True)  11.8 us
    all_to_all x3, starting transfers between devices, spread(): lax.all_to_all(jnp.broadcast_to(piece[None], (n,) + piece.shape), axes, 0...  11.6 us
    all_to_all x1, waiting for transfers between devices, body(): quarter = lax.all_to_all(quarter, 'z', 0, 0, tiled=True)  9.61 us
    all_to_all x1, starting transfers between devices, body(): chip = lax.all_to_all(chip, ('y', 'x'), 0, 0, tiled=True)  6.65 us
    reshape x1, local copies, waits for them, and re-layouts, body(): partial = partial.reshape(KEPT, NX, NC, width)  6.58 us
  transfers between devices with their start and end apart: 7, of which 6 were waited for; matrix products, arithmetic and copies ran while one was open for 6% of the time, Pallas kernels for 0%

profile of v1, /device:TPU:6, one launch (start us, length us, event | category | flops | bytes accessed | tf_op | source)
XLA Modules:
  0.0 210.8 jit_solution(8810821132652881101)
XLA Ops:
  1.4 0.7 pad_convert_fusion
  2.1 0.7 pad.17
  2.7 1.1 convolution_convert_fusion.9
  3.9 1.2 convolution_convert_fusion.10
  5.1 0.7 broadcast_in_dim.174
  5.8 4.5 %all-to-all-start = ((bf16[4,16,1152]{2,1,0:T(8,128)(2,1)}), bf16[4,16,1152]{2,1,0:T(8,128)(2,1)S(1)}, u32[]{:S(2)}, u32[]{:S(2)}) async-start(bf16[4,16,1152]{2,1,0:T(8,128)(2,1)} %broadcast_in_dim.174), calls=%async_computation | async-start | bytes 294912 | tf_op jit(solution)/shard_map/all_to_all | solution.py:20
  10.3 6.0 %all-to-all-done = bf16[4,16,1152]{2,1,0:T(8,128)(2,1)S(1)} async-done(((bf16[4,16,1152]{2,1,0:T(8,128)(2,1)}), bf16[4,16,1152]{2,1,0:T(8,128)(2,1)S(1)}, u32[]{:S(2)}, u32[]{:S(2)}) %all-to-all-start) | async-done | bytes 147488 | tf_op jit(solution)/shard_map/all_to_all | solution.py:20
  16.3 0.2 compare_reduce_fusion
  16.8 0.2 convolution_convert_fusion.5
  17.0 0.2 convolution_convert_fusion.6
  17.2 33.3 %all_to_all.35 = bf16[16,8,1152]{2,1,0:T(8,128)(2,1)S(1)} all-to-all(bf16[16,8,1152]{2,1,0:T(8,128)(2,1)S(1)} %broadcast_in_dim.176), channel_id=1, replica_groups=mesh['y'=4,'z'=16,'x'=4,'core'=2] {'z'}, dimensions={0} | all-to-all | bytes 589824 | tf_op jit(solution)/shard_map/all_to_all | solution.py:20
  50.7 0.2 copy.55
  51.2 0.2 convolution_convert_fusion.11
  51.4 0.1 convolution_convert_fusion.8
  51.7 0.1 convolution_convert_fusion.7
  51.9 0.3 broadcast_in_dim.177
  52.2 27.5 %all_to_all.36 = bf16[16,72,1024]{2,1,0:T(8,128)(2,1)S(1)} all-to-all(bf16[16,72,1024]{2,1,0:T(8,128)(2,1)S(1)} %broadcast_in_dim.177), channel_id=1, replica_groups=mesh['y'=4,'z'=16,'x'=4,'core'=2] {'y','x'}, dimensions={0} | all-to-all | bytes 4718592 | tf_op jit(solution)/shard_map/all_to_all | solution.py:20
  79.8 2.1 slice_bitcast_fusion.1
  82.0 2.2 %copy.58 = bf16[4,35,4,1024]{3,2,1,0:T(4,128)(2,1)S(1)} copy(bf16[4,35,4,1024]{3,1,2,0:T(8,128)(2,1)} %get-tuple-element.11) | data formatting | bytes 2293760 | tf_op jit(solution)/shard_map/transpose | solution.py:101
  84.3 0.4 pad.37
  84.7 0.4 copy.70
  85.2 0.2 convert_reduce_fusion
  85.4 1.6 convolution_convert_fusion.4
  86.9 1.6 copy.65
  88.6 0.9 copy.59
  89.5 0.4 pad.38
  89.9 0.4 copy.71
  90.4 1.6 convolution_convert_fusion.3
  91.9 1.6 copy.66
  93.6 1.5 pad_maximum_fusion.1
  95.1 2.1 collective-permute-start
  97.3 0.1 select_reduce_fusion
  97.4 4.1 %collective-permute-done = bf16[2,128,4,1,1024]{1,4,3,2,0:T(8,128)(2,1)} collective-permute-done((bf16[2,128,4,1,1024]{1,4,3,2,0:T(8,128)(2,1)}, bf16[2,128,4,1,1024]{1,4,3,2,0:T(8,128)(2,1)}, u32[]{:S(2)}, u32[]{:S(2)}) %collective-permute-start) | collective-permute-done | bytes 2097184 | tf_op jit(solution)/shard_map/ppermute | solution.py:107
  101.5 1.9 broadcast_select_fusion.1
  103.3 0.4 fusion
  103.8 0.4 fusion.56
  104.3 0.9 copy-done.3
  105.2 0.5 fusion.57
  105.7 0.5 multiply_convert_fusion.3
  106.2 0.7 fusion.55
  106.9 2.7 %convolution_add_fusion = f32[128,8192]{1,0:T(8,128)} fusion(f32[128,8192]{1,0:T(8,128)S(1)} %fusion.55, bf16[128,32]{0,1:T(8,128)(2,1)S(1)} %get-tuple-element.15, bf16[32,8192]{1,0:T(8,128)(2,1)S(1)} %copy-done.3), kind=kOutput, calls=%fused_computation | convolution fusion | flops 68157440 | bytes 8921088 | tf_op jit(solution)/shard_map/kf,fd->kd/dot_general | solution.py:127
  109.6 6.6 %reshape.216 = f32[128,4,2,1024]{3,2,1,0:T(2,128)} reshape(f32[128,8192]{1,0:T(8,128)} %convolution_add_fusion) | data formatting | bytes 8388608 | tf_op jit(solution)/shard_map/reshape | solution.py:128
  116.2 4.4 %constant_dynamic-slice_fusion = bf16[128,4,1,1024]{3,2,1,0:T(2,128)(2,1)S(1)} fusion(f32[128,4,2,1024]{3,2,1,0:T(2,128)} %reshape.216, s32[]{:T(128)S(6)} %select_n.157), kind=kLoop, calls=%fused_computation.113 | loop fusion | bytes 2097156 | tf_op jit(solution)/shard_map/jit(dynamic_index_in_dim)/dynamic_slice | solution.py:130
  120.6 2.1 copy.79
  122.7 2.0 collective-permute-start.1
  124.8 4.4 %constant_dynamic-slice_fusion.1 = f32[128,4,1,1024]{3,2,1,0:T(1,128)S(1)} fusion(f32[128,4,2,1024]{3,2,1,0:T(2,128)} %reshape.216, s32[]{:T(128)S(6)} %select_n.156), kind=kLoop, calls=%fused_computation.114 | loop fusion | bytes 4194308 | tf_op jit(solution)/shard_map/jit(dynamic_index_in_dim)/dynamic_slice | solution.py:129
  129.2 2.4 %fusion.1 = bf16[128,4,1024]{2,0,1:T(8,128)(2,1)S(1)} fusion(f32[128,4,1,1024]{3,2,1,0:T(1,128)S(1)} %constant_dynamic-slice_fusion.1, bf16[128,4,1024]{2,0,1:T(8,128)(2,1)} %collective-permute-done.1), kind=kLoop, calls=%fused_computation.16 | loop fusion | flops 1572864 | bytes 4194304 | tf_op jit(solution)/shard_map/convert_element_type | solution.py:137
  131.6 1.1 copy.64
  132.7 6.7 %all-to-all-start.3 = ((bf16[16,32,1024]{2,1,0:T(8,128)(2,1)}), bf16[16,32,1024]{2,1,0:T(8,128)(2,1)}, u32[]{:S(2)}, u32[]{:S(2)}) async-start(bf16[16,32,1024]{2,1,0:T(8,128)(2,1)} %bitcast.105), calls=%async_computation.3 | async-start | bytes 2097152 | tf_op jit(solution)/shard_map/all_to_all | solution.py:140
  139.4 0.6 fusion.42
  142.0 12.9 %all-to-all-done.3 = bf16[16,32,1024]{2,1,0:T(8,128)(2,1)} async-done(((bf16[16,32,1024]{2,1,0:T(8,128)(2,1)}), bf16[16,32,1024]{2,1,0:T(8,128)(2,1)}, u32[]{:S(2)}, u32[]{:S(2)}) %all-to-all-start.3) | async-done | bytes 1048608 | tf_op jit(solution)/shard_map/all_to_all | solution.py:140
  154.9 2.1 reduce_sum.73
  156.9 11.8 %all-to-all-start.4 = ((bf16[16,8,256]{2,1,0:T(8,128)(2,1)}), bf16[16,8,256]{2,1,0:T(8,128)(2,1)S(1)}, u32[]{:S(2)}, u32[]{:S(2)}) async-start(bf16[16,8,256]{2,1,0:T(8,128)(2,1)} %bitcast.22), calls=%async_computation.4 | async-start | bytes 131072 | tf_op jit(solution)/shard_map/all_to_all | solution.py:144
  168.8 3.2 %convolution_convert_fusion = bf16[32,8192]{1,0:T(8,128)(2,1)} fusion(bf16[128,8192]{0,1:T(8,128)(2,1)} %bitcast.92, f32[128]{0:T(128)S(1)} %select_reduce_fusion, f32[128,32]{0,1:T(8,128)S(1)} %fusion.57, f32[128,32]{0,1:T(8,128)S(1)} %fusion.56), kind=kOutput, calls=%fused_computation.1 | convolution fusion | flops 70541312 | bytes 2654720 | tf_op jit(solution)/shard_map/kf,kd->fd/dot_general | solution.py:133
  172.0 9.6 %all-to-all-done.4 = bf16[16,8,256]{2,1,0:T(8,128)(2,1)S(1)} async-done(((bf16[16,8,256]{2,1,0:T(8,128)(2,1)}), bf16[16,8,256]{2,1,0:T(8,128)(2,1)S(1)}, u32[]{:S(2)}, u32[]{:S(2)}) %all-to-all-start.4) | async-done | bytes 65568 | tf_op jit(solution)/shard_map/all_to_all | solution.py:144
  181.6 0.6 broadcast_in_dim.181
  182.3 3.5 %all-to-all-start.5 = ((bf16[16,8,256]{2,1,0:T(8,128)(2,1)}), bf16[16,8,256]{2,1,0:T(8,128)(2,1)S(1)}, u32[]{:S(2)}, u32[]{:S(2)}) async-start(bf16[16,8,256]{2,1,0:T(8,128)(2,1)} %broadcast_in_dim.181), calls=%async_computation.5 | async-start | bytes 131072 | tf_op jit(solution)/shard_map/all_to_all | solution.py:20
  185.8 1.6 convolution_convert_fusion.1
  187.4 11.0 %all-to-all-done.5 = bf16[16,8,256]{2,1,0:T(8,128)(2,1)S(1)} async-done(((bf16[16,8,256]{2,1,0:T(8,128)(2,1)}), bf16[16,8,256]{2,1,0:T(8,128)(2,1)S(1)}, u32[]{:S(2)}, u32[]{:S(2)}) %all-to-all-start.5) | async-done | bytes 65568 | tf_op jit(solution)/shard_map/all_to_all | solution.py:20
  198.4 0.7 broadcast_in_dim.183
  199.2 3.7 %all-to-all-start.6 = ((bf16[4,32,1024]{2,1,0:T(8,128)(2,1)}), bf16[4,32,1024]{2,1,0:T(8,128)(2,1)S(1)}, u32[]{:S(2)}, u32[]{:S(2)}) async-start(bf16[4,32,1024]{2,1,0:T(8,128)(2,1)} %broadcast_in_dim.183), calls=%async_computation.6 | async-start | bytes 524288 | tf_op jit(solution)/shard_map/all_to_all | solution.py:20
  202.8 1.6 convolution_convert_fusion.2
  204.4 5.1 %all-to-all-done.6 = bf16[4,32,1024]{2,1,0:T(8,128)(2,1)S(1)} async-done(((bf16[4,32,1024]{2,1,0:T(8,128)(2,1)}), bf16[4,32,1024]{2,1,0:T(8,128)(2,1)S(1)}, u32[]{:S(2)}, u32[]{:S(2)}) %all-to-all-start.6) | async-done | bytes 262176 | tf_op jit(solution)/shard_map/all_to_all | solution.py:20
  209.6 1.2 fusion.3
  (51 shorter events, 1.5 us)
Async XLA Ops:
  0.6 103.2 %copy-start = (bf16[32,8192]{1,0:T(8,128)(2,1)S(1)}, bf16[32,8192]{1,0:T(8,128)(2,1)}, u32[]{:S(2)}) copy-start(bf16[32,8192]{1,0:T(8,128)(2,1)} %param.13) | copy-start | bytes 1572868
  5.8 10.5 %all-to-all-start = ((bf16[4,16,1152]{2,1,0:T(8,128)(2,1)}), bf16[4,16,1152]{2,1,0:T(8,128)(2,1)S(1)}, u32[]{:S(2)}, u32[]{:S(2)}) async-start(bf16[4,16,1152]{2,1,0:T(8,128)(2,1)} %broadcast_in_dim.174), calls=%async_computation | async-start | bytes 294912 | tf_op jit(solution)/shard_map/all_to_all | solution.py:20
  85.4 3.2 %copy-start.2 = (bf16[4,35,4,1024]{3,1,2,0:T(8,128)(2,1)S(1)}, bf16[4,35,4,1024]{3,1,2,0:T(8,128)(2,1)}, u32[]{:S(2)}) copy-start(bf16[4,35,4,1024]{3,1,2,0:T(8,128)(2,1)} %get-tuple-element.12) | copy-start | bytes 3440644
  95.1 6.4 %collective-permute-start = (bf16[2,128,4,1,1024]{1,4,3,2,0:T(8,128)(2,1)}, bf16[2,128,4,1,1024]{1,4,3,2,0:T(8,128)(2,1)}, u32[]{:S(2)}, u32[]{:S(2)}) collective-permute-start(bf16[2,128,4,1,1024]{1,4,3,2,0:T(8,128)(2,1)} %pad_maximum_fusion.1), channel_id=1, source_target_pairs={{0,1},{1,0},{2,3},{3,2},{4,5},{5,4},{6,7},{7,6},{8,9},{9,8},{10,11... | collective-permute-start | bytes 6291464 | tf_op jit(solution)/shard_map/ppermute | solution.py:107
  103.8 1.9 copy-start.1
  103.8 1.4 copy-start.3
  103.8 1.9 copy-start.5
  122.7 6.5 %collective-permute-start.1 = (bf16[128,4,1024]{2,0,1:T(8,128)(2,1)}, bf16[128,4,1024]{2,0,1:T(8,128)(2,1)}, u32[]{:S(2)}, u32[]{:S(2)}) collective-permute-start(bf16[128,4,1024]{2,0,1:T(8,128)(2,1)} %bitcast.84), channel_id=1, source_target_pairs={{0,1},{1,0},{2,3},{3,2},{4,5},{5,4},{6,7},{7,6},{8,9},{9,8},{10,11... | collective-permute-start | bytes 3145736 | tf_op jit(solution)/shard_map/ppermute | solution.py:131
  132.7 22.1 %all-to-all-start.3 = ((bf16[16,32,1024]{2,1,0:T(8,128)(2,1)}), bf16[16,32,1024]{2,1,0:T(8,128)(2,1)}, u32[]{:S(2)}, u32[]{:S(2)}) async-start(bf16[16,32,1024]{2,1,0:T(8,128)(2,1)} %bitcast.105), calls=%async_computation.3 | async-start | bytes 2097152 | tf_op jit(solution)/shard_map/all_to_all | solution.py:140
  156.9 24.7 %all-to-all-start.4 = ((bf16[16,8,256]{2,1,0:T(8,128)(2,1)}), bf16[16,8,256]{2,1,0:T(8,128)(2,1)S(1)}, u32[]{:S(2)}, u32[]{:S(2)}) async-start(bf16[16,8,256]{2,1,0:T(8,128)(2,1)} %bitcast.22), calls=%async_computation.4 | async-start | bytes 131072 | tf_op jit(solution)/shard_map/all_to_all | solution.py:144
  182.3 16.2 %all-to-all-start.5 = ((bf16[16,8,256]{2,1,0:T(8,128)(2,1)}), bf16[16,8,256]{2,1,0:T(8,128)(2,1)S(1)}, u32[]{:S(2)}, u32[]{:S(2)}) async-start(bf16[16,8,256]{2,1,0:T(8,128)(2,1)} %broadcast_in_dim.181), calls=%async_computation.5 | async-start | bytes 131072 | tf_op jit(solution)/shard_map/all_to_all | solution.py:20
  198.4 11.2 %copy-start.6 = (bf16[128,1024]{1,0:T(8,128)(2,1)S(1)}, bf16[128,1024]{1,0:T(8,128)(2,1)}, u32[]{:S(2)}) copy-start(bf16[128,1024]{1,0:T(8,128)(2,1)} %param.9) | copy-start | bytes 786436
  199.2 10.4 %all-to-all-start.6 = ((bf16[4,32,1024]{2,1,0:T(8,128)(2,1)}), bf16[4,32,1024]{2,1,0:T(8,128)(2,1)S(1)}, u32[]{:S(2)}, u32[]{:S(2)}) async-start(bf16[4,32,1024]{2,1,0:T(8,128)(2,1)} %broadcast_in_dim.183), calls=%async_computation.6 | async-start | bytes 524288 | tf_op jit(solution)/shard_map/all_to_all | solution.py:20
  209.6 1.2 copy-start.4

commit v2 on v1

v2 whole, which is shorter than its diff:
```python
import jax
import jax.numpy as jnp
from jax import lax
from jax.experimental import pallas as pl
from jax.experimental.pallas import tpu as pltpu
from jax.sharding import Mesh, PartitionSpec as P

NY, NZ, NX, NC = 4, 16, 4, 2
NT = NX * NC
HEAVY = 12
MOST = 6
PLANE = 35
SENT = 80
KEPT = 128
ROWS, COLS = 8, 256
BF = jnp.bfloat16
F32 = jnp.float32
VMEM = pl.BlockSpec(memory_space=pltpu.VMEM)
SMEM = pl.BlockSpec(memory_space=pltpu.SMEM)
ANY = pl.BlockSpec(memory_space=pl.ANY)
ROOM = pltpu.CompilerParams(vmem_limit_bytes=40 << 20)


def cost(flops, size):
    return pl.CostEstimate(flops=flops, bytes_accessed=size, transcendentals=0)


def dot_t(a, b):
    return lax.dot_general(a, b, (((1,), (1,)), ((), ())), preferred_element_type=F32)


def t_dot(a, b):
    return lax.dot_general(a, b, (((0,), (0,)), ((), ())), preferred_element_type=F32)


def exchange(pieces, axes):
    return lax.all_to_all(pieces, axes, 0, 0, tiled=True)


def spread(piece, axes, n):
    return exchange(jnp.broadcast_to(piece[None], (n,) + piece.shape), axes)


def along_x(array, s):
    return lax.ppermute(array, "x", [(i, (i + s) % NX) for i in range(NX)])


def other_core(array):
    return lax.ppermute(array, "core", [(0, 1), (1, 0)])


def pick_kernel(shard, count, pos, router, tokens, grad_out, out):
    tok_dev, width = tokens.shape
    row = lax.broadcasted_iota(jnp.int32, (8, tok_dev), 0)
    lane = lax.broadcasted_iota(jnp.int32, (8, tok_dev), 1)
    at = jnp.full((8, tok_dev), -1, jnp.int32)
    weight = jnp.zeros((8, tok_dev), F32)
    for j in range(MOST):
        at = jnp.where((row == j) & (j < count[0]), pos[0, j], at)
        weight = jnp.where(row == j, router[0:1, j : j + 1].astype(F32), weight)
    picker = jnp.where(lane == at, 1.0, 0.0).astype(BF)
    meta = jnp.where(lane == 0, weight, 0.0)
    meta = jnp.where(lane == 1, 1.0, meta)
    meta = jnp.where(lane == 2, shard[0].astype(F32), meta)
    meta = jnp.where(lane == 3, row.astype(F32), meta)
    meta = jnp.where(row < count[0], meta, 0.0)
    x = jnp.dot(picker, tokens[...], preferred_element_type=F32)
    dy = jnp.dot(picker, grad_out[...], preferred_element_type=F32)
    both = jnp.concatenate(
        [jnp.concatenate([x, meta], axis=1), jnp.concatenate([dy, meta], axis=1)], axis=0
    ).astype(BF)
    for y in range(NY):
        out[y] = both


def pick_rows(shard, keep_count, keep_pos, router, tokens, grad_out):
    tok_dev, width = tokens.shape
    return pl.pallas_call(
        pick_kernel,
        in_specs=[SMEM, SMEM, SMEM, VMEM, VMEM, VMEM],
        out_specs=VMEM,
        out_shape=jax.ShapeDtypeStruct((NY, 16, width + 128), BF),
        cost_estimate=cost(32 * tok_dev * width, 4 * tok_dev * width),
        name="pick_rows",
    )(shard, keep_count, keep_pos, router, tokens, grad_out)


def select_kernel(where, column, _0, _1, _2, _3, out):
    flat = column[...].reshape(64, column.shape[2])
    m = lax.broadcasted_iota(jnp.int32, (64, 8), 0)
    o = lax.broadcasted_iota(jnp.int32, (64, 8), 1)
    qy, half, qj = m // 16, m // 8 % 2, m % 8
    width = column.shape[2] - 128
    valid = flat[:, width + 1 : width + 2].astype(F32) > 0.5
    heavy = where[1] < HEAVY
    steady = jnp.where(
        heavy,
        jnp.where(qy == 0, jnp.where(qj < MOST, qj, 99), jnp.where(qj == 0, 5 + qy, 99)),
        jnp.where(qj == 0, qy, 99),
    )
    light = jnp.logical_or(qy > 0, jnp.logical_not(heavy))
    extra = jnp.where(valid & (qj >= 1) & light, 1.0, 0.0)
    r = lax.broadcasted_iota(jnp.int32, (64, 64), 0)
    c = lax.broadcasted_iota(jnp.int32, (64, 64), 1)
    before = jnp.where((c < r) & (c // 8 % 2 == r // 8 % 2), 1.0, 0.0).astype(BF)
    nth = jnp.dot(before, extra.astype(BF), preferred_element_type=F32)
    p = o % 4
    turn = lax.rem(where[0] - where[1] + NZ, NY)
    take = jnp.where(
        p < 3,
        jnp.where(steady == 4 * p + turn, 1.0, 0.0),
        jnp.where(nth == where[0].astype(F32), extra, 0.0),
    )
    hot = jnp.where(half == o // 4, take, 0.0).astype(BF)
    picked = t_dot(hot, flat).astype(BF)
    for z in range(NZ):
        out[z] = picked


def select_rows(where, column, after):
    return pl.pallas_call(
        select_kernel,
        in_specs=[SMEM, VMEM] + [ANY] * NX,
        out_specs=VMEM,
        out_shape=jax.ShapeDtypeStruct((NZ, 8, column.shape[2]), BF),
        cost_estimate=cost(16 * column.size, 8 * column.size),
        name="select_rows",
    )(where, column, *after)


def compact_kernel(plane, _1, _2, _3, out):
    width = out.shape[2]
    flat = plane[...].astype(F32).reshape(128, width + 128).astype(BF)
    valid = jnp.where(flat[:, width + 1 : width + 2].astype(F32) > 0.5, 1.0, 0.0)
    r = lax.broadcasted_iota(jnp.int32, (128, 128), 0)
    c = lax.broadcasted_iota(jnp.int32, (128, 128), 1)
    before = jnp.where((c < r) & (c // 4 % 2 == r // 4 % 2), 1.0, 0.0).astype(BF)
    valid = jnp.broadcast_to(valid, (128, 128))
    rank = jnp.dot(before, valid.astype(BF), preferred_element_type=F32)
    rank = rank + jnp.where(r // 4 % 2 == 1, float(PLANE), 0.0)
    hot = jnp.where(rank == c.astype(F32), valid, 0.0).astype(BF)
    rows = t_dot(hot[:, :SENT], flat[:, :width])
    facts = t_dot(flat[:, width:], hot)
    facts = jnp.concatenate([facts[v : v + 1] for v in range(4)], axis=1)
    facts = jnp.concatenate([facts, jnp.zeros((1, width - 512), F32)], axis=1)
    row = lax.broadcasted_iota(jnp.int32, (SENT, width), 0)
    rows = jnp.where(row == 2 * PLANE, facts, rows).astype(BF)
    for y in range(NY):
        out[y] = rows


def compact_rows(plane, after):
    width = plane.shape[2] - 128
    return pl.pallas_call(
        compact_kernel,
        in_specs=[VMEM] + [ANY] * (NX - 1),
        out_specs=VMEM,
        out_shape=jax.ShapeDtypeStruct((NY, SENT, width), BF),
        cost_estimate=cost(256 * plane.size, 8 * plane.size),
        name="compact_rows",
    )(plane, *after)


def run_copies(pairs, sems):
    copies = [
        pltpu.make_async_copy(source, target, sems.at[i])
        for i, (source, target) in enumerate(pairs)
    ]
    for copy in copies:
        copy.start()
    for copy in copies:
        copy.wait()


def peer(place, s, d):
    return lax.rem(place[0] + s + NX, NX) * NC + lax.rem(place[1] + d, NC)


def features(whole, t, width):
    return whole.at[:, pl.ds(pl.multiple_of(t * width, width), width)]


def third(packed, k):
    units = packed.shape[-2] // 3
    return pl.ds(k * units, units)


def pack_kernel(place, gate_w, up_w, down_w, _, out0, out1, out2, out3, sems):
    width = out0.shape[2]
    pairs = []
    for s, out in enumerate((out0, out1, out2, out3)):
        for d in range(NC):
            for k, w in enumerate((gate_w, up_w, down_w)):
                pairs.append((features(w, peer(place, s, d), width), out.at[d, third(out, k)]))
    run_copies(pairs, sems)


def pack_weights(place, gate_weight, up_weight, down_weight, after):
    units, full = gate_weight.shape
    out = jax.ShapeDtypeStruct((NC, 3 * units, full // NT), BF)
    return pl.pallas_call(
        pack_kernel,
        in_specs=[SMEM, ANY, ANY, ANY, ANY],
        out_specs=[VMEM] * NX,
        out_shape=[out] * NX,
        scratch_shapes=[pltpu.SemaphoreType.DMA((3 * NT,))],
        cost_estimate=cost(0, 12 * units * full),
        name="pack_weights",
    )(place, gate_weight, up_weight, down_weight, after)


def join_kernel(in0, in1, in2, in3, out):
    for s, part in enumerate((in0, in1, in2, in3)):
        out[s] = part[0]


def join_far(parts):
    _, units3, width = parts[0].shape
    return pl.pallas_call(
        join_kernel,
        grid=(1,),
        in_specs=[pl.BlockSpec((1, units3, width), lambda i: (1, 0, 0))] * NX,
        out_specs=VMEM,
        out_shape=jax.ShapeDtypeStruct((NX, units3, width), BF),
        cost_estimate=cost(0, 4 * NX * units3 * width),
        name="join_far",
    )(*parts)


def unpack_kernel(place, in0, in1, in2, in3, far, grad_gate, grad_up, grad_down, sems):
    width = far.shape[2]
    pairs = []
    for s, near in enumerate((in0, in1, in2, in3)):
        for d, part in enumerate((near.at[0], far.at[s])):
            for k, out in enumerate((grad_gate, grad_up, grad_down)):
                pairs.append((part.at[third(near, k)], features(out, peer(place, s, d), width)))
    run_copies(pairs, sems)


def unpack_grads(place, parts, far):
    _, units3, width = far.shape
    out = jax.ShapeDtypeStruct((units3 // 3, NT * width), BF)
    return pl.pallas_call(
        unpack_kernel,
        grid=(1,),
        in_specs=[SMEM] + [near_spec(units3, width)] * NX + [VMEM],
        out_specs=[ANY] * 3,
        out_shape=[out] * 3,
        scratch_shapes=[pltpu.SemaphoreType.DMA((3 * NT,))],
        cost_estimate=cost(0, 4 * NT * units3 * width),
        name="unpack_grads",
    )(place, *parts, far)


def near_spec(units3, width):
    return pl.BlockSpec((1, units3, width), lambda i: (0, 0, 0))


def blocks_of(near, far):
    for s in range(NX):
        yield s, 0, near[s][0]
        yield s, 1, far[s]


def forward_kernel(place, slots, messages, w0, w1, w2, w3, far, rows, pre):
    _, units3, width = far.shape
    units = units3 // 3
    slot_id = lax.broadcasted_iota(jnp.int32, (2 * KEPT, SENT), 0)
    total = jnp.zeros((2 * KEPT, width), F32)
    for y in range(NY):
        hot = jnp.where(slot_id == slots[y], 1.0, 0.0).astype(BF)
        total += jnp.dot(hot, messages[y], preferred_element_type=F32)
    ordered = total.astype(BF)
    rows[...] = ordered
    blocks = list(blocks_of((w0, w1, w2, w3), far))
    both = jnp.concatenate([w[: 2 * units] for _, _, w in blocks], axis=0)
    both = dot_t(both, ordered[:KEPT])
    down = jnp.concatenate([w[2 * units :] for _, _, w in blocks], axis=0)
    down = dot_t(down, ordered[KEPT:])
    for i, (s, d, _) in enumerate(blocks):
        t = peer(place, -s, d)
        pre[t, : 2 * units] = both[2 * units * i : 2 * units * (i + 1)]
        pre[t, 2 * units :] = down[units * i : units * (i + 1)]


def forward(place, slots, messages, near, far):
    _, units3, width = far.shape
    return pl.pallas_call(
        forward_kernel,
        grid=(1,),
        in_specs=[SMEM, VMEM, VMEM] + [near_spec(units3, width)] * NX + [VMEM],
        out_specs=[VMEM] * 2,
        out_shape=[
            jax.ShapeDtypeStruct((2 * KEPT, width), BF),
            jax.ShapeDtypeStruct((NT, units3, KEPT), F32),
        ],
        cost_estimate=cost(2 * NT * units3 * width * KEPT, 2 * NT * units3 * width),
        compiler_params=ROOM,
        name="forward",
    )(place, slots, messages, *near, far)


def hidden_kernel(pre, row_scale, out):
    _, units3, _ = pre.shape
    units = units3 // 3
    total = jnp.sum(pre[...], axis=0)
    gate_pre, up_pre, back_proj = total[:units], total[units : 2 * units], total[2 * units :]
    sigmoid_gate = jax.nn.sigmoid(gate_pre)
    activated = gate_pre * sigmoid_gate
    hidden_grad = row_scale[...] * back_proj
    gate = hidden_grad * sigmoid_gate * (1.0 + gate_pre * (1.0 - sigmoid_gate)) * up_pre
    up = hidden_grad * activated
    hidden = activated * up_pre
    both = jnp.concatenate([gate, up, hidden], axis=0).astype(BF)
    for t in range(NT):
        out[t] = both


def hidden_grads(pre, row_scale):
    return pl.pallas_call(
        hidden_kernel,
        in_specs=[VMEM] * 2,
        out_specs=VMEM,
        out_shape=jax.ShapeDtypeStruct(pre.shape, BF),
        cost_estimate=cost(20 * pre.size, 6 * pre.size),
        name="hidden_grads",
    )(pre, row_scale)


def input_grad_kernel(place, grads, w0, w1, w2, w3, far, out):
    _, units3, width = far.shape
    units2 = units3 // 3 * 2
    blocks = list(blocks_of((w0, w1, w2, w3), far))
    g = jnp.concatenate([grads[peer(place, -s, d), :units2] for s, d, _ in blocks], axis=0)
    w = jnp.concatenate([w[:units2] for _, _, w in blocks], axis=0)
    total = t_dot(g, w).astype(BF)
    wide = width // COLS
    for i in range(KEPT // ROWS):
        for k in range(wide):
            out[wide * i + k] = total[ROWS * i : ROWS * (i + 1), COLS * k : COLS * (k + 1)]


def input_grad(place, grads, near, far):
    _, units3, width = far.shape
    pieces = KEPT // ROWS * (width // COLS)
    return pl.pallas_call(
        input_grad_kernel,
        grid=(1,),
        in_specs=[SMEM, VMEM] + [near_spec(units3, width)] * NX + [VMEM],
        out_specs=VMEM,
        out_shape=jax.ShapeDtypeStruct((pieces, ROWS, COLS), BF),
        cost_estimate=cost(2 * NT * units3 * width * KEPT, 2 * NT * units3 * width),
        compiler_params=ROOM,
        name="input_grad",
    )(place, grads, *near, far)


def weight_grads_kernel(place, grads, rows, row_scale, out0, out1, out2, out3):
    _, units3, _ = out0.shape
    units = units3 // 3
    x = rows[:KEPT]
    scaled_dy = (row_scale[...] * rows[KEPT:].astype(F32)).astype(BF)
    for s, out in enumerate((out0, out1, out2, out3)):
        for d in range(NC):
            g = grads[peer(place, -s, d)]
            both = jnp.dot(g[: 2 * units], x, preferred_element_type=F32)
            out[d, : 2 * units] = both.astype(BF)
            down = jnp.dot(g[2 * units :], scaled_dy, preferred_element_type=F32)
            out[d, 2 * units :] = down.astype(BF)


def weight_grads(place, grads, rows, row_scale):
    _, units3, _ = grads.shape
    width = rows.shape[1]
    return pl.pallas_call(
        weight_grads_kernel,
        in_specs=[SMEM] + [VMEM] * 3,
        out_specs=[VMEM] * NX,
        out_shape=[jax.ShapeDtypeStruct((NC, units3, width), BF)] * NX,
        cost_estimate=cost(2 * NT * units3 * width * KEPT, 2 * NT * units3 * width),
        compiler_params=ROOM,
        name="weight_grads",
    )(place, grads, rows, row_scale)


def finish_kernel(blocks, owner, grad_out, grad_tokens, summed):
    width = grad_out.shape[1]
    wide = width // COLS
    rows = []
    for i in range(KEPT // ROWS):
        parts = [blocks[wide * i + k].astype(F32) for k in range(wide)]
        rows.append(jnp.concatenate(parts, axis=1))
    whole = jnp.concatenate(rows, axis=0)
    summed[...] = whole
    added = jnp.dot(owner[...], whole.astype(BF), preferred_element_type=F32)
    grad_tokens[...] = (grad_out[...].astype(F32) + added).astype(BF)


def finish(blocks, owner, grad_out):
    width = grad_out.shape[1]
    return pl.pallas_call(
        finish_kernel,
        in_specs=[VMEM] * 3,
        out_specs=[VMEM] * 2,
        out_shape=[
            jax.ShapeDtypeStruct(grad_out.shape, BF),
            jax.ShapeDtypeStruct((KEPT, width), F32),
        ],
        cost_estimate=cost(2 * KEPT * grad_out.size, 10 * grad_out.size),
        name="finish",
    )(blocks, owner, grad_out)


def body(tokens, grad_out, keep_count, keep_pos, router, gate_weight, up_weight, down_weight):
    tok_dev, width = tokens.shape
    yi, zi = lax.axis_index("y"), lax.axis_index("z")
    place = jnp.stack([lax.axis_index("x"), lax.axis_index("core")])
    shard = yi * NZ + zi
    tensor, context = ("x", "core"), ("y", "z")

    picked = pick_rows(jnp.reshape(shard, (1,)), keep_count, keep_pos, router, tokens, grad_out)
    column = exchange(picked, "y")

    sent = pack_weights(place, gate_weight, up_weight, down_weight, picked)
    near = [sent[0]] + [along_x(sent[s], s) for s in range(1, NX)]
    plane = exchange(select_rows(jnp.stack([yi, zi]), column, sent), "z")
    messages = exchange(compact_rows(plane, near[1:]), "y")
    far = other_core(join_far(near))

    facts = messages[:, 2 * PLANE, :512].reshape(NY, 4, 128).astype(F32)[:, :, :PLANE]
    facts = facts.transpose(1, 0, 2).reshape(4, NY * PLANE)
    valid = facts[1] > 0.5
    key = facts[2] * 8 + facts[3]
    slot = jnp.sum((key[None, :] < key[:, None]) & valid[None, :], axis=1)
    hot = (slot[None, :] == jnp.arange(KEPT)[:, None]) & valid[None, :]
    row_scale = jnp.sum(jnp.where(hot, facts[0][None, :], 0.0), axis=1)
    start_here = jnp.sum((valid & (facts[2] < shard.astype(F32))).astype(jnp.int32))
    slot = jnp.where(valid, slot, -2 * KEPT).reshape(NY, 1, PLANE)
    slot = jnp.pad(
        jnp.concatenate([slot, slot + KEPT], axis=2),
        ((0, 0), (0, 0), (0, SENT - 2 * PLANE)),
        constant_values=-1,
    )

    rows, pre = forward(place, slot, messages, near, far)
    grads = hidden_grads(exchange(pre, tensor), row_scale[None, :])
    grads = exchange(grads, tensor)
    blocks = exchange(input_grad(place, grads, near, far), context)
    units = weight_grads(place, grads, rows, row_scale[:, None])
    units = [units[0]] + [along_x(units[s], -s) for s in range(1, NX)]
    far_units = other_core(join_far(units))
    block = jnp.sum(blocks.astype(F32), axis=0).astype(BF)
    blocks = spread(block, context, NY * NZ)

    j6 = jnp.arange(MOST)
    token_is = (keep_pos[0][None, :] == jnp.arange(tok_dev)[:, None]) & (j6 < keep_count[0])[None, :]
    slot_of = jnp.max(jnp.where(token_is, start_here + j6[None, :], -1), axis=1)
    owner = (slot_of[:, None] == jnp.arange(KEPT)[None, :]).astype(BF)
    grad_tokens, summed = finish(blocks, owner, grad_out)
    grad_gate, grad_up, grad_down = unpack_grads(place, units, far_units)
    return (grad_tokens, grad_gate, grad_up, grad_down, summed)


def solution(mesh):
    grid = Mesh(mesh.devices.reshape(NY, NZ, NX, NC), ("y", "z", "x", "core"))
    context, tensor = ("y", "z"), ("x", "core")
    units = P(tensor + context, None)
    return jax.shard_map(
        body,
        mesh=grid,
        in_specs=(
            P(context, tensor),
            P(context, tensor),
            P(context),
            P(context, None),
            P(context, None),
            units,
            units,
            units,
        ),
        out_specs=(P(context, tensor), units, units, units, P(None, tensor)),
        check_vma=False,
    )
```

time: 214 us -> 171 us (0.80)
  blocking collectives: 60.8 us -> 10.1 us
  starting transfers between devices: 34.2 us -> 72.3 us
  Pallas kernels: 0 us -> 25.3 us
  local copies, waits for them, and re-layouts: 34.5 us -> 10.6 us
  matrix products: 18.7 us -> 0 us
  waiting for transfers between devices: 48.7 us -> 43.4 us
  other arithmetic: 10.1 us -> 4.88 us
    all_to_all x2 -> x1, blocking collectives: 60.8 us -> 10.1 us  [exchange(): return lax.all_to_all(pieces, axes, 0, 0, tiled=True)]
    pallas_call x0 -> x12, Pallas kernels: none -> 25.3 us  [the longest x2 4.42 us: join_far(): pl.pallas_call(join_kernel, grid=(1,), in_specs=[pl.BlockSpec((1, units3,...]
    all_to_all x5 -> x6, starting transfers between devices: 30.1 us -> 49.4 us  [exchange(): return lax.all_to_all(pieces, axes, 0, 0, tiled=True)]
    ppermute x2 -> x8, starting transfers between devices: 4.12 us -> 22.9 us  [the longest x6 19.1 us: along_x(): return lax.ppermute(array, 'x', [(i, (i + s) % NX) for i in range(NX)])]
    dot_general x18 -> x0, matrix products: 18.7 us -> none  [the longest x8 6.09 us: one_hot_rows(): return jnp.dot(hot.astype(BF), rows, preferred_element_type=F32).astype(BF)]
    all_to_all x5 -> x6, waiting for transfers between devices: 44.7 us -> 29 us  [exchange(): return lax.all_to_all(pieces, axes, 0, 0, tiled=True)]
    ppermute x2 -> x8, waiting for transfers between devices: 4.06 us -> 14.4 us  [the longest x6 14.4 us: along_x(): return lax.ppermute(array, 'x', [(i, (i + s) % NX) for i in range(NX)])]
    dynamic_slice x2 -> x0, local copies, waits for them, and re-layouts: 8.82 us -> none  [the longest x1 4.42 us: body(): lax.dynamic_index_in_dim(partial, 1 - ci, 2, keepdims=False).astype(BF)]
  transfers between devices with their start and end apart: 7 -> 14, of which waited for: 6 -> 8; matrix products, arithmetic and copies ran while one was open for 6% -> 4% of each run, Pallas kernels for 0% -> 7%
where the time goes in v2:
time: 171 us; the launch traced here: 168 us
  starting transfers between devices  72.3 us (42%)
  waiting for transfers between devices  43.4 us (25%)
  Pallas kernels  25.3 us (15%)
  local copies, waits for them, and re-layouts  10.6 us (6%)
  blocking collectives  10.1 us (6%)
  other arithmetic  4.88 us (3%)
    all_to_all x6, starting transfers between devices, exchange(): return lax.all_to_all(pieces, axes, 0, 0, tiled=True)  49.4 us
    all_to_all x6, waiting for transfers between devices, exchange(): return lax.all_to_all(pieces, axes, 0, 0, tiled=True)  29 us
    ppermute x6, starting transfers between devices, along_x(): return lax.ppermute(array, 'x', [(i, (i + s) % NX) for i in range(NX)])  19.1 us
    ppermute x6, waiting for transfers between devices, along_x(): return lax.ppermute(array, 'x', [(i, (i + s) % NX) for i in range(NX)])  14.4 us
    all_to_all x1, blocking collectives, exchange(): return lax.all_to_all(pieces, axes, 0, 0, tiled=True)  10.1 us
    unnamed x52, local copies, waits for them, and re-layouts  9.35 us
    pallas_call x2, Pallas kernels, join_far(): pl.pallas_call(join_kernel, grid=(1,), in_specs=[pl.BlockSpec((1, units3,...  4.42 us
    ppermute x2, starting transfers between devices, other_core(): return lax.ppermute(array, 'core', [(0, 1), (1, 0)])  3.82 us
  transfers between devices with their start and end apart: 14, of which 8 were waited for; matrix products, arithmetic and copies ran while one was open for 4% of the time, Pallas kernels for 7%

profile of v2, /device:TPU:6, one launch (start us, length us, event | category | flops | bytes accessed | tf_op | source)
XLA Modules:
  0.0 168.2 jit_solution(9531077898654684675)
XLA Ops:
  1.3 1.9 %pick_rows.1._ = bf16[4,16,1152]{2,1,0:T(8,128)(2,1)} custom-call(s32[1]{0:T(128)} %bitcast.4.shard, s32[1]{0:T(128)} %copy.21.count, s32[1,6]{1,0:T(1,128)} %pos.1, bf16[1,6]{1,0:T(2,128)(2,1)} %router.1, bf16[128,1024]{1,0:T(8,128)(2,1)} %tokens.1, bf16[128,1024]{1,0:T(8,128)(2,1)} %grad_out.3), custom_call_target="tpu_custom_call" | custom-call | flops 4194304 | bytes 524288 | tf_op jit(solution)/shard_map/pick_rows/pallas_call | solution.py:78
  3.2 4.5 %all-to-all-start = ((bf16[4,16,1152]{2,1,0:T(8,128)(2,1)}), bf16[4,16,1152]{2,1,0:T(8,128)(2,1)S(1)}, u32[]{:S(2)}, u32[]{:S(2)}) async-start(bf16[4,16,1152]{2,1,0:T(8,128)(2,1)} %pick_rows.1._), calls=%async_computation | async-start | bytes 294912 | tf_op jit(solution)/shard_map/all_to_all | solution.py:37
  7.7 0.6 pad_add_fusion.1.place
  8.2 3.4 %pack_weights.1 = (bf16[2,96,1024]{2,1,0:T(8,128)(2,1)}, bf16[2,96,1024]{2,1,0:T(8,128)(2,1)}, bf16[2,96,1024]{2,1,0:T(8,128)(2,1)}, bf16[2,96,1024]{2,1,0:T(8,128)(2,1)}) custom-call(s32[2]{0:T(128)} %pad_add_fusion.1.place, bf16[32,8192]{1,0:T(8,128)(2,1)} %gate_w.1, bf16[32,8192]{1,0:T(8,128)(2,1)} %up_w.1, bf16[32,8192]{1,0:T(8,128)(2,1)} %down_w.1, ...), custom_call_target="tpu_custom_call" | custom-call | bytes 3145728 | tf_op jit(solution)/shard_map/pack_weights/pallas_call | solution.py:201
  11.7 0.6 pad_add_fusion.2.where
  12.3 1.5 all-to-all-done.column
  13.7 0.7 copy-done.17
  14.4 2.1 %select_rows.1 = bf16[16,8,1152]{2,1,0:T(8,128)(2,1)} custom-call(s32[2]{0:T(128)} %pad_add_fusion.2.where, bf16[4,16,1152]{2,1,0:T(8,128)(2,1)} %copy-done.17, bf16[2,96,1024]{2,1,0:T(8,128)(2,1)} %get-tuple-element.20._0.in0.w0, bf16[2,96,1024]{2,1,0:T(8,128)(2,1)} %get-tuple-element.21._1, bf16[2,96,1024]{2,1,0:T(8,128)(2,1)} %get-tuple-element.22._2, ...), custom_call_target="tpu_custom_call" | custom-call | flops 1179648 | bytes 589824 | tf_op jit(solution)/shard_map/select_rows/pallas_call | solution.py:121
  16.5 15.3 %all-to-all-start.1 = ((bf16[16,8,1152]{2,1,0:T(8,128)(2,1)}), bf16[16,8,1152]{2,1,0:T(8,128)(2,1)S(1)}, u32[]{:S(2)}, u32[]{:S(2)}) async-start(bf16[16,8,1152]{2,1,0:T(8,128)(2,1)} %select_rows.1), calls=%async_computation.1 | async-start | bytes 589824 | tf_op jit(solution)/shard_map/all_to_all | solution.py:37
  31.8 2.4 %collective-permute-start = (bf16[2,96,1024]{2,1,0:T(8,128)(2,1)S(1)}, bf16[2,96,1024]{2,1,0:T(8,128)(2,1)S(1)}, u32[]{:S(2)}, u32[]{:S(2)}) collective-permute-start(bf16[2,96,1024]{2,1,0:T(8,128)(2,1)S(1)} %copy-done.20), channel_id=1, source_target_pairs={{0,2},{2,4},{4,6},{6,0},{1,3},{3,5},{5,7},{7,1},{8,10},{10,12},{12... | collective-permute-start | bytes 1179656 | tf_op jit(solution)/shard_map/ppermute | solution.py:45
  34.2 4.3 %collective-permute-start.1 = (bf16[2,96,1024]{2,1,0:T(8,128)(2,1)S(1)}, bf16[2,96,1024]{2,1,0:T(8,128)(2,1)S(1)}, u32[]{:S(2)}, u32[]{:S(2)}) collective-permute-start(bf16[2,96,1024]{2,1,0:T(8,128)(2,1)S(1)} %copy-done.19), channel_id=1, source_target_pairs={{0,4},{2,6},{4,0},{6,2},{1,5},{3,7},{5,1},{7,3},{8,12},{10,14},{12... | collective-permute-start | bytes 1179656 | tf_op jit(solution)/shard_map/ppermute | solution.py:45
  38.6 1.9 %collective-permute-start.2 = (bf16[2,96,1024]{2,1,0:T(8,128)(2,1)S(1)}, bf16[2,96,1024]{2,1,0:T(8,128)(2,1)S(1)}, u32[]{:S(2)}, u32[]{:S(2)}) collective-permute-start(bf16[2,96,1024]{2,1,0:T(8,128)(2,1)S(1)} %copy-done.18), channel_id=1, source_target_pairs={{0,6},{2,0},{4,2},{6,4},{1,7},{3,1},{5,3},{7,5},{8,14},{10,8},{12,... | collective-permute-start | bytes 1179656 | tf_op jit(solution)/shard_map/ppermute | solution.py:45
  40.5 5.3 %collective-permute-done._1.in1.w1 = bf16[2,96,1024]{2,1,0:T(8,128)(2,1)S(1)} collective-permute-done((bf16[2,96,1024]{2,1,0:T(8,128)(2,1)S(1)}, bf16[2,96,1024]{2,1,0:T(8,128)(2,1)S(1)}, u32[]{:S(2)}, u32[]{:S(2)}) %collective-permute-start) | collective-permute-done | bytes 393248 | tf_op jit(solution)/shard_map/ppermute | solution.py:45
  45.8 3.9 %collective-permute-done.1._2.in2.w2 = bf16[2,96,1024]{2,1,0:T(8,128)(2,1)S(1)} collective-permute-done((bf16[2,96,1024]{2,1,0:T(8,128)(2,1)S(1)}, bf16[2,96,1024]{2,1,0:T(8,128)(2,1)S(1)}, u32[]{:S(2)}, u32[]{:S(2)}) %collective-permute-start.1) | collective-permute-done | bytes 393248 | tf_op jit(solution)/shard_map/ppermute | solution.py:45
  49.7 5.2 %collective-permute-done.2._3.in3.w3 = bf16[2,96,1024]{2,1,0:T(8,128)(2,1)S(1)} collective-permute-done((bf16[2,96,1024]{2,1,0:T(8,128)(2,1)S(1)}, bf16[2,96,1024]{2,1,0:T(8,128)(2,1)S(1)}, u32[]{:S(2)}, u32[]{:S(2)}) %collective-permute-start.2) | collective-permute-done | bytes 393248 | tf_op jit(solution)/shard_map/ppermute | solution.py:45
  55.0 0.7 copy-done.4
  55.7 0.7 copy-done.14
  56.4 2.3 %compact_rows.1 = bf16[4,80,1024]{2,1,0:T(8,128)(2,1)} custom-call(bf16[16,8,1152]{2,1,0:T(8,128)(2,1)} %copy-done.14, bf16[2,96,1024]{2,1,0:T(8,128)(2,1)} %copy-done, bf16[2,96,1024]{2,1,0:T(8,128)(2,1)} %copy-done.2, bf16[2,96,1024]{2,1,0:T(8,128)(2,1)} %copy-done.4), custom_call_target="tpu_custom_call" | custom-call | flops 37748736 | bytes 1179648 | tf_op jit(solution)/shard_map/compact_rows/pallas_call | solution.py:154
  58.7 4.2 %all-to-all-start.2 = ((bf16[4,80,1024]{2,1,0:T(8,128)(2,1)}), bf16[4,80,1024]{2,1,0:T(8,128)(2,1)S(1)}, u32[]{:S(2)}, u32[]{:S(2)}) async-start(bf16[4,80,1024]{2,1,0:T(8,128)(2,1)} %compact_rows.1), calls=%async_computation.2 | async-start | bytes 1310720 | tf_op jit(solution)/shard_map/all_to_all | solution.py:37
  62.9 2.3 %join_far.2 = bf16[4,96,1024]{2,1,0:T(8,128)(2,1)} custom-call(bf16[2,96,1024]{2,1,0:T(8,128)(2,1)} %get-tuple-element.20._0.in0.w0, bf16[2,96,1024]{2,1,0:T(8,128)(2,1)} %copy-done, bf16[2,96,1024]{2,1,0:T(8,128)(2,1)} %copy-done.2, bf16[2,96,1024]{2,1,0:T(8,128)(2,1)} %copy-done.4), custom_call_target="tpu_custom_call" | custom-call | bytes 1572864 | tf_op jit(solution)/shard_map/join_far/pallas_call | solution.py:219
  65.2 1.9 %collective-permute-start.3 = (bf16[4,96,1024]{2,1,0:T(8,128)(2,1)}, bf16[4,96,1024]{2,1,0:T(8,128)(2,1)S(1)}, u32[]{:S(2)}, u32[]{:S(2)}) collective-permute-start(bf16[4,96,1024]{2,1,0:T(8,128)(2,1)} %join_far.2), channel_id=1, source_target_pairs={{0,1},{1,0},{2,3},{3,2},{4,5},{5,4},{6,7},{7,6},{8,9},{9,8},{10,11... | collective-permute-start | bytes 2359304 | tf_op jit(solution)/shard_map/ppermute | solution.py:49
  67.1 6.8 %all-to-all-done.2.messages = bf16[4,80,1024]{2,1,0:T(8,128)(2,1)S(1)} async-done(((bf16[4,80,1024]{2,1,0:T(8,128)(2,1)}), bf16[4,80,1024]{2,1,0:T(8,128)(2,1)S(1)}, u32[]{:S(2)}, u32[]{:S(2)}) %all-to-all-start.2) | async-done | bytes 655392 | tf_op jit(solution)/shard_map/all_to_all | solution.py:37
  74.0 0.1 gt.32
  74.1 0.6 slice_reduce_fusion.1
  74.7 0.1 add.46
  74.8 0.2 convert_reduce_fusion
  75.0 0.1 reduce_sum.42
  75.2 0.5 copy-done.9
  75.8 1.7 forward.1
  77.4 0.7 copy-done.8
  78.2 4.6 %all-to-all-start.3 = ((f32[8,96,128]{2,1,0:T(8,128)}), f32[8,96,128]{2,1,0:T(8,128)S(1)}, u32[]{:S(2)}, u32[]{:S(2)}) async-start(f32[8,96,128]{2,1,0:T(8,128)} %copy-done.8), calls=%async_computation.3 | async-start | bytes 786432 | tf_op jit(solution)/shard_map/all_to_all | solution.py:37
  82.9 0.5 copy-done.24
  83.4 0.6 select_reduce_fusion
  84.1 5.6 %all-to-all-done.3.pre = f32[8,96,128]{2,1,0:T(8,128)S(1)} async-done(((f32[8,96,128]{2,1,0:T(8,128)}), f32[8,96,128]{2,1,0:T(8,128)S(1)}, u32[]{:S(2)}, u32[]{:S(2)}) %all-to-all-start.3) | async-done | bytes 393248 | tf_op jit(solution)/shard_map/all_to_all | solution.py:37
  89.7 0.7 copy-done.13
  90.4 1.7 %hidden_grads.1 = bf16[8,96,128]{2,1,0:T(8,128)(2,1)} custom-call(f32[8,96,128]{2,1,0:T(8,128)} %copy-done.13, f32[1,128]{1,0:T(1,128)} %bitcast.15), custom_call_target="tpu_custom_call" | custom-call | flops 1966080 | bytes 589824 | tf_op jit(solution)/shard_map/hidden_grads/pallas_call | solution.py:320
  92.1 10.1 %all_to_all.35.grads = bf16[8,96,128]{2,1,0:T(8,128)(2,1)S(1)} all-to-all(bf16[8,96,128]{2,1,0:T(8,128)(2,1)} %hidden_grads.1), channel_id=1, replica_groups=mesh['y'=4,'z'=16,'x'=4,'core'=2] {'x','core'}, dimensions={0} | all-to-all | bytes 393216 | tf_op jit(solution)/shard_map/all_to_all | solution.py:37
  102.3 1.6 input_grad.1
  103.9 13.0 %all-to-all-start.5 = ((bf16[64,8,256]{2,1,0:T(8,128)(2,1)}), bf16[64,8,256]{2,1,0:T(8,128)(2,1)S(1)}, u32[]{:S(2)}, u32[]{:S(2)}) async-start(bf16[64,8,256]{2,1,0:T(8,128)(2,1)} %input_grad.1), calls=%async_computation.5 | async-start | bytes 524288 | tf_op jit(solution)/shard_map/all_to_all | solution.py:37
  116.9 0.6 copy-done.22
  117.6 0.1 copy.20.row_scale
  117.7 1.3 weight_grads.1
  119.0 0.7 copy-done.7
  119.8 1.9 %collective-permute-start.4 = (bf16[2,96,1024]{2,1,0:T(8,128)(2,1)S(1)}, bf16[2,96,1024]{2,1,0:T(8,128)(2,1)S(1)}, u32[]{:S(2)}, u32[]{:S(2)}) collective-permute-start(bf16[2,96,1024]{2,1,0:T(8,128)(2,1)S(1)} %get-tuple-element.28), channel_id=1, source_target_pairs={{0,6},{2,0},{4,2},{6,4},{1,7},{3,1},{5,3},{7,5},{8,14},{10,8},{12,... | collective-permute-start | bytes 1179656 | tf_op jit(solution)/shard_map/ppermute | solution.py:45
  121.7 5.4 %collective-permute-start.5 = (bf16[2,96,1024]{2,1,0:T(8,128)(2,1)S(1)}, bf16[2,96,1024]{2,1,0:T(8,128)(2,1)S(1)}, u32[]{:S(2)}, u32[]{:S(2)}) collective-permute-start(bf16[2,96,1024]{2,1,0:T(8,128)(2,1)S(1)} %get-tuple-element.29), channel_id=1, source_target_pairs={{0,4},{2,6},{4,0},{6,2},{1,5},{3,7},{5,1},{7,3},{8,12},{10,14},{12... | collective-permute-start | bytes 1179656 | tf_op jit(solution)/shard_map/ppermute | solution.py:45
  127.1 3.1 %collective-permute-start.6 = (bf16[2,96,1024]{2,1,0:T(8,128)(2,1)S(1)}, bf16[2,96,1024]{2,1,0:T(8,128)(2,1)S(1)}, u32[]{:S(2)}, u32[]{:S(2)}) collective-permute-start(bf16[2,96,1024]{2,1,0:T(8,128)(2,1)S(1)} %get-tuple-element.30), channel_id=1, source_target_pairs={{0,2},{2,4},{4,6},{6,0},{1,3},{3,5},{5,7},{7,1},{8,10},{10,12},{12... | collective-permute-start | bytes 1179656 | tf_op jit(solution)/shard_map/ppermute | solution.py:45
  130.2 7.4 %all-to-all-done.5 = bf16[64,8,256]{2,1,0:T(8,128)(2,1)S(1)} async-done(((bf16[64,8,256]{2,1,0:T(8,128)(2,1)}), bf16[64,8,256]{2,1,0:T(8,128)(2,1)S(1)}, u32[]{:S(2)}, u32[]{:S(2)}) %all-to-all-start.5) | async-done | bytes 262176 | tf_op jit(solution)/shard_map/all_to_all | solution.py:37
  137.7 0.7 broadcast_in_dim.58
  138.4 7.7 %all-to-all-start.6 = ((bf16[64,8,256]{2,1,0:T(8,128)(2,1)}), bf16[64,8,256]{2,1,0:T(8,128)(2,1)S(1)}, u32[]{:S(2)}, u32[]{:S(2)}) async-start(bf16[64,8,256]{2,1,0:T(8,128)(2,1)} %broadcast_in_dim.58), calls=%async_computation.6 | async-start | bytes 524288 | tf_op jit(solution)/shard_map/all_to_all | solution.py:37
  146.2 0.7 copy-done.10
  146.9 0.2 copy-done.11
  147.1 0.1 copy-done.12
  147.2 2.2 %join_far.3 = bf16[4,96,1024]{2,1,0:T(8,128)(2,1)} custom-call(bf16[2,96,1024]{2,1,0:T(8,128)(2,1)} %copy-done.7, bf16[2,96,1024]{2,1,0:T(8,128)(2,1)} %copy-done.10, bf16[2,96,1024]{2,1,0:T(8,128)(2,1)} %copy-done.11, bf16[2,96,1024]{2,1,0:T(8,128)(2,1)} %copy-done.12), custom_call_target="tpu_custom_call" | custom-call | bytes 1572864 | tf_op jit(solution)/shard_map/join_far/pallas_call | solution.py:219
  149.4 1.9 %collective-permute-start.7 = (bf16[4,96,1024]{2,1,0:T(8,128)(2,1)}, bf16[4,96,1024]{2,1,0:T(8,128)(2,1)S(1)}, u32[]{:S(2)}, u32[]{:S(2)}) collective-permute-start(bf16[4,96,1024]{2,1,0:T(8,128)(2,1)} %join_far.3), channel_id=1, source_target_pairs={{0,1},{1,0},{2,3},{3,2},{4,5},{5,4},{6,7},{7,6},{8,9},{9,8},{10,11... | collective-permute-start | bytes 2359304 | tf_op jit(solution)/shard_map/ppermute | solution.py:49
  151.3 0.6 fusion.4
  152.0 0.6 iota_add_fusion
  152.6 0.6 copy-done.25
  153.3 0.1 select_reduce_fusion.1
  153.4 0.7 fusion.1.owner
  154.1 0.9 copy-done.16
  154.9 2.8 %unpack_grads.1 = (bf16[32,8192]{1,0:T(8,128)(2,1)}, bf16[32,8192]{1,0:T(8,128)(2,1)}, bf16[32,8192]{1,0:T(8,128)(2,1)}) custom-call(s32[2]{0:T(128)} %pad_add_fusion.1.place, bf16[2,96,1024]{2,1,0:T(8,128)(2,1)} %copy-done.7, bf16[2,96,1024]{2,1,0:T(8,128)(2,1)} %copy-done.10, bf16[2,96,1024]{2,1,0:T(8,128)(2,1)} %copy-done.11, ...), custom_call_target="tpu_custom_call" | custom-call | bytes 3145728 | tf_op jit(solution)/shard_map/unpack_grads/pallas_call | solution.py:243
  157.8 7.7 %all-to-all-done.6.blocks = bf16[64,8,256]{2,1,0:T(8,128)(2,1)S(1)} async-done(((bf16[64,8,256]{2,1,0:T(8,128)(2,1)}), bf16[64,8,256]{2,1,0:T(8,128)(2,1)S(1)}, u32[]{:S(2)}, u32[]{:S(2)}) %all-to-all-start.6) | async-done | bytes 262176 | tf_op jit(solution)/shard_map/all_to_all | solution.py:37
  165.5 0.7 copy-done.15
  166.2 2.0 %finish.1 = (bf16[128,1024]{1,0:T(8,128)(2,1)}, f32[128,1024]{1,0:T(8,128)}) custom-call(bf16[64,8,256]{2,1,0:T(8,128)(2,1)} %copy-done.15, bf16[128,128]{1,0:T(8,128)(2,1)} %fusion.1.owner, bf16[128,1024]{1,0:T(8,128)(2,1)} %grad_out.3), custom_call_target="tpu_custom_call" | custom-call | flops 33554432 | bytes 1310720 | tf_op jit(solution)/shard_map/finish/pallas_call | solution.py:401
  (53 shorter events, 0.4 us)
Async XLA Ops:
  3.2 10.5 %all-to-all-start = ((bf16[4,16,1152]{2,1,0:T(8,128)(2,1)}), bf16[4,16,1152]{2,1,0:T(8,128)(2,1)S(1)}, u32[]{:S(2)}, u32[]{:S(2)}) async-start(bf16[4,16,1152]{2,1,0:T(8,128)(2,1)} %pick_rows.1._), calls=%async_computation | async-start | bytes 294912 | tf_op jit(solution)/shard_map/all_to_all | solution.py:37
  13.7 0.7 copy-start.17
  14.4 17.4 %copy-start.20 = (bf16[2,96,1024]{2,1,0:T(8,128)(2,1)S(1)}, bf16[2,96,1024]{2,1,0:T(8,128)(2,1)}, u32[]{:S(2)}) copy-start(bf16[2,96,1024]{2,1,0:T(8,128)(2,1)} %get-tuple-element.21._1) | copy-start | bytes 1179652
  14.4 19.8 %copy-start.19 = (bf16[2,96,1024]{2,1,0:T(8,128)(2,1)S(1)}, bf16[2,96,1024]{2,1,0:T(8,128)(2,1)}, u32[]{:S(2)}) copy-start(bf16[2,96,1024]{2,1,0:T(8,128)(2,1)} %get-tuple-element.22._2) | copy-start | bytes 1179652
  16.5 22.1 %copy-start.18 = (bf16[2,96,1024]{2,1,0:T(8,128)(2,1)S(1)}, bf16[2,96,1024]{2,1,0:T(8,128)(2,1)}, u32[]{:S(2)}) copy-start(bf16[2,96,1024]{2,1,0:T(8,128)(2,1)} %get-tuple-element.23._3) | copy-start | bytes 1179652
  16.5 38.4 %all-to-all-start.1 = ((bf16[16,8,1152]{2,1,0:T(8,128)(2,1)}), bf16[16,8,1152]{2,1,0:T(8,128)(2,1)S(1)}, u32[]{:S(2)}, u32[]{:S(2)}) async-start(bf16[16,8,1152]{2,1,0:T(8,128)(2,1)} %select_rows.1), calls=%async_computation.1 | async-start | bytes 589824 | tf_op jit(solution)/shard_map/all_to_all | solution.py:37
  31.8 13.9 %collective-permute-start = (bf16[2,96,1024]{2,1,0:T(8,128)(2,1)S(1)}, bf16[2,96,1024]{2,1,0:T(8,128)(2,1)S(1)}, u32[]{:S(2)}, u32[]{:S(2)}) collective-permute-start(bf16[2,96,1024]{2,1,0:T(8,128)(2,1)S(1)} %copy-done.20), channel_id=1, source_target_pairs={{0,2},{2,4},{4,6},{6,0},{1,3},{3,5},{5,7},{7,1},{8,10},{10,12},{12... | collective-permute-start | bytes 1179656 | tf_op jit(solution)/shard_map/ppermute | solution.py:45
  34.2 15.5 %collective-permute-start.1 = (bf16[2,96,1024]{2,1,0:T(8,128)(2,1)S(1)}, bf16[2,96,1024]{2,1,0:T(8,128)(2,1)S(1)}, u32[]{:S(2)}, u32[]{:S(2)}) collective-permute-start(bf16[2,96,1024]{2,1,0:T(8,128)(2,1)S(1)} %copy-done.19), channel_id=1, source_target_pairs={{0,4},{2,6},{4,0},{6,2},{1,5},{3,7},{5,1},{7,3},{8,12},{10,14},{12... | collective-permute-start | bytes 1179656 | tf_op jit(solution)/shard_map/ppermute | solution.py:45
  38.6 16.3 %collective-permute-start.2 = (bf16[2,96,1024]{2,1,0:T(8,128)(2,1)S(1)}, bf16[2,96,1024]{2,1,0:T(8,128)(2,1)S(1)}, u32[]{:S(2)}, u32[]{:S(2)}) collective-permute-start(bf16[2,96,1024]{2,1,0:T(8,128)(2,1)S(1)} %copy-done.18), channel_id=1, source_target_pairs={{0,6},{2,0},{4,2},{6,4},{1,7},{3,1},{5,3},{7,5},{8,14},{10,8},{12,... | collective-permute-start | bytes 1179656 | tf_op jit(solution)/shard_map/ppermute | solution.py:45
  45.8 9.2 %copy-start = (bf16[2,96,1024]{2,1,0:T(8,128)(2,1)}, bf16[2,96,1024]{2,1,0:T(8,128)(2,1)S(1)}, u32[]{:S(2)}) copy-start(bf16[2,96,1024]{2,1,0:T(8,128)(2,1)S(1)} %collective-permute-done._1.in1.w1) | copy-start | bytes 1179652
  49.7 5.3 %copy-start.2 = (bf16[2,96,1024]{2,1,0:T(8,128)(2,1)}, bf16[2,96,1024]{2,1,0:T(8,128)(2,1)S(1)}, u32[]{:S(2)}) copy-start(bf16[2,96,1024]{2,1,0:T(8,128)(2,1)S(1)} %collective-permute-done.1._2.in2.w2) | copy-start | bytes 1179652
  54.9 0.7 copy-start.4
  55.7 0.7 copy-start.14
  58.7 15.2 %all-to-all-start.2 = ((bf16[4,80,1024]{2,1,0:T(8,128)(2,1)}), bf16[4,80,1024]{2,1,0:T(8,128)(2,1)S(1)}, u32[]{:S(2)}, u32[]{:S(2)}) async-start(bf16[4,80,1024]{2,1,0:T(8,128)(2,1)} %compact_rows.1), calls=%async_computation.2 | async-start | bytes 1310720 | tf_op jit(solution)/shard_map/all_to_all | solution.py:37
  62.9 12.3 %copy-start.1 = (bf16[2,96,1024]{2,1,0:T(8,128)(2,1)S(1)}, bf16[2,96,1024]{2,1,0:T(8,128)(2,1)}, u32[]{:S(2)}) copy-start(bf16[2,96,1024]{2,1,0:T(8,128)(2,1)} %copy-done) | copy-start | bytes 1179652
  62.9 12.3 %copy-start.3 = (bf16[2,96,1024]{2,1,0:T(8,128)(2,1)S(1)}, bf16[2,96,1024]{2,1,0:T(8,128)(2,1)}, u32[]{:S(2)}) copy-start(bf16[2,96,1024]{2,1,0:T(8,128)(2,1)} %copy-done.2) | copy-start | bytes 1179652
  62.9 12.3 %copy-start.5 = (bf16[2,96,1024]{2,1,0:T(8,128)(2,1)S(1)}, bf16[2,96,1024]{2,1,0:T(8,128)(2,1)}, u32[]{:S(2)}) copy-start(bf16[2,96,1024]{2,1,0:T(8,128)(2,1)} %copy-done.4) | copy-start | bytes 1179652
  62.9 12.3 %copy-start.6 = (bf16[2,96,1024]{2,1,0:T(8,128)(2,1)S(1)}, bf16[2,96,1024]{2,1,0:T(8,128)(2,1)}, u32[]{:S(2)}) copy-start(bf16[2,96,1024]{2,1,0:T(8,128)(2,1)} %get-tuple-element.20._0.in0.w0) | copy-start | bytes 1179652
  65.2 10.0 %collective-permute-start.3 = (bf16[4,96,1024]{2,1,0:T(8,128)(2,1)}, bf16[4,96,1024]{2,1,0:T(8,128)(2,1)S(1)}, u32[]{:S(2)}, u32[]{:S(2)}) collective-permute-start(bf16[4,96,1024]{2,1,0:T(8,128)(2,1)} %join_far.2), channel_id=1, source_target_pairs={{0,1},{1,0},{2,3},{3,2},{4,5},{5,4},{6,7},{7,6},{8,9},{9,8},{10,11... | collective-permute-start | bytes 2359304 | tf_op jit(solution)/shard_map/ppermute | solution.py:49
  74.1 0.7 copy-start.23
  75.2 0.6 copy-start.9
  77.4 0.7 copy-start.8
  78.2 4.6 %copy-start.21 = (f32[4,35]{1,0:T(4,128)S(1)}, f32[4,35]{1,0:T(4,128)}, u32[]{:S(2)}) copy-start(f32[4,35]{1,0:T(4,128)} %get-tuple-element.35) | copy-start | bytes 1684
  78.2 11.5 %all-to-all-start.3 = ((f32[8,96,128]{2,1,0:T(8,128)}), f32[8,96,128]{2,1,0:T(8,128)S(1)}, u32[]{:S(2)}, u32[]{:S(2)}) async-start(f32[8,96,128]{2,1,0:T(8,128)} %copy-done.8), calls=%async_computation.3 | async-start | bytes 786432 | tf_op jit(solution)/shard_map/all_to_all | solution.py:37
  82.8 0.6 copy-start.24
  89.7 0.7 copy-start.13
  103.9 33.8 %all-to-all-start.5 = ((bf16[64,8,256]{2,1,0:T(8,128)(2,1)}), bf16[64,8,256]{2,1,0:T(8,128)(2,1)S(1)}, u32[]{:S(2)}, u32[]{:S(2)}) async-start(bf16[64,8,256]{2,1,0:T(8,128)(2,1)} %input_grad.1), calls=%async_computation.5 | async-start | bytes 524288 | tf_op jit(solution)/shard_map/all_to_all | solution.py:37
  116.9 0.7 copy-start.22
  119.0 0.8 copy-start.7
  119.8 26.4 %collective-permute-start.4 = (bf16[2,96,1024]{2,1,0:T(8,128)(2,1)S(1)}, bf16[2,96,1024]{2,1,0:T(8,128)(2,1)S(1)}, u32[]{:S(2)}, u32[]{:S(2)}) collective-permute-start(bf16[2,96,1024]{2,1,0:T(8,128)(2,1)S(1)} %get-tuple-element.28), channel_id=1, source_target_pairs={{0,6},{2,0},{4,2},{6,4},{1,7},{3,1},{5,3},{7,5},{8,14},{10,8},{12,... | collective-permute-start | bytes 1179656 | tf_op jit(solution)/shard_map/ppermute | solution.py:45
  121.7 24.5 %collective-permute-start.5 = (bf16[2,96,1024]{2,1,0:T(8,128)(2,1)S(1)}, bf16[2,96,1024]{2,1,0:T(8,128)(2,1)S(1)}, u32[]{:S(2)}, u32[]{:S(2)}) collective-permute-start(bf16[2,96,1024]{2,1,0:T(8,128)(2,1)S(1)} %get-tuple-element.29), channel_id=1, source_target_pairs={{0,4},{2,6},{4,0},{6,2},{1,5},{3,7},{5,1},{7,3},{8,12},{10,14},{12... | collective-permute-start | bytes 1179656 | tf_op jit(solution)/shard_map/ppermute | solution.py:45
  127.1 19.1 %collective-permute-start.6 = (bf16[2,96,1024]{2,1,0:T(8,128)(2,1)S(1)}, bf16[2,96,1024]{2,1,0:T(8,128)(2,1)S(1)}, u32[]{:S(2)}, u32[]{:S(2)}) collective-permute-start(bf16[2,96,1024]{2,1,0:T(8,128)(2,1)S(1)} %get-tuple-element.30), channel_id=1, source_target_pairs={{0,2},{2,4},{4,6},{6,0},{1,3},{3,5},{5,7},{7,1},{8,10},{10,12},{12... | collective-permute-start | bytes 1179656 | tf_op jit(solution)/shard_map/ppermute | solution.py:45
  138.4 27.1 %all-to-all-start.6 = ((bf16[64,8,256]{2,1,0:T(8,128)(2,1)}), bf16[64,8,256]{2,1,0:T(8,128)(2,1)S(1)}, u32[]{:S(2)}, u32[]{:S(2)}) async-start(bf16[64,8,256]{2,1,0:T(8,128)(2,1)} %broadcast_in_dim.58), calls=%async_computation.6 | async-start | bytes 524288 | tf_op jit(solution)/shard_map/all_to_all | solution.py:37
  146.2 0.8 copy-start.10
  146.2 0.9 copy-start.11
  146.2 1.0 copy-start.12
  149.4 4.7 %collective-permute-start.7 = (bf16[4,96,1024]{2,1,0:T(8,128)(2,1)}, bf16[4,96,1024]{2,1,0:T(8,128)(2,1)S(1)}, u32[]{:S(2)}, u32[]{:S(2)}) collective-permute-start(bf16[4,96,1024]{2,1,0:T(8,128)(2,1)} %join_far.3), channel_id=1, source_target_pairs={{0,1},{1,0},{2,3},{3,2},{4,5},{5,4},{6,7},{7,6},{8,9},{9,8},{10,11... | collective-permute-start | bytes 2359304 | tf_op jit(solution)/shard_map/ppermute | solution.py:49
  152.6 0.7 copy-start.25
  154.1 0.9 copy-start.16
  165.5 0.7 copy-start.15

commit v3 on v2

--- a/solution.py
+++ b/solution.py
@@ -10,7 +10,7 @@
 HEAVY = 12
 MOST = 6
 PLANE = 35
-SENT = 80
+SENT = 72
 KEPT = 128
 ROWS, COLS = 8, 256
 BF = jnp.bfloat16
@@ -49,7 +49,7 @@
     return lax.ppermute(array, "core", [(0, 1), (1, 0)])
 
 
-def pick_kernel(shard, count, pos, router, tokens, grad_out, out):
+def pick_kernel(count, pos, router, tokens, grad_out, out):
     tok_dev, width = tokens.shape
     row = lax.broadcasted_iota(jnp.int32, (8, tok_dev), 0)
     lane = lax.broadcasted_iota(jnp.int32, (8, tok_dev), 1)
@@ -61,7 +61,6 @@
     picker = jnp.where(lane == at, 1.0, 0.0).astype(BF)
     meta = jnp.where(lane == 0, weight, 0.0)
     meta = jnp.where(lane == 1, 1.0, meta)
-    meta = jnp.where(lane == 2, shard[0].astype(F32), meta)
     meta = jnp.where(lane == 3, row.astype(F32), meta)
     meta = jnp.where(row < count[0], meta, 0.0)
     x = jnp.dot(picker, tokens[...], preferred_element_type=F32)
@@ -73,26 +72,30 @@
         out[y] = both
 
 
-def pick_rows(shard, keep_count, keep_pos, router, tokens, grad_out):
+def pick_rows(keep_count, keep_pos, router, tokens, grad_out):
     tok_dev, width = tokens.shape
     return pl.pallas_call(
         pick_kernel,
-        in_specs=[SMEM, SMEM, SMEM, VMEM, VMEM, VMEM],
+        in_specs=[SMEM, SMEM, VMEM, VMEM, VMEM],
         out_specs=VMEM,
         out_shape=jax.ShapeDtypeStruct((NY, 16, width + 128), BF),
         cost_estimate=cost(32 * tok_dev * width, 4 * tok_dev * width),
         name="pick_rows",
-    )(shard, keep_count, keep_pos, router, tokens, grad_out)
-
-
-def select_kernel(where, column, _0, _1, _2, _3, out):
+    )(keep_count, keep_pos, router, tokens, grad_out)
+
+
+def select_kernel(place, column, _0, _1, _2, _3, out):
     flat = column[...].reshape(64, column.shape[2])
+    width = column.shape[2] - 128
+    row = lax.broadcasted_iota(jnp.int32, (64, 128), 0)
+    lane = lax.broadcasted_iota(jnp.int32, (64, 128), 1)
+    shard = (row // 16 * NZ + place[3]).astype(F32).astype(BF)
+    meta = jnp.where(lane == 2, shard, flat[:, width:])
     m = lax.broadcasted_iota(jnp.int32, (64, 8), 0)
     o = lax.broadcasted_iota(jnp.int32, (64, 8), 1)
     qy, half, qj = m // 16, m // 8 % 2, m % 8
-    width = column.shape[2] - 128
     valid = flat[:, width + 1 : width + 2].astype(F32) > 0.5
-    heavy = where[1] < HEAVY
+    heavy = place[3] < HEAVY
     steady = jnp.where(
         heavy,
         jnp.where(qy == 0, jnp.where(qj < MOST, qj, 99), jnp.where(qj == 0, 5 + qy, 99)),
@@ -105,19 +108,21 @@
     before = jnp.where((c < r) & (c // 8 % 2 == r // 8 % 2), 1.0, 0.0).astype(BF)
     nth = jnp.dot(before, extra.astype(BF), preferred_element_type=F32)
     p = o % 4
-    turn = lax.rem(where[0] - where[1] + NZ, NY)
+    turn = lax.rem(place[2] - place[3] + NZ, NY)
     take = jnp.where(
         p < 3,
         jnp.where(steady == 4 * p + turn, 1.0, 0.0),
-        jnp.where(nth == where[0].astype(F32), extra, 0.0),
+        jnp.where(nth == place[2].astype(F32), extra, 0.0),
     )
     hot = jnp.where(half == o // 4, take, 0.0).astype(BF)
-    picked = t_dot(hot, flat).astype(BF)
+    picked = t_dot(hot, flat[:, :width]).astype(BF)
+    facts = t_dot(hot, meta).astype(BF)
     for z in range(NZ):
-        out[z] = picked
-
-
-def select_rows(where, column, after):
+        out[z, :, :width] = picked
+        out[z, :, width:] = facts
+
+
+def select_rows(place, column, after):
     return pl.pallas_call(
         select_kernel,
         in_specs=[SMEM, VMEM] + [ANY] * NX,
@@ -125,10 +130,10 @@
         out_shape=jax.ShapeDtypeStruct((NZ, 8, column.shape[2]), BF),
         cost_estimate=cost(16 * column.size, 8 * column.size),
         name="select_rows",
-    )(where, column, *after)
-
-
-def compact_kernel(plane, _1, _2, _3, out):
+    )(place, column, *after)
+
+
+def compact_kernel(plane, _, out):
     width = out.shape[2]
     flat = plane[...].astype(F32).reshape(128, width + 128).astype(BF)
     valid = jnp.where(flat[:, width + 1 : width + 2].astype(F32) > 0.5, 1.0, 0.0)
@@ -153,12 +158,12 @@
     width = plane.shape[2] - 128
     return pl.pallas_call(
         compact_kernel,
-        in_specs=[VMEM] + [ANY] * (NX - 1),
+        in_specs=[VMEM, ANY],
         out_specs=VMEM,
         out_shape=jax.ShapeDtypeStruct((NY, SENT, width), BF),
         cost_estimate=cost(256 * plane.size, 8 * plane.size),
         name="compact_rows",
-    )(plane, *after)
+    )(plane, after)
 
 
 def run_copies(pairs, sems):
@@ -209,20 +214,22 @@
     )(place, gate_weight, up_weight, down_weight, after)
 
 
-def join_kernel(in0, in1, in2, in3, out):
-    for s, part in enumerate((in0, in1, in2, in3)):
+def join_kernel(*refs):
+    out = refs[-1]
+    for s, part in enumerate(refs[:-1]):
         out[s] = part[0]
 
 
 def join_far(parts):
+    n = len(parts)
     _, units3, width = parts[0].shape
     return pl.pallas_call(
         join_kernel,
         grid=(1,),
-        in_specs=[pl.BlockSpec((1, units3, width), lambda i: (1, 0, 0))] * NX,
-        out_specs=VMEM,
-        out_shape=jax.ShapeDtypeStruct((NX, units3, width), BF),
-        cost_estimate=cost(0, 4 * NX * units3 * width),
+        in_specs=[pl.BlockSpec((1, units3, width), lambda i: (1, 0, 0))] * n,
+        out_specs=VMEM,
+        out_shape=jax.ShapeDtypeStruct((n, units3, width), BF),
+        cost_estimate=cost(0, 4 * n * units3 * width),
         name="join_far",
     )(*parts)
 
@@ -262,16 +269,37 @@
         yield s, 1, far[s]
 
 
-def forward_kernel(place, slots, messages, w0, w1, w2, w3, far, rows, pre):
+def slots_of(messages):
+    lane = lax.broadcasted_iota(jnp.int32, (1, 128), 1)
+    rows = []
+    for y in range(NY):
+        facts = messages[y][2 * PLANE : 2 * PLANE + 1, :512].astype(F32)
+        key = facts[:, 256:384] * 8.0 + facts[:, 384:512]
+        rows.append(jnp.where(facts[:, 128:256] > 0.5, key, 1e6))
+    keys = jnp.concatenate([jnp.where(lane < PLANE, r, 1e6) for r in rows] * 2, axis=0).T
+    for key in rows:
+        slot = jnp.zeros((1, 128), F32)
+        for y in range(NY):
+            less = jnp.where(keys[:, y : y + 1] < key, 1.0, 0.0)
+            slot += jnp.sum(less, axis=0, keepdims=True)
+        yield jnp.where(key < 1e5, slot, -1000.0).astype(jnp.int32)
+
+
+def order_rows(messages):
+    lane = lax.broadcasted_iota(jnp.int32, (2 * KEPT, 128), 1)
+    slot_id = lax.broadcasted_iota(jnp.int32, (2 * KEPT, 128), 0)
+    slot_id = slot_id - jnp.where(lane < PLANE, 0, KEPT)
+    total = jnp.zeros((2 * KEPT, messages.shape[2]), F32)
+    for y, slots in enumerate(slots_of(messages)):
+        hot = jnp.where(slot_id == slots, 1.0, 0.0).astype(BF)[:, :SENT]
+        total += jnp.dot(hot, messages[y], preferred_element_type=F32)
+    return total.astype(BF)
+
+
+def forward_kernel(place, messages, w0, w1, w2, w3, far, pre):
     _, units3, width = far.shape
     units = units3 // 3
-    slot_id = lax.broadcasted_iota(jnp.int32, (2 * KEPT, SENT), 0)
-    total = jnp.zeros((2 * KEPT, width), F32)
-    for y in range(NY):
-        hot = jnp.where(slot_id == slots[y], 1.0, 0.0).astype(BF)
-        total += jnp.dot(hot, messages[y], preferred_element_type=F32)
-    ordered = total.astype(BF)
-    rows[...] = ordered
+    ordered = order_rows(messages)
     blocks = list(blocks_of((w0, w1, w2, w3), far))
     both = jnp.concatenate([w[: 2 * units] for _, _, w in blocks], axis=0)
     both = dot_t(both, ordered[:KEPT])
@@ -283,21 +311,18 @@
         pre[t, 2 * units :] = down[units * i : units * (i + 1)]
 
 
-def forward(place, slots, messages, near, far):
+def forward(place, messages, near, far):
     _, units3, width = far.shape
     return pl.pallas_call(
         forward_kernel,
         grid=(1,),
-        in_specs=[SMEM, VMEM, VMEM] + [near_spec(units3, width)] * NX + [VMEM],
-        out_specs=[VMEM] * 2,
-        out_shape=[
-            jax.ShapeDtypeStruct((2 * KEPT, width), BF),
-            jax.ShapeDtypeStruct((NT, units3, KEPT), F32),
-        ],
+        in_specs=[SMEM, VMEM] + [near_spec(units3, width)] * NX + [VMEM],
+        out_specs=VMEM,
+        out_shape=jax.ShapeDtypeStruct((NT, units3, KEPT), F32),
         cost_estimate=cost(2 * NT * units3 * width * KEPT, 2 * NT * units3 * width),
         compiler_params=ROOM,
         name="forward",
-    )(place, slots, messages, *near, far)
+    )(place, messages, *near, far)
 
 
 def hidden_kernel(pre, row_scale, out):
@@ -355,9 +380,10 @@
     )(place, grads, *near, far)
 
 
-def weight_grads_kernel(place, grads, rows, row_scale, out0, out1, out2, out3):
+def weight_grads_kernel(place, grads, messages, row_scale, out0, out1, out2, out3):
     _, units3, _ = out0.shape
     units = units3 // 3
+    rows = order_rows(messages)
     x = rows[:KEPT]
     scaled_dy = (row_scale[...] * rows[KEPT:].astype(F32)).astype(BF)
     for s, out in enumerate((out0, out1, out2, out3)):
@@ -369,9 +395,9 @@
             out[d, 2 * units :] = down.astype(BF)
 
 
-def weight_grads(place, grads, rows, row_scale):
+def weight_grads(place, grads, messages, row_scale):
     _, units3, _ = grads.shape
-    width = rows.shape[1]
+    width = messages.shape[2]
     return pl.pallas_call(
         weight_grads_kernel,
         in_specs=[SMEM] + [VMEM] * 3,
@@ -380,7 +406,7 @@
         cost_estimate=cost(2 * NT * units3 * width * KEPT, 2 * NT * units3 * width),
         compiler_params=ROOM,
         name="weight_grads",
-    )(place, grads, rows, row_scale)
+    )(place, grads, messages, row_scale)
 
 
 def finish_kernel(blocks, owner, grad_out, grad_tokens, summed):
@@ -414,18 +440,18 @@
 def body(tokens, grad_out, keep_count, keep_pos, router, gate_weight, up_weight, down_weight):
     tok_dev, width = tokens.shape
     yi, zi = lax.axis_index("y"), lax.axis_index("z")
-    place = jnp.stack([lax.axis_index("x"), lax.axis_index("core")])
     shard = yi * NZ + zi
+    place = jnp.stack([lax.axis_index("x"), lax.axis_index("core"), yi, zi])
     tensor, context = ("x", "core"), ("y", "z")
 
-    picked = pick_rows(jnp.reshape(shard, (1,)), keep_count, keep_pos, router, tokens, grad_out)
+    picked = pick_rows(keep_count, keep_pos, router, tokens, grad_out)
     column = exchange(picked, "y")
 
     sent = pack_weights(place, gate_weight, up_weight, down_weight, picked)
     near = [sent[0]] + [along_x(sent[s], s) for s in range(1, NX)]
-    plane = exchange(select_rows(jnp.stack([yi, zi]), column, sent), "z")
-    messages = exchange(compact_rows(plane, near[1:]), "y")
     far = other_core(join_far(near))
+    plane = exchange(select_rows(place, column, sent), "z")
+    messages = exchange(compact_rows(plane, far), "y")
 
     facts = messages[:, 2 * PLANE, :512].reshape(NY, 4, 128).astype(F32)[:, :, :PLANE]
     facts = facts.transpose(1, 0, 2).reshape(4, NY * PLANE)
@@ -435,18 +461,12 @@
     hot = (slot[None, :] == jnp.arange(KEPT)[:, None]) & valid[None, :]
     row_scale = jnp.sum(jnp.where(hot, facts[0][None, :], 0.0), axis=1)
     start_here = jnp.sum((valid & (facts[2] < shard.astype(F32))).astype(jnp.int32))
-    slot = jnp.where(valid, slot, -2 * KEPT).reshape(NY, 1, PLANE)
-    slot = jnp.pad(
-        jnp.concatenate([slot, slot + KEPT], axis=2),
-        ((0, 0), (0, 0), (0, SENT - 2 * PLANE)),
-        constant_values=-1,
-    )
-
-    rows, pre = forward(place, slot, messages, near, far)
+
+    pre = forward(place, messages, near, far)
     grads = hidden_grads(exchange(pre, tensor), row_scale[None, :])
     grads = exchange(grads, tensor)
     blocks = exchange(input_grad(place, grads, near, far), context)
-    units = weight_grads(place, grads, rows, row_scale[:, None])
+    units = weight_grads(place, grads, messages, row_scale[:, None])
     units = [units[0]] + [along_x(units[s], -s) for s in range(1, NX)]
     far_units = other_core(join_far(units))
     block = jnp.sum(blocks.astype(F32), axis=0).astype(BF)

time: 171 us -> 166 us (0.971)
  blocking collectives: 10.1 us -> 23.1 us
  waiting for transfers between devices: 43.4 us -> 33.4 us
  starting transfers between devices: 72.3 us -> 65.5 us
    ppermute x6, waiting for transfers between devices: 14.4 us -> 0.02 us  [along_x(): return lax.ppermute(array, 'x', [(i, (i + s) % NX) for i in range(NX)])]
    all_to_all x1 -> x2, blocking collectives: 10.1 us -> 23.1 us  [exchange(): return lax.all_to_all(pieces, axes, 0, 0, tiled=True)]
    all_to_all x6 -> x5, starting transfers between devices: 49.4 us -> 39.9 us  [exchange(): return lax.all_to_all(pieces, axes, 0, 0, tiled=True)]
    ppermute x6, starting transfers between devices: 19.1 us -> 21.8 us  [along_x(): return lax.ppermute(array, 'x', [(i, (i + s) % NX) for i in range(NX)])]
    ppermute x2, waiting for transfers between devices: 0.01 us -> 2.46 us  [other_core(): return lax.ppermute(array, 'core', [(0, 1), (1, 0)])]
    all_to_all x6 -> x5, waiting for transfers between devices: 29 us -> 30.9 us  [exchange(): return lax.all_to_all(pieces, axes, 0, 0, tiled=True)]
    unnamed x52 -> x42, local copies, waits for them, and re-layouts: 9.35 us -> 8.89 us
  transfers between devices with their start and end apart: 14 -> 13, of which waited for: 8 -> 5; matrix products, arithmetic and copies ran while one was open for 4% -> 3% of each run, Pallas kernels for 7% -> 9%
where the time goes in v3:
time: 166 us; the launch traced here: 164 us
  starting transfers between devices  65.5 us (39%)
  waiting for transfers between devices  33.4 us (20%)
  Pallas kernels  27 us (16%)
  blocking collectives  23.1 us (14%)
  local copies, waits for them, and re-layouts  10 us (6%)
  other arithmetic  3.71 us (2%)
    all_to_all x5, starting transfers between devices, exchange(): return lax.all_to_all(pieces, axes, 0, 0, tiled=True)  39.9 us
    all_to_all x5, waiting for transfers between devices, exchange(): return lax.all_to_all(pieces, axes, 0, 0, tiled=True)  30.9 us
    all_to_all x2, blocking collectives, exchange(): return lax.all_to_all(pieces, axes, 0, 0, tiled=True)  23.1 us
    ppermute x6, starting transfers between devices, along_x(): return lax.ppermute(array, 'x', [(i, (i + s) % NX) for i in range(NX)])  21.8 us
    unnamed x42, local copies, waits for them, and re-layouts  8.89 us
    pallas_call x2, Pallas kernels, join_far(): pl.pallas_call(join_kernel, grid=(1,), in_specs=[pl.BlockSpec((1, units3,...  4.33 us
    ppermute x2, starting transfers between devices, other_core(): return lax.ppermute(array, 'core', [(0, 1), (1, 0)])  3.82 us
    pallas_call x1, Pallas kernels, pack_weights(): pl.pallas_call(pack_kernel, in_specs=[SMEM, ANY, ANY, ANY, ANY], out_spec...  3.43 us
  transfers between devices with their start and end apart: 13, of which 5 were waited for; matrix products, arithmetic and copies ran while one was open for 3% of the time, Pallas kernels for 9%

profile of v3, /device:TPU:6, one launch (start us, length us, event | category | flops | bytes accessed | tf_op | source)
XLA Modules:
  0.0 164.3 jit_solution(6014829828784106946)
XLA Ops:
  1.3 1.9 %pick_rows.1._ = bf16[4,16,1152]{2,1,0:T(8,128)(2,1)} custom-call(s32[1]{0:T(128)} %copy.16.count, s32[1,6]{1,0:T(1,128)} %pos.1, bf16[1,6]{1,0:T(2,128)(2,1)} %router.1, bf16[128,1024]{1,0:T(8,128)(2,1)} %tokens.1, bf16[128,1024]{1,0:T(8,128)(2,1)} %grad_out.3), custom_call_target="tpu_custom_call" | custom-call | flops 4194304 | bytes 524288 | tf_op jit(solution)/shard_map/pick_rows/pallas_call | solution.py:77
  3.2 4.5 %all-to-all-start = ((bf16[4,16,1152]{2,1,0:T(8,128)(2,1)}), bf16[4,16,1152]{2,1,0:T(8,128)(2,1)S(1)}, u32[]{:S(2)}, u32[]{:S(2)}) async-start(bf16[4,16,1152]{2,1,0:T(8,128)(2,1)} %pick_rows.1._), calls=%async_computation | async-start | bytes 294912 | tf_op jit(solution)/shard_map/all_to_all | solution.py:37
  7.7 0.7 pad_add_fusion.place
  8.3 3.4 %pack_weights.1 = (bf16[2,96,1024]{2,1,0:T(8,128)(2,1)}, bf16[2,96,1024]{2,1,0:T(8,128)(2,1)}, bf16[2,96,1024]{2,1,0:T(8,128)(2,1)}, bf16[2,96,1024]{2,1,0:T(8,128)(2,1)}) custom-call(s32[4]{0:T(128)} %pad_add_fusion.place, bf16[32,8192]{1,0:T(8,128)(2,1)} %gate_w.1, bf16[32,8192]{1,0:T(8,128)(2,1)} %up_w.1, bf16[32,8192]{1,0:T(8,128)(2,1)} %down_w.1, ...), custom_call_target="tpu_custom_call" | custom-call | bytes 3145728 | tf_op jit(solution)/shard_map/pack_weights/pallas_call | solution.py:206
  11.7 6.6 %collective-permute-start = (bf16[2,96,1024]{2,1,0:T(8,128)(2,1)}, bf16[2,96,1024]{2,1,0:T(8,128)(2,1)S(1)}, u32[]{:S(2)}, u32[]{:S(2)}) collective-permute-start(bf16[2,96,1024]{2,1,0:T(8,128)(2,1)} %get-tuple-element.19._1), channel_id=1, source_target_pairs={{0,2},{2,4},{4,6},{6,0},{1,3},{3,5},{5,7},{7,1},{8,10},{10,12},{12... | collective-permute-start | bytes 1179656 | tf_op jit(solution)/shard_map/ppermute | solution.py:45
  18.4 1.9 %collective-permute-start.1 = (bf16[2,96,1024]{2,1,0:T(8,128)(2,1)}, bf16[2,96,1024]{2,1,0:T(8,128)(2,1)S(1)}, u32[]{:S(2)}, u32[]{:S(2)}) collective-permute-start(bf16[2,96,1024]{2,1,0:T(8,128)(2,1)} %get-tuple-element.20._2), channel_id=1, source_target_pairs={{0,4},{2,6},{4,0},{6,2},{1,5},{3,7},{5,1},{7,3},{8,12},{10,14},{12... | collective-permute-start | bytes 1179656 | tf_op jit(solution)/shard_map/ppermute | solution.py:45
  20.3 2.8 %collective-permute-start.2 = (bf16[2,96,1024]{2,1,0:T(8,128)(2,1)}, bf16[2,96,1024]{2,1,0:T(8,128)(2,1)S(1)}, u32[]{:S(2)}, u32[]{:S(2)}) collective-permute-start(bf16[2,96,1024]{2,1,0:T(8,128)(2,1)} %get-tuple-element.21._3), channel_id=1, source_target_pairs={{0,6},{2,0},{4,2},{6,4},{1,7},{3,1},{5,3},{7,5},{8,14},{10,8},{12,... | collective-permute-start | bytes 1179656 | tf_op jit(solution)/shard_map/ppermute | solution.py:45
  23.1 0.0 copy-start.18
  23.1 0.7 copy-done.18
  23.8 2.0 %select_rows.1 = bf16[16,8,1152]{2,1,0:T(8,128)(2,1)} custom-call(s32[4]{0:T(128)} %pad_add_fusion.place, bf16[4,16,1152]{2,1,0:T(8,128)(2,1)} %copy-done.18, bf16[2,96,1024]{2,1,0:T(8,128)(2,1)} %get-tuple-element.18._0.refs_0_.w0, bf16[2,96,1024]{2,1,0:T(8,128)(2,1)} %get-tuple-element.19._1, bf16[2,96,1024]{2,1,0:T(8,128)(2,1)} %get-tuple-element.20._2, ...), custom_call_target="tpu_custom_call" | custom-call | flops 1179648 | bytes 589824 | tf_op jit(solution)/shard_map/select_rows/pallas_call | solution.py:126
  25.8 12.5 %all-to-all-start.1 = ((bf16[16,8,1152]{2,1,0:T(8,128)(2,1)}), bf16[16,8,1152]{2,1,0:T(8,128)(2,1)S(1)}, u32[]{:S(2)}, u32[]{:S(2)}) async-start(bf16[16,8,1152]{2,1,0:T(8,128)(2,1)} %select_rows.1), calls=%async_computation.1 | async-start | bytes 589824 | tf_op jit(solution)/shard_map/all_to_all | solution.py:37
  38.3 0.0 copy-start.3
  38.4 0.7 copy-done.3
  39.1 0.1 copy-done.5
  39.2 0.7 copy-done.7
  39.9 2.2 %join_far.2 = bf16[4,96,1024]{2,1,0:T(8,128)(2,1)} custom-call(bf16[2,96,1024]{2,1,0:T(8,128)(2,1)} %get-tuple-element.18._0.refs_0_.w0, bf16[2,96,1024]{2,1,0:T(8,128)(2,1)} %copy-done.3, bf16[2,96,1024]{2,1,0:T(8,128)(2,1)} %copy-done.5, bf16[2,96,1024]{2,1,0:T(8,128)(2,1)} %copy-done.7), custom_call_target="tpu_custom_call" | custom-call | bytes 1572864 | tf_op jit(solution)/shard_map/join_far/pallas_call | solution.py:226
  42.1 1.9 %collective-permute-start.3 = (bf16[4,96,1024]{2,1,0:T(8,128)(2,1)}, bf16[4,96,1024]{2,1,0:T(8,128)(2,1)S(1)}, u32[]{:S(2)}, u32[]{:S(2)}) collective-permute-start(bf16[4,96,1024]{2,1,0:T(8,128)(2,1)} %join_far.2), channel_id=1, source_target_pairs={{0,1},{1,0},{2,3},{3,2},{4,5},{5,4},{6,7},{7,6},{8,9},{9,8},{10,11... | collective-permute-start | bytes 2359304 | tf_op jit(solution)/shard_map/ppermute | solution.py:49
  44.0 2.5 %collective-permute-done.3._.far = bf16[4,96,1024]{2,1,0:T(8,128)(2,1)S(1)} collective-permute-done((bf16[4,96,1024]{2,1,0:T(8,128)(2,1)}, bf16[4,96,1024]{2,1,0:T(8,128)(2,1)S(1)}, u32[]{:S(2)}, u32[]{:S(2)}) %collective-permute-start.3) | collective-permute-done | bytes 786464 | tf_op jit(solution)/shard_map/ppermute | solution.py:49
  46.5 10.9 %all-to-all-done.1.plane = bf16[16,8,1152]{2,1,0:T(8,128)(2,1)S(1)} async-done(((bf16[16,8,1152]{2,1,0:T(8,128)(2,1)}), bf16[16,8,1152]{2,1,0:T(8,128)(2,1)S(1)}, u32[]{:S(2)}, u32[]{:S(2)}) %all-to-all-start.1) | async-done | bytes 294944 | tf_op jit(solution)/shard_map/all_to_all | solution.py:37
  57.4 0.7 copy-done.15
  58.1 2.3 %compact_rows.1 = bf16[4,72,1024]{2,1,0:T(8,128)(2,1)} custom-call(bf16[16,8,1152]{2,1,0:T(8,128)(2,1)} %copy-done.15, bf16[4,96,1024]{2,1,0:T(8,128)(2,1)} %copy-done), custom_call_target="tpu_custom_call" | custom-call | flops 37748736 | bytes 1179648 | tf_op jit(solution)/shard_map/compact_rows/pallas_call | solution.py:159
  60.4 12.9 %all_to_all.35.messages = bf16[4,72,1024]{2,1,0:T(8,128)(2,1)S(1)} all-to-all(bf16[4,72,1024]{2,1,0:T(8,128)(2,1)} %compact_rows.1), channel_id=1, replica_groups=mesh['y'=4,'z'=16,'x'=4,'core'=2] {'y'}, dimensions={0} | all-to-all | bytes 1179648 | tf_op jit(solution)/shard_map/all_to_all | solution.py:37
  73.5 0.1 gt.16
  73.6 0.5 copy-done.10
  74.1 2.7 %forward.1 = f32[8,96,128]{2,1,0:T(8,128)} custom-call(s32[4]{0:T(128)S(1)} %copy-done.10, bf16[4,72,1024]{2,1,0:T(8,128)(2,1)S(1)} %all_to_all.35.messages, bf16[2,96,1024]{2,1,0:T(8,128)(2,1)S(1)} %copy-done.2, bf16[2,96,1024]{2,1,0:T(8,128)(2,1)S(1)} %copy-done.4, bf16[2,96,1024]{2,1,0:T(8,128)(2,1)S(1)} %copy-done.6, bf16[2,96,1024]{2,1,0:T(8,128)(2,1)S(1)} %copy-done.8, ...), custom_call_target="tpu_custom_call" | custom-call | flops 201326592 | bytes 1572864 | tf_op jit(solution)/shard_map/forward/pallas_call | solution.py:316
  76.8 6.3 %all-to-all-start.3 = ((f32[8,96,128]{2,1,0:T(8,128)}), f32[8,96,128]{2,1,0:T(8,128)S(1)}, u32[]{:S(2)}, u32[]{:S(2)}) async-start(f32[8,96,128]{2,1,0:T(8,128)} %forward.1), calls=%async_computation.3 | async-start | bytes 786432 | tf_op jit(solution)/shard_map/all_to_all | solution.py:37
  83.1 0.1 add.29
  83.2 0.1 broadcast_in_dim.32
  83.3 0.2 convert_reduce_fusion
  83.5 0.7 select_reduce_fusion
  84.2 5.8 %all-to-all-done.3.pre = f32[8,96,128]{2,1,0:T(8,128)S(1)} async-done(((f32[8,96,128]{2,1,0:T(8,128)}), f32[8,96,128]{2,1,0:T(8,128)S(1)}, u32[]{:S(2)}, u32[]{:S(2)}) %all-to-all-start.3) | async-done | bytes 393248 | tf_op jit(solution)/shard_map/all_to_all | solution.py:37
  90.0 0.7 copy-done.14
  90.7 1.7 %hidden_grads.1 = bf16[8,96,128]{2,1,0:T(8,128)(2,1)} custom-call(f32[8,96,128]{2,1,0:T(8,128)} %copy-done.14, f32[1,128]{1,0:T(1,128)} %bitcast.11), custom_call_target="tpu_custom_call" | custom-call | flops 1966080 | bytes 589824 | tf_op jit(solution)/shard_map/hidden_grads/pallas_call | solution.py:345
  92.4 10.1 %all_to_all.36.grads = bf16[8,96,128]{2,1,0:T(8,128)(2,1)S(1)} all-to-all(bf16[8,96,128]{2,1,0:T(8,128)(2,1)} %hidden_grads.1), channel_id=1, replica_groups=mesh['y'=4,'z'=16,'x'=4,'core'=2] {'x','core'}, dimensions={0} | all-to-all | bytes 393216 | tf_op jit(solution)/shard_map/all_to_all | solution.py:37
  102.6 1.6 input_grad.1
  104.2 8.0 %all-to-all-start.5 = ((bf16[64,8,256]{2,1,0:T(8,128)(2,1)}), bf16[64,8,256]{2,1,0:T(8,128)(2,1)S(1)}, u32[]{:S(2)}, u32[]{:S(2)}) async-start(bf16[64,8,256]{2,1,0:T(8,128)(2,1)} %input_grad.1), calls=%async_computation.5 | async-start | bytes 524288 | tf_op jit(solution)/shard_map/all_to_all | solution.py:37
  112.2 0.0 copy-start.19
  112.2 0.6 copy-done.19
  112.9 0.1 copy.15.row_scale
  113.0 2.2 %weight_grads.1 = (bf16[2,96,1024]{2,1,0:T(8,128)(2,1)S(1)}, bf16[2,96,1024]{2,1,0:T(8,128)(2,1)S(1)}, bf16[2,96,1024]{2,1,0:T(8,128)(2,1)S(1)}, bf16[2,96,1024]{2,1,0:T(8,128)(2,1)S(1)}) custom-call(s32[4]{0:T(128)S(1)} %copy-done.10, bf16[8,96,128]{2,1,0:T(8,128)(2,1)S(1)} %all_to_all.36.grads, bf16[4,72,1024]{2,1,0:T(8,128)(2,1)S(1)} %all_to_all.35.messages, ...), custom_call_target="tpu_custom_call" | custom-call | flops 201326592 | bytes 1572864 | tf_op jit(solution)/shard_map/weight_grads/pallas_call | solution.py:401
  115.2 0.7 copy-done.9
  115.9 1.9 %collective-permute-start.4 = (bf16[2,96,1024]{2,1,0:T(8,128)(2,1)S(1)}, bf16[2,96,1024]{2,1,0:T(8,128)(2,1)S(1)}, u32[]{:S(2)}, u32[]{:S(2)}) collective-permute-start(bf16[2,96,1024]{2,1,0:T(8,128)(2,1)S(1)} %get-tuple-element.24), channel_id=1, source_target_pairs={{0,6},{2,0},{4,2},{6,4},{1,7},{3,1},{5,3},{7,5},{8,14},{10,8},{12,... | collective-permute-start | bytes 1179656 | tf_op jit(solution)/shard_map/ppermute | solution.py:45
  117.9 5.4 %collective-permute-start.5 = (bf16[2,96,1024]{2,1,0:T(8,128)(2,1)S(1)}, bf16[2,96,1024]{2,1,0:T(8,128)(2,1)S(1)}, u32[]{:S(2)}, u32[]{:S(2)}) collective-permute-start(bf16[2,96,1024]{2,1,0:T(8,128)(2,1)S(1)} %get-tuple-element.25), channel_id=1, source_target_pairs={{0,4},{2,6},{4,0},{6,2},{1,5},{3,7},{5,1},{7,3},{8,12},{10,14},{12... | collective-permute-start | bytes 1179656 | tf_op jit(solution)/shard_map/ppermute | solution.py:45
  123.3 3.1 %collective-permute-start.6 = (bf16[2,96,1024]{2,1,0:T(8,128)(2,1)S(1)}, bf16[2,96,1024]{2,1,0:T(8,128)(2,1)S(1)}, u32[]{:S(2)}, u32[]{:S(2)}) collective-permute-start(bf16[2,96,1024]{2,1,0:T(8,128)(2,1)S(1)} %get-tuple-element.26), channel_id=1, source_target_pairs={{0,2},{2,4},{4,6},{6,0},{1,3},{3,5},{5,7},{7,1},{8,10},{10,12},{12... | collective-permute-start | bytes 1179656 | tf_op jit(solution)/shard_map/ppermute | solution.py:45
  126.4 6.6 %all-to-all-done.5 = bf16[64,8,256]{2,1,0:T(8,128)(2,1)S(1)} async-done(((bf16[64,8,256]{2,1,0:T(8,128)(2,1)}), bf16[64,8,256]{2,1,0:T(8,128)(2,1)S(1)}, u32[]{:S(2)}, u32[]{:S(2)}) %all-to-all-start.5) | async-done | bytes 262176 | tf_op jit(solution)/shard_map/all_to_all | solution.py:37
  132.9 0.1 reduce_sum.41
  133.0 0.7 broadcast_in_dim.53
  133.7 8.6 %all-to-all-start.6 = ((bf16[64,8,256]{2,1,0:T(8,128)(2,1)}), bf16[64,8,256]{2,1,0:T(8,128)(2,1)S(1)}, u32[]{:S(2)}, u32[]{:S(2)}) async-start(bf16[64,8,256]{2,1,0:T(8,128)(2,1)} %broadcast_in_dim.53), calls=%async_computation.6 | async-start | bytes 524288 | tf_op jit(solution)/shard_map/all_to_all | solution.py:37
  142.4 0.7 copy-done.11
  143.1 0.2 copy-done.12
  143.3 0.1 copy-done.13
  143.4 2.2 %join_far.3 = bf16[4,96,1024]{2,1,0:T(8,128)(2,1)} custom-call(bf16[2,96,1024]{2,1,0:T(8,128)(2,1)} %copy-done.9, bf16[2,96,1024]{2,1,0:T(8,128)(2,1)} %copy-done.11, bf16[2,96,1024]{2,1,0:T(8,128)(2,1)} %copy-done.12, bf16[2,96,1024]{2,1,0:T(8,128)(2,1)} %copy-done.13), custom_call_target="tpu_custom_call" | custom-call | bytes 1572864 | tf_op jit(solution)/shard_map/join_far/pallas_call | solution.py:226
  145.6 1.9 %collective-permute-start.7 = (bf16[4,96,1024]{2,1,0:T(8,128)(2,1)}, bf16[4,96,1024]{2,1,0:T(8,128)(2,1)S(1)}, u32[]{:S(2)}, u32[]{:S(2)}) collective-permute-start(bf16[4,96,1024]{2,1,0:T(8,128)(2,1)} %join_far.3), channel_id=1, source_target_pairs={{0,1},{1,0},{2,3},{3,2},{4,5},{5,4},{6,7},{7,6},{8,9},{9,8},{10,11... | collective-permute-start | bytes 2359304 | tf_op jit(solution)/shard_map/ppermute | solution.py:49
  147.5 0.6 fusion.4
  148.2 0.6 iota_add_fusion
  148.8 0.0 copy-start.20
  148.8 0.6 copy-done.20
  149.5 0.1 select_reduce_fusion.1
  149.6 0.7 fusion.1.owner
  150.3 0.9 copy-done.17
  151.2 2.8 %unpack_grads.1 = (bf16[32,8192]{1,0:T(8,128)(2,1)}, bf16[32,8192]{1,0:T(8,128)(2,1)}, bf16[32,8192]{1,0:T(8,128)(2,1)}) custom-call(s32[4]{0:T(128)} %pad_add_fusion.place, bf16[2,96,1024]{2,1,0:T(8,128)(2,1)} %copy-done.9, bf16[2,96,1024]{2,1,0:T(8,128)(2,1)} %copy-done.11, bf16[2,96,1024]{2,1,0:T(8,128)(2,1)} %copy-done.12, ...), custom_call_target="tpu_custom_call" | custom-call | bytes 3145728 | tf_op jit(solution)/shard_map/unpack_grads/pallas_call | solution.py:250
  154.0 7.7 %all-to-all-done.6.blocks = bf16[64,8,256]{2,1,0:T(8,128)(2,1)S(1)} async-done(((bf16[64,8,256]{2,1,0:T(8,128)(2,1)}), bf16[64,8,256]{2,1,0:T(8,128)(2,1)S(1)}, u32[]{:S(2)}, u32[]{:S(2)}) %all-to-all-start.6) | async-done | bytes 262176 | tf_op jit(solution)/shard_map/all_to_all | solution.py:37
  161.7 0.7 copy-done.16
  162.3 2.0 %finish.1 = (bf16[128,1024]{1,0:T(8,128)(2,1)}, f32[128,1024]{1,0:T(8,128)}) custom-call(bf16[64,8,256]{2,1,0:T(8,128)(2,1)} %copy-done.16, bf16[128,128]{1,0:T(8,128)(2,1)} %fusion.1.owner, bf16[128,1024]{1,0:T(8,128)(2,1)} %grad_out.3), custom_call_target="tpu_custom_call" | custom-call | flops 33554432 | bytes 1310720 | tf_op jit(solution)/shard_map/finish/pallas_call | solution.py:427
  (37 shorter events, 0.2 us)
Async XLA Ops:
  3.2 19.9 %all-to-all-start = ((bf16[4,16,1152]{2,1,0:T(8,128)(2,1)}), bf16[4,16,1152]{2,1,0:T(8,128)(2,1)S(1)}, u32[]{:S(2)}, u32[]{:S(2)}) async-start(bf16[4,16,1152]{2,1,0:T(8,128)(2,1)} %pick_rows.1._), calls=%async_computation | async-start | bytes 294912 | tf_op jit(solution)/shard_map/all_to_all | solution.py:37
  11.7 26.6 %collective-permute-start = (bf16[2,96,1024]{2,1,0:T(8,128)(2,1)}, bf16[2,96,1024]{2,1,0:T(8,128)(2,1)S(1)}, u32[]{:S(2)}, u32[]{:S(2)}) collective-permute-start(bf16[2,96,1024]{2,1,0:T(8,128)(2,1)} %get-tuple-element.19._1), channel_id=1, source_target_pairs={{0,2},{2,4},{4,6},{6,0},{1,3},{3,5},{5,7},{7,1},{8,10},{10,12},{12... | collective-permute-start | bytes 1179656 | tf_op jit(solution)/shard_map/ppermute | solution.py:45
  18.4 19.9 %collective-permute-start.1 = (bf16[2,96,1024]{2,1,0:T(8,128)(2,1)}, bf16[2,96,1024]{2,1,0:T(8,128)(2,1)S(1)}, u32[]{:S(2)}, u32[]{:S(2)}) collective-permute-start(bf16[2,96,1024]{2,1,0:T(8,128)(2,1)} %get-tuple-element.20._2), channel_id=1, source_target_pairs={{0,4},{2,6},{4,0},{6,2},{1,5},{3,7},{5,1},{7,3},{8,12},{10,14},{12... | collective-permute-start | bytes 1179656 | tf_op jit(solution)/shard_map/ppermute | solution.py:45
  20.3 18.0 %collective-permute-start.2 = (bf16[2,96,1024]{2,1,0:T(8,128)(2,1)}, bf16[2,96,1024]{2,1,0:T(8,128)(2,1)S(1)}, u32[]{:S(2)}, u32[]{:S(2)}) collective-permute-start(bf16[2,96,1024]{2,1,0:T(8,128)(2,1)} %get-tuple-element.21._3), channel_id=1, source_target_pairs={{0,6},{2,0},{4,2},{6,4},{1,7},{3,1},{5,3},{7,5},{8,14},{10,8},{12,... | collective-permute-start | bytes 1179656 | tf_op jit(solution)/shard_map/ppermute | solution.py:45
  23.1 0.7 copy-start.18
  25.8 31.6 %all-to-all-start.1 = ((bf16[16,8,1152]{2,1,0:T(8,128)(2,1)}), bf16[16,8,1152]{2,1,0:T(8,128)(2,1)S(1)}, u32[]{:S(2)}, u32[]{:S(2)}) async-start(bf16[16,8,1152]{2,1,0:T(8,128)(2,1)} %select_rows.1), calls=%async_computation.1 | async-start | bytes 589824 | tf_op jit(solution)/shard_map/all_to_all | solution.py:37
  38.3 0.7 copy-start.3
  38.3 0.9 copy-start.5
  39.2 0.7 copy-start.7
  42.1 4.4 %collective-permute-start.3 = (bf16[4,96,1024]{2,1,0:T(8,128)(2,1)}, bf16[4,96,1024]{2,1,0:T(8,128)(2,1)S(1)}, u32[]{:S(2)}, u32[]{:S(2)}) collective-permute-start(bf16[4,96,1024]{2,1,0:T(8,128)(2,1)} %join_far.2), channel_id=1, source_target_pairs={{0,1},{1,0},{2,3},{3,2},{4,5},{5,4},{6,7},{7,6},{8,9},{9,8},{10,11... | collective-permute-start | bytes 2359304 | tf_op jit(solution)/shard_map/ppermute | solution.py:49
  46.5 10.9 %copy-start = (bf16[4,96,1024]{2,1,0:T(8,128)(2,1)}, bf16[4,96,1024]{2,1,0:T(8,128)(2,1)S(1)}, u32[]{:S(2)}) copy-start(bf16[4,96,1024]{2,1,0:T(8,128)(2,1)S(1)} %collective-permute-done.3._.far) | copy-start | bytes 2359300
  57.4 0.7 copy-start.15
  58.1 15.5 %copy-start.4 = (bf16[2,96,1024]{2,1,0:T(8,128)(2,1)S(1)}, bf16[2,96,1024]{2,1,0:T(8,128)(2,1)}, u32[]{:S(2)}) copy-start(bf16[2,96,1024]{2,1,0:T(8,128)(2,1)} %copy-done.3) | copy-start | bytes 1179652
  58.1 15.5 %copy-start.6 = (bf16[2,96,1024]{2,1,0:T(8,128)(2,1)S(1)}, bf16[2,96,1024]{2,1,0:T(8,128)(2,1)}, u32[]{:S(2)}) copy-start(bf16[2,96,1024]{2,1,0:T(8,128)(2,1)} %copy-done.5) | copy-start | bytes 1179652
  58.1 15.5 %copy-start.8 = (bf16[2,96,1024]{2,1,0:T(8,128)(2,1)S(1)}, bf16[2,96,1024]{2,1,0:T(8,128)(2,1)}, u32[]{:S(2)}) copy-start(bf16[2,96,1024]{2,1,0:T(8,128)(2,1)} %copy-done.7) | copy-start | bytes 1179652
  60.4 13.1 %copy-start.1 = (bf16[4,96,1024]{2,1,0:T(8,128)(2,1)S(1)}, bf16[4,96,1024]{2,1,0:T(8,128)(2,1)}, u32[]{:S(2)}) copy-start(bf16[4,96,1024]{2,1,0:T(8,128)(2,1)} %copy-done) | copy-start | bytes 2359300
  60.4 13.1 %copy-start.2 = (bf16[2,96,1024]{2,1,0:T(8,128)(2,1)S(1)}, bf16[2,96,1024]{2,1,0:T(8,128)(2,1)}, u32[]{:S(2)}) copy-start(bf16[2,96,1024]{2,1,0:T(8,128)(2,1)} %get-tuple-element.18._0.refs_0_.w0) | copy-start | bytes 1179652
  73.4 0.7 copy-start.10
  76.8 13.2 %all-to-all-start.3 = ((f32[8,96,128]{2,1,0:T(8,128)}), f32[8,96,128]{2,1,0:T(8,128)S(1)}, u32[]{:S(2)}, u32[]{:S(2)}) async-start(f32[8,96,128]{2,1,0:T(8,128)} %forward.1), calls=%async_computation.3 | async-start | bytes 786432 | tf_op jit(solution)/shard_map/all_to_all | solution.py:37
  90.0 0.7 copy-start.14
  104.2 28.8 %all-to-all-start.5 = ((bf16[64,8,256]{2,1,0:T(8,128)(2,1)}), bf16[64,8,256]{2,1,0:T(8,128)(2,1)S(1)}, u32[]{:S(2)}, u32[]{:S(2)}) async-start(bf16[64,8,256]{2,1,0:T(8,128)(2,1)} %input_grad.1), calls=%async_computation.5 | async-start | bytes 524288 | tf_op jit(solution)/shard_map/all_to_all | solution.py:37
  112.2 0.7 copy-start.19
  115.2 0.8 copy-start.9
  115.9 26.4 %collective-permute-start.4 = (bf16[2,96,1024]{2,1,0:T(8,128)(2,1)S(1)}, bf16[2,96,1024]{2,1,0:T(8,128)(2,1)S(1)}, u32[]{:S(2)}, u32[]{:S(2)}) collective-permute-start(bf16[2,96,1024]{2,1,0:T(8,128)(2,1)S(1)} %get-tuple-element.24), channel_id=1, source_target_pairs={{0,6},{2,0},{4,2},{6,4},{1,7},{3,1},{5,3},{7,5},{8,14},{10,8},{12,... | collective-permute-start | bytes 1179656 | tf_op jit(solution)/shard_map/ppermute | solution.py:45
  117.9 24.5 %collective-permute-start.5 = (bf16[2,96,1024]{2,1,0:T(8,128)(2,1)S(1)}, bf16[2,96,1024]{2,1,0:T(8,128)(2,1)S(1)}, u32[]{:S(2)}, u32[]{:S(2)}) collective-permute-start(bf16[2,96,1024]{2,1,0:T(8,128)(2,1)S(1)} %get-tuple-element.25), channel_id=1, source_target_pairs={{0,4},{2,6},{4,0},{6,2},{1,5},{3,7},{5,1},{7,3},{8,12},{10,14},{12... | collective-permute-start | bytes 1179656 | tf_op jit(solution)/shard_map/ppermute | solution.py:45
  123.3 19.1 %collective-permute-start.6 = (bf16[2,96,1024]{2,1,0:T(8,128)(2,1)S(1)}, bf16[2,96,1024]{2,1,0:T(8,128)(2,1)S(1)}, u32[]{:S(2)}, u32[]{:S(2)}) collective-permute-start(bf16[2,96,1024]{2,1,0:T(8,128)(2,1)S(1)} %get-tuple-element.26), channel_id=1, source_target_pairs={{0,2},{2,4},{4,6},{6,0},{1,3},{3,5},{5,7},{7,1},{8,10},{10,12},{12... | collective-permute-start | bytes 1179656 | tf_op jit(solution)/shard_map/ppermute | solution.py:45
  133.7 27.9 %all-to-all-start.6 = ((bf16[64,8,256]{2,1,0:T(8,128)(2,1)}), bf16[64,8,256]{2,1,0:T(8,128)(2,1)S(1)}, u32[]{:S(2)}, u32[]{:S(2)}) async-start(bf16[64,8,256]{2,1,0:T(8,128)(2,1)} %broadcast_in_dim.53), calls=%async_computation.6 | async-start | bytes 524288 | tf_op jit(solution)/shard_map/all_to_all | solution.py:37
  142.3 0.8 copy-start.11
  142.4 0.9 copy-start.12
  142.4 1.0 copy-start.13
  145.6 4.7 %collective-permute-start.7 = (bf16[4,96,1024]{2,1,0:T(8,128)(2,1)}, bf16[4,96,1024]{2,1,0:T(8,128)(2,1)S(1)}, u32[]{:S(2)}, u32[]{:S(2)}) collective-permute-start(bf16[4,96,1024]{2,1,0:T(8,128)(2,1)} %join_far.3), channel_id=1, source_target_pairs={{0,1},{1,0},{2,3},{3,2},{4,5},{5,4},{6,7},{7,6},{8,9},{9,8},{10,11... | collective-permute-start | bytes 2359304 | tf_op jit(solution)/shard_map/ppermute | solution.py:49
  148.8 0.7 copy-start.20
  150.3 0.9 copy-start.17
  161.7 0.7 copy-start.16

commit v4 on v3

--- a/solution.py
+++ b/solution.py
@@ -84,18 +84,19 @@
     )(keep_count, keep_pos, router, tokens, grad_out)
 
 
-def select_kernel(place, column, _0, _1, _2, _3, out):
+def select_kernel(column, out):
+    yi, zi = lax.axis_index("y"), lax.axis_index("z")
     flat = column[...].reshape(64, column.shape[2])
     width = column.shape[2] - 128
     row = lax.broadcasted_iota(jnp.int32, (64, 128), 0)
     lane = lax.broadcasted_iota(jnp.int32, (64, 128), 1)
-    shard = (row // 16 * NZ + place[3]).astype(F32).astype(BF)
+    shard = (row // 16 * NZ + zi).astype(F32).astype(BF)
     meta = jnp.where(lane == 2, shard, flat[:, width:])
     m = lax.broadcasted_iota(jnp.int32, (64, 8), 0)
     o = lax.broadcasted_iota(jnp.int32, (64, 8), 1)
     qy, half, qj = m // 16, m // 8 % 2, m % 8
     valid = flat[:, width + 1 : width + 2].astype(F32) > 0.5
-    heavy = place[3] < HEAVY
+    heavy = zi < HEAVY
     steady = jnp.where(
         heavy,
         jnp.where(qy == 0, jnp.where(qj < MOST, qj, 99), jnp.where(qj == 0, 5 + qy, 99)),
@@ -108,11 +109,11 @@
     before = jnp.where((c < r) & (c // 8 % 2 == r // 8 % 2), 1.0, 0.0).astype(BF)
     nth = jnp.dot(before, extra.astype(BF), preferred_element_type=F32)
     p = o % 4
-    turn = lax.rem(place[2] - place[3] + NZ, NY)
+    turn = lax.rem(yi - zi + NZ, NY)
     take = jnp.where(
         p < 3,
         jnp.where(steady == 4 * p + turn, 1.0, 0.0),
-        jnp.where(nth == place[2].astype(F32), extra, 0.0),
+        jnp.where(nth == yi.astype(F32), extra, 0.0),
     )
     hot = jnp.where(half == o // 4, take, 0.0).astype(BF)
     picked = t_dot(hot, flat[:, :width]).astype(BF)
@@ -122,15 +123,15 @@
         out[z, :, width:] = facts
 
 
-def select_rows(place, column, after):
+def select_rows(column):
     return pl.pallas_call(
         select_kernel,
-        in_specs=[SMEM, VMEM] + [ANY] * NX,
+        in_specs=[VMEM],
         out_specs=VMEM,
         out_shape=jax.ShapeDtypeStruct((NZ, 8, column.shape[2]), BF),
         cost_estimate=cost(16 * column.size, 8 * column.size),
         name="select_rows",
-    )(place, column, *after)
+    )(column)
 
 
 def compact_kernel(plane, _, out):
@@ -177,8 +178,9 @@
         copy.wait()
 
 
-def peer(place, s, d):
-    return lax.rem(place[0] + s + NX, NX) * NC + lax.rem(place[1] + d, NC)
+def peer(s, d):
+    x, core = lax.axis_index("x"), lax.axis_index("core")
+    return lax.rem(x + s + NX, NX) * NC + lax.rem(core + d, NC)
 
 
 def features(whole, t, width):
@@ -190,28 +192,28 @@
     return pl.ds(k * units, units)
 
 
-def pack_kernel(place, gate_w, up_w, down_w, _, out0, out1, out2, out3, sems):
+def pack_kernel(gate_w, up_w, down_w, _, out0, out1, out2, out3, sems):
     width = out0.shape[2]
     pairs = []
     for s, out in enumerate((out0, out1, out2, out3)):
         for d in range(NC):
             for k, w in enumerate((gate_w, up_w, down_w)):
-                pairs.append((features(w, peer(place, s, d), width), out.at[d, third(out, k)]))
+                pairs.append((features(w, peer(s, d), width), out.at[d, third(out, k)]))
     run_copies(pairs, sems)
 
 
-def pack_weights(place, gate_weight, up_weight, down_weight, after):
+def pack_weights(gate_weight, up_weight, down_weight, after):
     units, full = gate_weight.shape
     out = jax.ShapeDtypeStruct((NC, 3 * units, full // NT), BF)
     return pl.pallas_call(
         pack_kernel,
-        in_specs=[SMEM, ANY, ANY, ANY, ANY],
+        in_specs=[ANY] * 4,
         out_specs=[VMEM] * NX,
         out_shape=[out] * NX,
         scratch_shapes=[pltpu.SemaphoreType.DMA((3 * NT,))],
         cost_estimate=cost(0, 12 * units * full),
         name="pack_weights",
-    )(place, gate_weight, up_weight, down_weight, after)
+    )(gate_weight, up_weight, down_weight, after)
 
 
 def join_kernel(*refs):
@@ -234,29 +236,29 @@
     )(*parts)
 
 
-def unpack_kernel(place, in0, in1, in2, in3, far, grad_gate, grad_up, grad_down, sems):
+def unpack_kernel(in0, in1, in2, in3, far, grad_gate, grad_up, grad_down, sems):
     width = far.shape[2]
     pairs = []
     for s, near in enumerate((in0, in1, in2, in3)):
         for d, part in enumerate((near.at[0], far.at[s])):
             for k, out in enumerate((grad_gate, grad_up, grad_down)):
-                pairs.append((part.at[third(near, k)], features(out, peer(place, s, d), width)))
+                pairs.append((part.at[third(near, k)], features(out, peer(s, d), width)))
     run_copies(pairs, sems)
 
 
-def unpack_grads(place, parts, far):
+def unpack_grads(parts, far):
     _, units3, width = far.shape
     out = jax.ShapeDtypeStruct((units3 // 3, NT * width), BF)
     return pl.pallas_call(
         unpack_kernel,
         grid=(1,),
-        in_specs=[SMEM] + [near_spec(units3, width)] * NX + [VMEM],
+        in_specs=[near_spec(units3, width)] * NX + [VMEM],
         out_specs=[ANY] * 3,
         out_shape=[out] * 3,
         scratch_shapes=[pltpu.SemaphoreType.DMA((3 * NT,))],
         cost_estimate=cost(0, 4 * NT * units3 * width),
         name="unpack_grads",
-    )(place, *parts, far)
+    )(*parts, far)
 
 
 def near_spec(units3, width):
@@ -296,7 +298,7 @@
     return total.astype(BF)
 
 
-def forward_kernel(place, messages, w0, w1, w2, w3, far, pre):
+def forward_kernel(messages, w0, w1, w2, w3, far, pre):
     _, units3, width = far.shape
     units = units3 // 3
     ordered = order_rows(messages)
@@ -306,23 +308,23 @@
     down = jnp.concatenate([w[2 * units :] for _, _, w in blocks], axis=0)
     down = dot_t(down, ordered[KEPT:])
     for i, (s, d, _) in enumerate(blocks):
-        t = peer(place, -s, d)
+        t = peer(-s, d)
         pre[t, : 2 * units] = both[2 * units * i : 2 * units * (i + 1)]
         pre[t, 2 * units :] = down[units * i : units * (i + 1)]
 
 
-def forward(place, messages, near, far):
+def forward(messages, near, far):
     _, units3, width = far.shape
     return pl.pallas_call(
         forward_kernel,
         grid=(1,),
-        in_specs=[SMEM, VMEM] + [near_spec(units3, width)] * NX + [VMEM],
+        in_specs=[VMEM] + [near_spec(units3, width)] * NX + [VMEM],
         out_specs=VMEM,
         out_shape=jax.ShapeDtypeStruct((NT, units3, KEPT), F32),
         cost_estimate=cost(2 * NT * units3 * width * KEPT, 2 * NT * units3 * width),
         compiler_params=ROOM,
         name="forward",
-    )(place, messages, *near, far)
+    )(messages, *near, far)
 
 
 def hidden_kernel(pre, row_scale, out):
@@ -352,11 +354,11 @@
     )(pre, row_scale)
 
 
-def input_grad_kernel(place, grads, w0, w1, w2, w3, far, out):
+def input_grad_kernel(grads, w0, w1, w2, w3, far, out):
     _, units3, width = far.shape
     units2 = units3 // 3 * 2
     blocks = list(blocks_of((w0, w1, w2, w3), far))
-    g = jnp.concatenate([grads[peer(place, -s, d), :units2] for s, d, _ in blocks], axis=0)
+    g = jnp.concatenate([grads[peer(-s, d), :units2] for s, d, _ in blocks], axis=0)
     w = jnp.concatenate([w[:units2] for _, _, w in blocks], axis=0)
     total = t_dot(g, w).astype(BF)
     wide = width // COLS
@@ -365,22 +367,22 @@
             out[wide * i + k] = total[ROWS * i : ROWS * (i + 1), COLS * k : COLS * (k + 1)]
 
 
-def input_grad(place, grads, near, far):
+def input_grad(grads, near, far):
     _, units3, width = far.shape
     pieces = KEPT // ROWS * (width // COLS)
     return pl.pallas_call(
         input_grad_kernel,
         grid=(1,),
-        in_specs=[SMEM, VMEM] + [near_spec(units3, width)] * NX + [VMEM],
+        in_specs=[VMEM] + [near_spec(units3, width)] * NX + [VMEM],
         out_specs=VMEM,
         out_shape=jax.ShapeDtypeStruct((pieces, ROWS, COLS), BF),
         cost_estimate=cost(2 * NT * units3 * width * KEPT, 2 * NT * units3 * width),
         compiler_params=ROOM,
         name="input_grad",
-    )(place, grads, *near, far)
-
-
-def weight_grads_kernel(place, grads, messages, row_scale, out0, out1, out2, out3):
+    )(grads, *near, far)
+
+
+def weight_grads_kernel(grads, messages, row_scale, out0, out1, out2, out3):
     _, units3, _ = out0.shape
     units = units3 // 3
     rows = order_rows(messages)
@@ -388,25 +390,25 @@
     scaled_dy = (row_scale[...] * rows[KEPT:].astype(F32)).astype(BF)
     for s, out in enumerate((out0, out1, out2, out3)):
         for d in range(NC):
-            g = grads[peer(place, -s, d)]
+            g = grads[peer(-s, d)]
             both = jnp.dot(g[: 2 * units], x, preferred_element_type=F32)
             out[d, : 2 * units] = both.astype(BF)
             down = jnp.dot(g[2 * units :], scaled_dy, preferred_element_type=F32)
             out[d, 2 * units :] = down.astype(BF)
 
 
-def weight_grads(place, grads, messages, row_scale):
+def weight_grads(grads, messages, row_scale):
     _, units3, _ = grads.shape
     width = messages.shape[2]
     return pl.pallas_call(
         weight_grads_kernel,
-        in_specs=[SMEM] + [VMEM] * 3,
+        in_specs=[VMEM] * 3,
         out_specs=[VMEM] * NX,
         out_shape=[jax.ShapeDtypeStruct((NC, units3, width), BF)] * NX,
         cost_estimate=cost(2 * NT * units3 * width * KEPT, 2 * NT * units3 * width),
         compiler_params=ROOM,
         name="weight_grads",
-    )(place, grads, messages, row_scale)
+    )(grads, messages, row_scale)
 
 
 def finish_kernel(blocks, owner, grad_out, grad_tokens, summed):
@@ -441,16 +443,15 @@
     tok_dev, width = tokens.shape
     yi, zi = lax.axis_index("y"), lax.axis_index("z")
     shard = yi * NZ + zi
-    place = jnp.stack([lax.axis_index("x"), lax.axis_index("core"), yi, zi])
     tensor, context = ("x", "core"), ("y", "z")
 
     picked = pick_rows(keep_count, keep_pos, router, tokens, grad_out)
     column = exchange(picked, "y")
 
-    sent = pack_weights(place, gate_weight, up_weight, down_weight, picked)
+    sent = pack_weights(gate_weight, up_weight, down_weight, picked)
     near = [sent[0]] + [along_x(sent[s], s) for s in range(1, NX)]
     far = other_core(join_far(near))
-    plane = exchange(select_rows(place, column, sent), "z")
+    plane = exchange(select_rows(column), "z")
     messages = exchange(compact_rows(plane, far), "y")
 
     facts = messages[:, 2 * PLANE, :512].reshape(NY, 4, 128).astype(F32)[:, :, :PLANE]
@@ -462,11 +463,11 @@
     row_scale = jnp.sum(jnp.where(hot, facts[0][None, :], 0.0), axis=1)
     start_here = jnp.sum((valid & (facts[2] < shard.astype(F32))).astype(jnp.int32))
 
-    pre = forward(place, messages, near, far)
+    pre = forward(messages, near, far)
     grads = hidden_grads(exchange(pre, tensor), row_scale[None, :])
     grads = exchange(grads, tensor)
-    blocks = exchange(input_grad(place, grads, near, far), context)
-    units = weight_grads(place, grads, messages, row_scale[:, None])
+    blocks = exchange(input_grad(grads, near, far), context)
+    units = weight_grads(grads, messages, row_scale[:, None])
     units = [units[0]] + [along_x(units[s], -s) for s in range(1, NX)]
     far_units = other_core(join_far(units))
     block = jnp.sum(blocks.astype(F32), axis=0).astype(BF)
@@ -477,7 +478,7 @@
     slot_of = jnp.max(jnp.where(token_is, start_here + j6[None, :], -1), axis=1)
     owner = (slot_of[:, None] == jnp.arange(KEPT)[None, :]).astype(BF)
     grad_tokens, summed = finish(blocks, owner, grad_out)
-    grad_gate, grad_up, grad_down = unpack_grads(place, units, far_units)
+    grad_gate, grad_up, grad_down = unpack_grads(units, far_units)
     return (grad_tokens, grad_gate, grad_up, grad_down, summed)
 
 

time: 166 us -> 163 us (0.982)
  Pallas kernels: 27 us -> 24.7 us
    pallas_call x6, Pallas kernels: 14.8 us -> 12.5 us  [the longest x1 2.82 us: unpack_grads(): pl.pallas_call(unpack_kernel, grid=(1,), in_specs=[near_spec(units3, widt...]
    unnamed x42 -> x40, local copies, waits for them, and re-layouts: 8.89 us -> 7.75 us
  transfers between devices with their start and end apart: 13 -> 13, of which waited for: 5 -> 5; matrix products, arithmetic and copies ran while one was open for 3% -> 3% of each run, Pallas kernels for 9% -> 8%
where the time goes in v4:
time: 163 us; the launch traced here: 161 us
  starting transfers between devices  64.9 us (40%)
  waiting for transfers between devices  34.6 us (21%)
  Pallas kernels  24.7 us (15%)
  blocking collectives  23.1 us (14%)
  local copies, waits for them, and re-layouts  8.89 us (5%)
  other arithmetic  3.07 us (2%)
    all_to_all x5, starting transfers between devices, exchange(): return lax.all_to_all(pieces, axes, 0, 0, tiled=True)  39.3 us
    all_to_all x5, waiting for transfers between devices, exchange(): return lax.all_to_all(pieces, axes, 0, 0, tiled=True)  32.1 us
    all_to_all x2, blocking collectives, exchange(): return lax.all_to_all(pieces, axes, 0, 0, tiled=True)  23.1 us
    ppermute x6, starting transfers between devices, along_x(): return lax.ppermute(array, 'x', [(i, (i + s) % NX) for i in range(NX)])  21.8 us
    unnamed x40, local copies, waits for them, and re-layouts  7.75 us
    pallas_call x2, Pallas kernels, join_far(): pl.pallas_call(join_kernel, grid=(1,), in_specs=[pl.BlockSpec((1, units3,...  4.34 us
    ppermute x2, starting transfers between devices, other_core(): return lax.ppermute(array, 'core', [(0, 1), (1, 0)])  3.82 us
  transfers between devices with their start and end apart: 13, of which 5 were waited for; matrix products, arithmetic and copies ran while one was open for 3% of the time, Pallas kernels for 8%

profile of v4, /device:TPU:6, one launch (start us, length us, event | category | flops | bytes accessed | tf_op | source)
XLA Modules:
  0.0 160.8 jit_solution(12991896246544950304)
XLA Ops:
  1.3 1.9 %pick_rows.1._ = bf16[4,16,1152]{2,1,0:T(8,128)(2,1)} custom-call(s32[1]{0:T(128)} %copy.16.count, s32[1,6]{1,0:T(1,128)} %pos.1, bf16[1,6]{1,0:T(2,128)(2,1)} %router.1, bf16[128,1024]{1,0:T(8,128)(2,1)} %tokens.1, bf16[128,1024]{1,0:T(8,128)(2,1)} %grad_out.3), custom_call_target="tpu_custom_call" | custom-call | flops 4194304 | bytes 524288 | tf_op jit(solution)/shard_map/pick_rows/pallas_call | solution.py:77
  3.2 4.5 %all-to-all-start = ((bf16[4,16,1152]{2,1,0:T(8,128)(2,1)}), bf16[4,16,1152]{2,1,0:T(8,128)(2,1)S(1)}, u32[]{:S(2)}, u32[]{:S(2)}) async-start(bf16[4,16,1152]{2,1,0:T(8,128)(2,1)} %pick_rows.1._), calls=%async_computation | async-start | bytes 294912 | tf_op jit(solution)/shard_map/all_to_all | solution.py:37
  7.7 2.8 %pack_weights.1 = (bf16[2,96,1024]{2,1,0:T(8,128)(2,1)}, bf16[2,96,1024]{2,1,0:T(8,128)(2,1)}, bf16[2,96,1024]{2,1,0:T(8,128)(2,1)}, bf16[2,96,1024]{2,1,0:T(8,128)(2,1)}) custom-call(bf16[32,8192]{1,0:T(8,128)(2,1)} %gate_w.1, bf16[32,8192]{1,0:T(8,128)(2,1)} %up_w.1, bf16[32,8192]{1,0:T(8,128)(2,1)} %down_w.1, bf16[4,16,1152]{2,1,0:T(8,128)(2,1)} %pick_rows.1._), custom_call_target="tpu_custom_call" | custom-call | bytes 3145728 | tf_op jit(solution)/shard_map/pack_weights/pallas_call | solution.py:208
  10.4 6.7 %collective-permute-start = (bf16[2,96,1024]{2,1,0:T(8,128)(2,1)}, bf16[2,96,1024]{2,1,0:T(8,128)(2,1)S(1)}, u32[]{:S(2)}, u32[]{:S(2)}) collective-permute-start(bf16[2,96,1024]{2,1,0:T(8,128)(2,1)} %get-tuple-element.19), channel_id=1, source_target_pairs={{0,2},{2,4},{4,6},{6,0},{1,3},{3,5},{5,7},{7,1},{8,10},{10,12},{12... | collective-permute-start | bytes 1179656 | tf_op jit(solution)/shard_map/ppermute | solution.py:45
  17.1 1.9 %collective-permute-start.1 = (bf16[2,96,1024]{2,1,0:T(8,128)(2,1)}, bf16[2,96,1024]{2,1,0:T(8,128)(2,1)S(1)}, u32[]{:S(2)}, u32[]{:S(2)}) collective-permute-start(bf16[2,96,1024]{2,1,0:T(8,128)(2,1)} %get-tuple-element.20), channel_id=1, source_target_pairs={{0,4},{2,6},{4,0},{6,2},{1,5},{3,7},{5,1},{7,3},{8,12},{10,14},{12... | collective-permute-start | bytes 1179656 | tf_op jit(solution)/shard_map/ppermute | solution.py:45
  19.0 2.8 %collective-permute-start.2 = (bf16[2,96,1024]{2,1,0:T(8,128)(2,1)}, bf16[2,96,1024]{2,1,0:T(8,128)(2,1)S(1)}, u32[]{:S(2)}, u32[]{:S(2)}) collective-permute-start(bf16[2,96,1024]{2,1,0:T(8,128)(2,1)} %get-tuple-element.21), channel_id=1, source_target_pairs={{0,6},{2,0},{4,2},{6,4},{1,7},{3,1},{5,3},{7,5},{8,14},{10,8},{12,... | collective-permute-start | bytes 1179656 | tf_op jit(solution)/shard_map/ppermute | solution.py:45
  21.8 0.0 copy-start.17
  21.8 0.7 copy-done.17
  22.5 2.0 %select_rows.1 = bf16[16,8,1152]{2,1,0:T(8,128)(2,1)} custom-call(bf16[4,16,1152]{2,1,0:T(8,128)(2,1)} %copy-done.17), custom_call_target="tpu_custom_call" | custom-call | flops 1179648 | bytes 589824 | tf_op jit(solution)/shard_map/select_rows/pallas_call | solution.py:127
  24.5 12.5 %all-to-all-start.1 = ((bf16[16,8,1152]{2,1,0:T(8,128)(2,1)}), bf16[16,8,1152]{2,1,0:T(8,128)(2,1)S(1)}, u32[]{:S(2)}, u32[]{:S(2)}) async-start(bf16[16,8,1152]{2,1,0:T(8,128)(2,1)} %select_rows.1), calls=%async_computation.1 | async-start | bytes 589824 | tf_op jit(solution)/shard_map/all_to_all | solution.py:37
  37.0 0.0 copy-start.3
  37.0 0.0 copy-start.5
  37.0 0.0 copy-start.7
  37.0 0.7 copy-done.3
  37.7 0.1 copy-done.5
  37.9 0.1 copy-done.7
  38.0 2.2 %join_far.2 = bf16[4,96,1024]{2,1,0:T(8,128)(2,1)} custom-call(bf16[2,96,1024]{2,1,0:T(8,128)(2,1)} %get-tuple-element.18.refs_0_.w0, bf16[2,96,1024]{2,1,0:T(8,128)(2,1)} %copy-done.3, bf16[2,96,1024]{2,1,0:T(8,128)(2,1)} %copy-done.5, bf16[2,96,1024]{2,1,0:T(8,128)(2,1)} %copy-done.7), custom_call_target="tpu_custom_call" | custom-call | bytes 1572864 | tf_op jit(solution)/shard_map/join_far/pallas_call | solution.py:228
  40.2 1.9 %collective-permute-start.3 = (bf16[4,96,1024]{2,1,0:T(8,128)(2,1)}, bf16[4,96,1024]{2,1,0:T(8,128)(2,1)S(1)}, u32[]{:S(2)}, u32[]{:S(2)}) collective-permute-start(bf16[4,96,1024]{2,1,0:T(8,128)(2,1)} %join_far.2), channel_id=1, source_target_pairs={{0,1},{1,0},{2,3},{3,2},{4,5},{5,4},{6,7},{7,6},{8,9},{9,8},{10,11... | collective-permute-start | bytes 2359304 | tf_op jit(solution)/shard_map/ppermute | solution.py:49
  42.1 2.5 %collective-permute-done.3._.far = bf16[4,96,1024]{2,1,0:T(8,128)(2,1)S(1)} collective-permute-done((bf16[4,96,1024]{2,1,0:T(8,128)(2,1)}, bf16[4,96,1024]{2,1,0:T(8,128)(2,1)S(1)}, u32[]{:S(2)}, u32[]{:S(2)}) %collective-permute-start.3) | collective-permute-done | bytes 786464 | tf_op jit(solution)/shard_map/ppermute | solution.py:49
  44.5 11.5 %all-to-all-done.1.plane = bf16[16,8,1152]{2,1,0:T(8,128)(2,1)S(1)} async-done(((bf16[16,8,1152]{2,1,0:T(8,128)(2,1)}), bf16[16,8,1152]{2,1,0:T(8,128)(2,1)S(1)}, u32[]{:S(2)}, u32[]{:S(2)}) %all-to-all-start.1) | async-done | bytes 294944 | tf_op jit(solution)/shard_map/all_to_all | solution.py:37
  56.1 0.7 copy-done.14
  56.8 2.3 %compact_rows.1 = bf16[4,72,1024]{2,1,0:T(8,128)(2,1)} custom-call(bf16[16,8,1152]{2,1,0:T(8,128)(2,1)} %copy-done.14, bf16[4,96,1024]{2,1,0:T(8,128)(2,1)} %copy-done), custom_call_target="tpu_custom_call" | custom-call | flops 37748736 | bytes 1179648 | tf_op jit(solution)/shard_map/compact_rows/pallas_call | solution.py:160
  59.1 12.9 %all_to_all.35.messages = bf16[4,72,1024]{2,1,0:T(8,128)(2,1)S(1)} all-to-all(bf16[4,72,1024]{2,1,0:T(8,128)(2,1)} %compact_rows.1), channel_id=1, replica_groups=mesh['y'=4,'z'=16,'x'=4,'core'=2] {'y'}, dimensions={0} | all-to-all | bytes 1179648 | tf_op jit(solution)/shard_map/all_to_all | solution.py:37
  72.1 0.1 gt.16
  72.2 2.2 %forward.1 = f32[8,96,128]{2,1,0:T(8,128)} custom-call(bf16[4,72,1024]{2,1,0:T(8,128)(2,1)S(1)} %all_to_all.35.messages, bf16[2,96,1024]{2,1,0:T(8,128)(2,1)S(1)} %copy-done.2, bf16[2,96,1024]{2,1,0:T(8,128)(2,1)S(1)} %copy-done.4, bf16[2,96,1024]{2,1,0:T(8,128)(2,1)S(1)} %copy-done.6, bf16[2,96,1024]{2,1,0:T(8,128)(2,1)S(1)} %copy-done.8, ...), custom_call_target="tpu_custom_call" | custom-call | flops 201326592 | bytes 1572864 | tf_op jit(solution)/shard_map/forward/pallas_call | solution.py:318
  74.4 6.3 %all-to-all-start.3 = ((f32[8,96,128]{2,1,0:T(8,128)}), f32[8,96,128]{2,1,0:T(8,128)S(1)}, u32[]{:S(2)}, u32[]{:S(2)}) async-start(f32[8,96,128]{2,1,0:T(8,128)} %forward.1), calls=%async_computation.3 | async-start | bytes 786432 | tf_op jit(solution)/shard_map/all_to_all | solution.py:37
  80.7 0.1 add.29
  80.8 0.1 broadcast_in_dim.32
  80.9 0.2 convert_reduce_fusion
  81.1 0.7 select_reduce_fusion
  81.8 5.8 %all-to-all-done.3.pre = f32[8,96,128]{2,1,0:T(8,128)S(1)} async-done(((f32[8,96,128]{2,1,0:T(8,128)}), f32[8,96,128]{2,1,0:T(8,128)S(1)}, u32[]{:S(2)}, u32[]{:S(2)}) %all-to-all-start.3) | async-done | bytes 393248 | tf_op jit(solution)/shard_map/all_to_all | solution.py:37
  87.6 0.7 copy-done.13
  88.3 1.7 %hidden_grads.1 = bf16[8,96,128]{2,1,0:T(8,128)(2,1)} custom-call(f32[8,96,128]{2,1,0:T(8,128)} %copy-done.13, f32[1,128]{1,0:T(1,128)} %bitcast.7), custom_call_target="tpu_custom_call" | custom-call | flops 1966080 | bytes 589824 | tf_op jit(solution)/shard_map/hidden_grads/pallas_call | solution.py:347
  90.0 10.1 %all_to_all.36.grads = bf16[8,96,128]{2,1,0:T(8,128)(2,1)S(1)} all-to-all(bf16[8,96,128]{2,1,0:T(8,128)(2,1)} %hidden_grads.1), channel_id=1, replica_groups=mesh['y'=4,'z'=16,'x'=4,'core'=2] {'x','core'}, dimensions={0} | all-to-all | bytes 393216 | tf_op jit(solution)/shard_map/all_to_all | solution.py:37
  100.2 1.1 input_grad.1
  101.2 8.0 %all-to-all-start.5 = ((bf16[64,8,256]{2,1,0:T(8,128)(2,1)}), bf16[64,8,256]{2,1,0:T(8,128)(2,1)S(1)}, u32[]{:S(2)}, u32[]{:S(2)}) async-start(bf16[64,8,256]{2,1,0:T(8,128)(2,1)} %input_grad.1), calls=%async_computation.5 | async-start | bytes 524288 | tf_op jit(solution)/shard_map/all_to_all | solution.py:37
  109.3 0.0 copy-start.18
  109.3 0.6 copy-done.18
  109.9 0.1 copy.15.row_scale
  110.0 1.7 %weight_grads.1 = (bf16[2,96,1024]{2,1,0:T(8,128)(2,1)S(1)}, bf16[2,96,1024]{2,1,0:T(8,128)(2,1)S(1)}, bf16[2,96,1024]{2,1,0:T(8,128)(2,1)S(1)}, bf16[2,96,1024]{2,1,0:T(8,128)(2,1)S(1)}) custom-call(bf16[8,96,128]{2,1,0:T(8,128)(2,1)S(1)} %all_to_all.36.grads, bf16[4,72,1024]{2,1,0:T(8,128)(2,1)S(1)} %all_to_all.35.messages, f32[128,1]{1,0:T(8,128)S(1)} %copy.15.row_scale), custom_call_target="tpu_custom_call" | custom-call | flops 201326592 | bytes 1572864 | tf_op jit(solution)/shard_map/weight_grads/pallas_call | solution.py:403
  111.7 0.7 copy-done.9
  112.5 1.9 %collective-permute-start.4 = (bf16[2,96,1024]{2,1,0:T(8,128)(2,1)S(1)}, bf16[2,96,1024]{2,1,0:T(8,128)(2,1)S(1)}, u32[]{:S(2)}, u32[]{:S(2)}) collective-permute-start(bf16[2,96,1024]{2,1,0:T(8,128)(2,1)S(1)} %get-tuple-element.24), channel_id=1, source_target_pairs={{0,6},{2,0},{4,2},{6,4},{1,7},{3,1},{5,3},{7,5},{8,14},{10,8},{12,... | collective-permute-start | bytes 1179656 | tf_op jit(solution)/shard_map/ppermute | solution.py:45
  114.4 5.4 %collective-permute-start.5 = (bf16[2,96,1024]{2,1,0:T(8,128)(2,1)S(1)}, bf16[2,96,1024]{2,1,0:T(8,128)(2,1)S(1)}, u32[]{:S(2)}, u32[]{:S(2)}) collective-permute-start(bf16[2,96,1024]{2,1,0:T(8,128)(2,1)S(1)} %get-tuple-element.25), channel_id=1, source_target_pairs={{0,4},{2,6},{4,0},{6,2},{1,5},{3,7},{5,1},{7,3},{8,12},{10,14},{12... | collective-permute-start | bytes 1179656 | tf_op jit(solution)/shard_map/ppermute | solution.py:45
  119.8 3.1 %collective-permute-start.6 = (bf16[2,96,1024]{2,1,0:T(8,128)(2,1)S(1)}, bf16[2,96,1024]{2,1,0:T(8,128)(2,1)S(1)}, u32[]{:S(2)}, u32[]{:S(2)}) collective-permute-start(bf16[2,96,1024]{2,1,0:T(8,128)(2,1)S(1)} %get-tuple-element.26), channel_id=1, source_target_pairs={{0,2},{2,4},{4,6},{6,0},{1,3},{3,5},{5,7},{7,1},{8,10},{10,12},{12... | collective-permute-start | bytes 1179656 | tf_op jit(solution)/shard_map/ppermute | solution.py:45
  122.9 7.1 %all-to-all-done.5 = bf16[64,8,256]{2,1,0:T(8,128)(2,1)S(1)} async-done(((bf16[64,8,256]{2,1,0:T(8,128)(2,1)}), bf16[64,8,256]{2,1,0:T(8,128)(2,1)S(1)}, u32[]{:S(2)}, u32[]{:S(2)}) %all-to-all-start.5) | async-done | bytes 262176 | tf_op jit(solution)/shard_map/all_to_all | solution.py:37
  130.0 0.1 reduce_sum.41
  130.1 0.7 broadcast_in_dim.53
  130.8 8.0 %all-to-all-start.6 = ((bf16[64,8,256]{2,1,0:T(8,128)(2,1)}), bf16[64,8,256]{2,1,0:T(8,128)(2,1)S(1)}, u32[]{:S(2)}, u32[]{:S(2)}) async-start(bf16[64,8,256]{2,1,0:T(8,128)(2,1)} %broadcast_in_dim.53), calls=%async_computation.6 | async-start | bytes 524288 | tf_op jit(solution)/shard_map/all_to_all | solution.py:37
  138.9 0.7 copy-done.10
  139.6 0.2 copy-done.11
  139.8 0.1 copy-done.12
  139.9 2.2 %join_far.3 = bf16[4,96,1024]{2,1,0:T(8,128)(2,1)} custom-call(bf16[2,96,1024]{2,1,0:T(8,128)(2,1)} %copy-done.9, bf16[2,96,1024]{2,1,0:T(8,128)(2,1)} %copy-done.10, bf16[2,96,1024]{2,1,0:T(8,128)(2,1)} %copy-done.11, bf16[2,96,1024]{2,1,0:T(8,128)(2,1)} %copy-done.12), custom_call_target="tpu_custom_call" | custom-call | bytes 1572864 | tf_op jit(solution)/shard_map/join_far/pallas_call | solution.py:228
  142.1 1.9 %collective-permute-start.7 = (bf16[4,96,1024]{2,1,0:T(8,128)(2,1)}, bf16[4,96,1024]{2,1,0:T(8,128)(2,1)S(1)}, u32[]{:S(2)}, u32[]{:S(2)}) collective-permute-start(bf16[4,96,1024]{2,1,0:T(8,128)(2,1)} %join_far.3), channel_id=1, source_target_pairs={{0,1},{1,0},{2,3},{3,2},{4,5},{5,4},{6,7},{7,6},{8,9},{9,8},{10,11... | collective-permute-start | bytes 2359304 | tf_op jit(solution)/shard_map/ppermute | solution.py:49
  144.0 0.6 fusion.4
  144.7 0.6 iota_add_fusion
  145.3 0.0 copy-start.19
  145.3 0.6 copy-done.19
  146.0 0.1 select_reduce_fusion.1
  146.1 0.7 fusion.1.owner
  146.8 0.9 copy-done.16
  147.7 2.8 %unpack_grads.1 = (bf16[32,8192]{1,0:T(8,128)(2,1)}, bf16[32,8192]{1,0:T(8,128)(2,1)}, bf16[32,8192]{1,0:T(8,128)(2,1)}) custom-call(bf16[2,96,1024]{2,1,0:T(8,128)(2,1)} %copy-done.9, bf16[2,96,1024]{2,1,0:T(8,128)(2,1)} %copy-done.10, bf16[2,96,1024]{2,1,0:T(8,128)(2,1)} %copy-done.11, bf16[2,96,1024]{2,1,0:T(8,128)(2,1)} %copy-done.12, ...), custom_call_target="tpu_custom_call" | custom-call | bytes 3145728 | tf_op jit(solution)/shard_map/unpack_grads/pallas_call | solution.py:252
  150.5 7.7 %all-to-all-done.6.blocks = bf16[64,8,256]{2,1,0:T(8,128)(2,1)S(1)} async-done(((bf16[64,8,256]{2,1,0:T(8,128)(2,1)}), bf16[64,8,256]{2,1,0:T(8,128)(2,1)S(1)}, u32[]{:S(2)}, u32[]{:S(2)}) %all-to-all-start.6) | async-done | bytes 262176 | tf_op jit(solution)/shard_map/all_to_all | solution.py:37
  158.2 0.7 copy-done.15
  158.9 2.0 %finish.1 = (bf16[128,1024]{1,0:T(8,128)(2,1)}, f32[128,1024]{1,0:T(8,128)}) custom-call(bf16[64,8,256]{2,1,0:T(8,128)(2,1)} %copy-done.15, bf16[128,128]{1,0:T(8,128)(2,1)} %fusion.1.owner, bf16[128,1024]{1,0:T(8,128)(2,1)} %grad_out.3), custom_call_target="tpu_custom_call" | custom-call | flops 33554432 | bytes 1310720 | tf_op jit(solution)/shard_map/finish/pallas_call | solution.py:429
  (34 shorter events, 0.2 us)
Async XLA Ops:
  3.2 18.6 %all-to-all-start = ((bf16[4,16,1152]{2,1,0:T(8,128)(2,1)}), bf16[4,16,1152]{2,1,0:T(8,128)(2,1)S(1)}, u32[]{:S(2)}, u32[]{:S(2)}) async-start(bf16[4,16,1152]{2,1,0:T(8,128)(2,1)} %pick_rows.1._), calls=%async_computation | async-start | bytes 294912 | tf_op jit(solution)/shard_map/all_to_all | solution.py:37
  10.4 26.6 %collective-permute-start = (bf16[2,96,1024]{2,1,0:T(8,128)(2,1)}, bf16[2,96,1024]{2,1,0:T(8,128)(2,1)S(1)}, u32[]{:S(2)}, u32[]{:S(2)}) collective-permute-start(bf16[2,96,1024]{2,1,0:T(8,128)(2,1)} %get-tuple-element.19), channel_id=1, source_target_pairs={{0,2},{2,4},{4,6},{6,0},{1,3},{3,5},{5,7},{7,1},{8,10},{10,12},{12... | collective-permute-start | bytes 1179656 | tf_op jit(solution)/shard_map/ppermute | solution.py:45
  17.1 19.9 %collective-permute-start.1 = (bf16[2,96,1024]{2,1,0:T(8,128)(2,1)}, bf16[2,96,1024]{2,1,0:T(8,128)(2,1)S(1)}, u32[]{:S(2)}, u32[]{:S(2)}) collective-permute-start(bf16[2,96,1024]{2,1,0:T(8,128)(2,1)} %get-tuple-element.20), channel_id=1, source_target_pairs={{0,4},{2,6},{4,0},{6,2},{1,5},{3,7},{5,1},{7,3},{8,12},{10,14},{12... | collective-permute-start | bytes 1179656 | tf_op jit(solution)/shard_map/ppermute | solution.py:45
  19.0 18.0 %collective-permute-start.2 = (bf16[2,96,1024]{2,1,0:T(8,128)(2,1)}, bf16[2,96,1024]{2,1,0:T(8,128)(2,1)S(1)}, u32[]{:S(2)}, u32[]{:S(2)}) collective-permute-start(bf16[2,96,1024]{2,1,0:T(8,128)(2,1)} %get-tuple-element.21), channel_id=1, source_target_pairs={{0,6},{2,0},{4,2},{6,4},{1,7},{3,1},{5,3},{7,5},{8,14},{10,8},{12,... | collective-permute-start | bytes 1179656 | tf_op jit(solution)/shard_map/ppermute | solution.py:45
  21.8 0.7 copy-start.17
  24.5 31.6 %all-to-all-start.1 = ((bf16[16,8,1152]{2,1,0:T(8,128)(2,1)}), bf16[16,8,1152]{2,1,0:T(8,128)(2,1)S(1)}, u32[]{:S(2)}, u32[]{:S(2)}) async-start(bf16[16,8,1152]{2,1,0:T(8,128)(2,1)} %select_rows.1), calls=%async_computation.1 | async-start | bytes 589824 | tf_op jit(solution)/shard_map/all_to_all | solution.py:37
  37.0 0.7 copy-start.3
  37.0 0.9 copy-start.5
  37.0 1.0 copy-start.7
  40.2 4.4 %collective-permute-start.3 = (bf16[4,96,1024]{2,1,0:T(8,128)(2,1)}, bf16[4,96,1024]{2,1,0:T(8,128)(2,1)S(1)}, u32[]{:S(2)}, u32[]{:S(2)}) collective-permute-start(bf16[4,96,1024]{2,1,0:T(8,128)(2,1)} %join_far.2), channel_id=1, source_target_pairs={{0,1},{1,0},{2,3},{3,2},{4,5},{5,4},{6,7},{7,6},{8,9},{9,8},{10,11... | collective-permute-start | bytes 2359304 | tf_op jit(solution)/shard_map/ppermute | solution.py:49
  44.5 11.5 %copy-start = (bf16[4,96,1024]{2,1,0:T(8,128)(2,1)}, bf16[4,96,1024]{2,1,0:T(8,128)(2,1)S(1)}, u32[]{:S(2)}) copy-start(bf16[4,96,1024]{2,1,0:T(8,128)(2,1)S(1)} %collective-permute-done.3._.far) | copy-start | bytes 2359300
  56.0 0.7 copy-start.14
  56.8 15.5 %copy-start.4 = (bf16[2,96,1024]{2,1,0:T(8,128)(2,1)S(1)}, bf16[2,96,1024]{2,1,0:T(8,128)(2,1)}, u32[]{:S(2)}) copy-start(bf16[2,96,1024]{2,1,0:T(8,128)(2,1)} %copy-done.3) | copy-start | bytes 1179652
  56.8 15.5 %copy-start.6 = (bf16[2,96,1024]{2,1,0:T(8,128)(2,1)S(1)}, bf16[2,96,1024]{2,1,0:T(8,128)(2,1)}, u32[]{:S(2)}) copy-start(bf16[2,96,1024]{2,1,0:T(8,128)(2,1)} %copy-done.5) | copy-start | bytes 1179652
  56.8 15.5 %copy-start.8 = (bf16[2,96,1024]{2,1,0:T(8,128)(2,1)S(1)}, bf16[2,96,1024]{2,1,0:T(8,128)(2,1)}, u32[]{:S(2)}) copy-start(bf16[2,96,1024]{2,1,0:T(8,128)(2,1)} %copy-done.7) | copy-start | bytes 1179652
  59.1 13.1 %copy-start.1 = (bf16[4,96,1024]{2,1,0:T(8,128)(2,1)S(1)}, bf16[4,96,1024]{2,1,0:T(8,128)(2,1)}, u32[]{:S(2)}) copy-start(bf16[4,96,1024]{2,1,0:T(8,128)(2,1)} %copy-done) | copy-start | bytes 2359300
  59.1 13.1 %copy-start.2 = (bf16[2,96,1024]{2,1,0:T(8,128)(2,1)S(1)}, bf16[2,96,1024]{2,1,0:T(8,128)(2,1)}, u32[]{:S(2)}) copy-start(bf16[2,96,1024]{2,1,0:T(8,128)(2,1)} %get-tuple-element.18.refs_0_.w0) | copy-start | bytes 1179652
  74.4 13.2 %all-to-all-start.3 = ((f32[8,96,128]{2,1,0:T(8,128)}), f32[8,96,128]{2,1,0:T(8,128)S(1)}, u32[]{:S(2)}, u32[]{:S(2)}) async-start(f32[8,96,128]{2,1,0:T(8,128)} %forward.1), calls=%async_computation.3 | async-start | bytes 786432 | tf_op jit(solution)/shard_map/all_to_all | solution.py:37
  87.6 0.7 copy-start.13
  101.2 28.8 %all-to-all-start.5 = ((bf16[64,8,256]{2,1,0:T(8,128)(2,1)}), bf16[64,8,256]{2,1,0:T(8,128)(2,1)S(1)}, u32[]{:S(2)}, u32[]{:S(2)}) async-start(bf16[64,8,256]{2,1,0:T(8,128)(2,1)} %input_grad.1), calls=%async_computation.5 | async-start | bytes 524288 | tf_op jit(solution)/shard_map/all_to_all | solution.py:37
  109.3 0.7 copy-start.18
  111.7 0.8 copy-start.9
  112.5 26.4 %collective-permute-start.4 = (bf16[2,96,1024]{2,1,0:T(8,128)(2,1)S(1)}, bf16[2,96,1024]{2,1,0:T(8,128)(2,1)S(1)}, u32[]{:S(2)}, u32[]{:S(2)}) collective-permute-start(bf16[2,96,1024]{2,1,0:T(8,128)(2,1)S(1)} %get-tuple-element.24), channel_id=1, source_target_pairs={{0,6},{2,0},{4,2},{6,4},{1,7},{3,1},{5,3},{7,5},{8,14},{10,8},{12,... | collective-permute-start | bytes 1179656 | tf_op jit(solution)/shard_map/ppermute | solution.py:45
  114.4 24.5 %collective-permute-start.5 = (bf16[2,96,1024]{2,1,0:T(8,128)(2,1)S(1)}, bf16[2,96,1024]{2,1,0:T(8,128)(2,1)S(1)}, u32[]{:S(2)}, u32[]{:S(2)}) collective-permute-start(bf16[2,96,1024]{2,1,0:T(8,128)(2,1)S(1)} %get-tuple-element.25), channel_id=1, source_target_pairs={{0,4},{2,6},{4,0},{6,2},{1,5},{3,7},{5,1},{7,3},{8,12},{10,14},{12... | collective-permute-start | bytes 1179656 | tf_op jit(solution)/shard_map/ppermute | solution.py:45
  119.8 19.1 %collective-permute-start.6 = (bf16[2,96,1024]{2,1,0:T(8,128)(2,1)S(1)}, bf16[2,96,1024]{2,1,0:T(8,128)(2,1)S(1)}, u32[]{:S(2)}, u32[]{:S(2)}) collective-permute-start(bf16[2,96,1024]{2,1,0:T(8,128)(2,1)S(1)} %get-tuple-element.26), channel_id=1, source_target_pairs={{0,2},{2,4},{4,6},{6,0},{1,3},{3,5},{5,7},{7,1},{8,10},{10,12},{12... | collective-permute-start | bytes 1179656 | tf_op jit(solution)/shard_map/ppermute | solution.py:45
  130.8 27.4 %all-to-all-start.6 = ((bf16[64,8,256]{2,1,0:T(8,128)(2,1)}), bf16[64,8,256]{2,1,0:T(8,128)(2,1)S(1)}, u32[]{:S(2)}, u32[]{:S(2)}) async-start(bf16[64,8,256]{2,1,0:T(8,128)(2,1)} %broadcast_in_dim.53), calls=%async_computation.6 | async-start | bytes 524288 | tf_op jit(solution)/shard_map/all_to_all | solution.py:37
  138.9 0.8 copy-start.10
  138.9 0.9 copy-start.11
  138.9 1.0 copy-start.12
  142.1 4.7 %collective-permute-start.7 = (bf16[4,96,1024]{2,1,0:T(8,128)(2,1)}, bf16[4,96,1024]{2,1,0:T(8,128)(2,1)S(1)}, u32[]{:S(2)}, u32[]{:S(2)}) collective-permute-start(bf16[4,96,1024]{2,1,0:T(8,128)(2,1)} %join_far.3), channel_id=1, source_target_pairs={{0,1},{1,0},{2,3},{3,2},{4,5},{5,4},{6,7},{7,6},{8,9},{9,8},{10,11... | collective-permute-start | bytes 2359304 | tf_op jit(solution)/shard_map/ppermute | solution.py:49
  145.3 0.7 copy-start.19
  146.8 0.9 copy-start.16
  158.2 0.7 copy-start.15

commit v5 on v4

--- a/solution.py
+++ b/solution.py
@@ -309,8 +309,8 @@
     down = dot_t(down, ordered[KEPT:])
     for i, (s, d, _) in enumerate(blocks):
         t = peer(-s, d)
-        pre[t, : 2 * units] = both[2 * units * i : 2 * units * (i + 1)]
-        pre[t, 2 * units :] = down[units * i : units * (i + 1)]
+        pre[t, : 2 * units] = both[2 * units * i : 2 * units * (i + 1)].astype(BF)
+        pre[t, 2 * units :] = down[units * i : units * (i + 1)].astype(BF)
 
 
 def forward(messages, near, far):
@@ -320,7 +320,7 @@
         grid=(1,),
         in_specs=[VMEM] + [near_spec(units3, width)] * NX + [VMEM],
         out_specs=VMEM,
-        out_shape=jax.ShapeDtypeStruct((NT, units3, KEPT), F32),
+        out_shape=jax.ShapeDtypeStruct((NT, units3, KEPT), BF),
         cost_estimate=cost(2 * NT * units3 * width * KEPT, 2 * NT * units3 * width),
         compiler_params=ROOM,
         name="forward",
@@ -330,7 +330,7 @@
 def hidden_kernel(pre, row_scale, out):
     _, units3, _ = pre.shape
     units = units3 // 3
-    total = jnp.sum(pre[...], axis=0)
+    total = jnp.sum(pre[...].astype(F32), axis=0)
     gate_pre, up_pre, back_proj = total[:units], total[units : 2 * units], total[2 * units :]
     sigmoid_gate = jax.nn.sigmoid(gate_pre)
     activated = gate_pre * sigmoid_gate

time: 163 us -> 161 us (0.988)
  waiting for transfers between devices: 34.6 us -> 32.6 us
    all_to_all x5, waiting for transfers between devices: 32.1 us -> 30.1 us  [exchange(): return lax.all_to_all(pieces, axes, 0, 0, tiled=True)]
  transfers between devices with their start and end apart: 13 -> 13, of which waited for: 5 -> 5; matrix products, arithmetic and copies ran while one was open for 3% -> 2% of each run, Pallas kernels for 8% -> 9%
where the time goes in v5:
time: 161 us; the launch traced here: 159 us
  starting transfers between devices  64.9 us (40%)
  waiting for transfers between devices  32.6 us (20%)
  Pallas kernels  24.6 us (15%)
  blocking collectives  23.1 us (14%)
  local copies, waits for them, and re-layouts  8.81 us (5%)
  other arithmetic  3.07 us (2%)
    all_to_all x5, starting transfers between devices, exchange(): return lax.all_to_all(pieces, axes, 0, 0, tiled=True)  39.3 us
    all_to_all x5, waiting for transfers between devices, exchange(): return lax.all_to_all(pieces, axes, 0, 0, tiled=True)  30.1 us
    all_to_all x2, blocking collectives, exchange(): return lax.all_to_all(pieces, axes, 0, 0, tiled=True)  23.1 us
    ppermute x6, starting transfers between devices, along_x(): return lax.ppermute(array, 'x', [(i, (i + s) % NX) for i in range(NX)])  21.8 us
    unnamed x40, local copies, waits for them, and re-layouts  7.68 us
    pallas_call x2, Pallas kernels, join_far(): pl.pallas_call(join_kernel, grid=(1,), in_specs=[pl.BlockSpec((1, units3,...  4.34 us
    ppermute x2, starting transfers between devices, other_core(): return lax.ppermute(array, 'core', [(0, 1), (1, 0)])  3.82 us
  transfers between devices with their start and end apart: 13, of which 5 were waited for; matrix products, arithmetic and copies ran while one was open for 2% of the time, Pallas kernels for 9%

profile of v5, /device:TPU:6, one launch (start us, length us, event | category | flops | bytes accessed | tf_op | source)
XLA Modules:
  0.0 158.6 jit_solution(7434813803890303733)
XLA Ops:
  1.3 1.9 %pick_rows.1._ = bf16[4,16,1152]{2,1,0:T(8,128)(2,1)} custom-call(s32[1]{0:T(128)} %copy.16.count, s32[1,6]{1,0:T(1,128)} %pos.1, bf16[1,6]{1,0:T(2,128)(2,1)} %router.1, bf16[128,1024]{1,0:T(8,128)(2,1)} %tokens.1, bf16[128,1024]{1,0:T(8,128)(2,1)} %grad_out.3), custom_call_target="tpu_custom_call" | custom-call | flops 4194304 | bytes 524288 | tf_op jit(solution)/shard_map/pick_rows/pallas_call | solution.py:77
  3.2 4.5 %all-to-all-start = ((bf16[4,16,1152]{2,1,0:T(8,128)(2,1)}), bf16[4,16,1152]{2,1,0:T(8,128)(2,1)S(1)}, u32[]{:S(2)}, u32[]{:S(2)}) async-start(bf16[4,16,1152]{2,1,0:T(8,128)(2,1)} %pick_rows.1._), calls=%async_computation | async-start | bytes 294912 | tf_op jit(solution)/shard_map/all_to_all | solution.py:37
  7.7 2.8 %pack_weights.1 = (bf16[2,96,1024]{2,1,0:T(8,128)(2,1)}, bf16[2,96,1024]{2,1,0:T(8,128)(2,1)}, bf16[2,96,1024]{2,1,0:T(8,128)(2,1)}, bf16[2,96,1024]{2,1,0:T(8,128)(2,1)}) custom-call(bf16[32,8192]{1,0:T(8,128)(2,1)} %gate_w.1, bf16[32,8192]{1,0:T(8,128)(2,1)} %up_w.1, bf16[32,8192]{1,0:T(8,128)(2,1)} %down_w.1, bf16[4,16,1152]{2,1,0:T(8,128)(2,1)} %pick_rows.1._), custom_call_target="tpu_custom_call" | custom-call | bytes 3145728 | tf_op jit(solution)/shard_map/pack_weights/pallas_call | solution.py:208
  10.4 6.7 %collective-permute-start = (bf16[2,96,1024]{2,1,0:T(8,128)(2,1)}, bf16[2,96,1024]{2,1,0:T(8,128)(2,1)S(1)}, u32[]{:S(2)}, u32[]{:S(2)}) collective-permute-start(bf16[2,96,1024]{2,1,0:T(8,128)(2,1)} %get-tuple-element.19), channel_id=1, source_target_pairs={{0,2},{2,4},{4,6},{6,0},{1,3},{3,5},{5,7},{7,1},{8,10},{10,12},{12... | collective-permute-start | bytes 1179656 | tf_op jit(solution)/shard_map/ppermute | solution.py:45
  17.1 1.9 %collective-permute-start.1 = (bf16[2,96,1024]{2,1,0:T(8,128)(2,1)}, bf16[2,96,1024]{2,1,0:T(8,128)(2,1)S(1)}, u32[]{:S(2)}, u32[]{:S(2)}) collective-permute-start(bf16[2,96,1024]{2,1,0:T(8,128)(2,1)} %get-tuple-element.20), channel_id=1, source_target_pairs={{0,4},{2,6},{4,0},{6,2},{1,5},{3,7},{5,1},{7,3},{8,12},{10,14},{12... | collective-permute-start | bytes 1179656 | tf_op jit(solution)/shard_map/ppermute | solution.py:45
  19.0 2.8 %collective-permute-start.2 = (bf16[2,96,1024]{2,1,0:T(8,128)(2,1)}, bf16[2,96,1024]{2,1,0:T(8,128)(2,1)S(1)}, u32[]{:S(2)}, u32[]{:S(2)}) collective-permute-start(bf16[2,96,1024]{2,1,0:T(8,128)(2,1)} %get-tuple-element.21), channel_id=1, source_target_pairs={{0,6},{2,0},{4,2},{6,4},{1,7},{3,1},{5,3},{7,5},{8,14},{10,8},{12,... | collective-permute-start | bytes 1179656 | tf_op jit(solution)/shard_map/ppermute | solution.py:45
  21.8 0.0 copy-start.17
  21.8 0.7 copy-done.17
  22.5 2.0 %select_rows.1 = bf16[16,8,1152]{2,1,0:T(8,128)(2,1)} custom-call(bf16[4,16,1152]{2,1,0:T(8,128)(2,1)} %copy-done.17), custom_call_target="tpu_custom_call" | custom-call | flops 1179648 | bytes 589824 | tf_op jit(solution)/shard_map/select_rows/pallas_call | solution.py:127
  24.5 12.5 %all-to-all-start.1 = ((bf16[16,8,1152]{2,1,0:T(8,128)(2,1)}), bf16[16,8,1152]{2,1,0:T(8,128)(2,1)S(1)}, u32[]{:S(2)}, u32[]{:S(2)}) async-start(bf16[16,8,1152]{2,1,0:T(8,128)(2,1)} %select_rows.1), calls=%async_computation.1 | async-start | bytes 589824 | tf_op jit(solution)/shard_map/all_to_all | solution.py:37
  37.0 0.0 copy-start.3
  37.0 0.0 copy-start.5
  37.0 0.0 copy-start.7
  37.0 0.7 copy-done.3
  37.7 0.1 copy-done.5
  37.9 0.1 copy-done.7
  38.0 2.2 %join_far.2 = bf16[4,96,1024]{2,1,0:T(8,128)(2,1)} custom-call(bf16[2,96,1024]{2,1,0:T(8,128)(2,1)} %get-tuple-element.18.refs_0_.w0, bf16[2,96,1024]{2,1,0:T(8,128)(2,1)} %copy-done.3, bf16[2,96,1024]{2,1,0:T(8,128)(2,1)} %copy-done.5, bf16[2,96,1024]{2,1,0:T(8,128)(2,1)} %copy-done.7), custom_call_target="tpu_custom_call" | custom-call | bytes 1572864 | tf_op jit(solution)/shard_map/join_far/pallas_call | solution.py:228
  40.2 1.9 %collective-permute-start.3 = (bf16[4,96,1024]{2,1,0:T(8,128)(2,1)}, bf16[4,96,1024]{2,1,0:T(8,128)(2,1)S(1)}, u32[]{:S(2)}, u32[]{:S(2)}) collective-permute-start(bf16[4,96,1024]{2,1,0:T(8,128)(2,1)} %join_far.2), channel_id=1, source_target_pairs={{0,1},{1,0},{2,3},{3,2},{4,5},{5,4},{6,7},{7,6},{8,9},{9,8},{10,11... | collective-permute-start | bytes 2359304 | tf_op jit(solution)/shard_map/ppermute | solution.py:49
  42.1 2.5 %collective-permute-done.3._.far = bf16[4,96,1024]{2,1,0:T(8,128)(2,1)S(1)} collective-permute-done((bf16[4,96,1024]{2,1,0:T(8,128)(2,1)}, bf16[4,96,1024]{2,1,0:T(8,128)(2,1)S(1)}, u32[]{:S(2)}, u32[]{:S(2)}) %collective-permute-start.3) | collective-permute-done | bytes 786464 | tf_op jit(solution)/shard_map/ppermute | solution.py:49
  44.5 11.5 %all-to-all-done.1.plane = bf16[16,8,1152]{2,1,0:T(8,128)(2,1)S(1)} async-done(((bf16[16,8,1152]{2,1,0:T(8,128)(2,1)}), bf16[16,8,1152]{2,1,0:T(8,128)(2,1)S(1)}, u32[]{:S(2)}, u32[]{:S(2)}) %all-to-all-start.1) | async-done | bytes 294944 | tf_op jit(solution)/shard_map/all_to_all | solution.py:37
  56.1 0.7 copy-done.13
  56.8 2.3 %compact_rows.1 = bf16[4,72,1024]{2,1,0:T(8,128)(2,1)} custom-call(bf16[16,8,1152]{2,1,0:T(8,128)(2,1)} %copy-done.13, bf16[4,96,1024]{2,1,0:T(8,128)(2,1)} %copy-done), custom_call_target="tpu_custom_call" | custom-call | flops 37748736 | bytes 1179648 | tf_op jit(solution)/shard_map/compact_rows/pallas_call | solution.py:160
  59.1 12.9 %all_to_all.35.messages = bf16[4,72,1024]{2,1,0:T(8,128)(2,1)S(1)} all-to-all(bf16[4,72,1024]{2,1,0:T(8,128)(2,1)} %compact_rows.1), channel_id=1, replica_groups=mesh['y'=4,'z'=16,'x'=4,'core'=2] {'y'}, dimensions={0} | all-to-all | bytes 1179648 | tf_op jit(solution)/shard_map/all_to_all | solution.py:37
  72.2 0.1 gt.16
  72.2 0.1 add.29
  72.4 2.1 %forward.1 = bf16[8,96,128]{2,1,0:T(8,128)(2,1)} custom-call(bf16[4,72,1024]{2,1,0:T(8,128)(2,1)S(1)} %all_to_all.35.messages, bf16[2,96,1024]{2,1,0:T(8,128)(2,1)S(1)} %copy-done.2, bf16[2,96,1024]{2,1,0:T(8,128)(2,1)S(1)} %copy-done.4, bf16[2,96,1024]{2,1,0:T(8,128)(2,1)S(1)} %copy-done.6, bf16[2,96,1024]{2,1,0:T(8,128)(2,1)S(1)} %copy-done.8, ...), custom_call_target="tpu_custom_call" | custom-call | flops 201326592 | bytes 1572864 | tf_op jit(solution)/shard_map/forward/pallas_call | solution.py:318
  74.4 6.2 %all-to-all-start.3 = ((bf16[8,96,128]{2,1,0:T(8,128)(2,1)}), bf16[8,96,128]{2,1,0:T(8,128)(2,1)S(1)}, u32[]{:S(2)}, u32[]{:S(2)}) async-start(bf16[8,96,128]{2,1,0:T(8,128)(2,1)} %forward.1), calls=%async_computation.3 | async-start | bytes 393216 | tf_op jit(solution)/shard_map/all_to_all | solution.py:37
  80.7 0.2 convert_reduce_fusion
  80.9 0.1 broadcast_in_dim.32
  81.0 0.7 select_reduce_fusion
  81.6 3.8 %all-to-all-done.3.pre = bf16[8,96,128]{2,1,0:T(8,128)(2,1)S(1)} async-done(((bf16[8,96,128]{2,1,0:T(8,128)(2,1)}), bf16[8,96,128]{2,1,0:T(8,128)(2,1)S(1)}, u32[]{:S(2)}, u32[]{:S(2)}) %all-to-all-start.3) | async-done | bytes 196640 | tf_op jit(solution)/shard_map/all_to_all | solution.py:37
  85.4 0.7 copy-done.15
  86.1 1.6 %hidden_grads.1 = bf16[8,96,128]{2,1,0:T(8,128)(2,1)} custom-call(bf16[8,96,128]{2,1,0:T(8,128)(2,1)} %copy-done.15, f32[1,128]{1,0:T(1,128)} %bitcast.7), custom_call_target="tpu_custom_call" | custom-call | flops 1966080 | bytes 589824 | tf_op jit(solution)/shard_map/hidden_grads/pallas_call | solution.py:347
  87.8 10.1 %all_to_all.36.grads = bf16[8,96,128]{2,1,0:T(8,128)(2,1)S(1)} all-to-all(bf16[8,96,128]{2,1,0:T(8,128)(2,1)} %hidden_grads.1), channel_id=1, replica_groups=mesh['y'=4,'z'=16,'x'=4,'core'=2] {'x','core'}, dimensions={0} | all-to-all | bytes 393216 | tf_op jit(solution)/shard_map/all_to_all | solution.py:37
  97.9 1.1 input_grad.1
  99.0 8.0 %all-to-all-start.5 = ((bf16[64,8,256]{2,1,0:T(8,128)(2,1)}), bf16[64,8,256]{2,1,0:T(8,128)(2,1)S(1)}, u32[]{:S(2)}, u32[]{:S(2)}) async-start(bf16[64,8,256]{2,1,0:T(8,128)(2,1)} %input_grad.1), calls=%async_computation.5 | async-start | bytes 524288 | tf_op jit(solution)/shard_map/all_to_all | solution.py:37
  107.0 0.0 copy-start.18
  107.0 0.6 copy-done.18
  107.7 0.1 copy.15.row_scale
  107.8 1.7 %weight_grads.1 = (bf16[2,96,1024]{2,1,0:T(8,128)(2,1)S(1)}, bf16[2,96,1024]{2,1,0:T(8,128)(2,1)S(1)}, bf16[2,96,1024]{2,1,0:T(8,128)(2,1)S(1)}, bf16[2,96,1024]{2,1,0:T(8,128)(2,1)S(1)}) custom-call(bf16[8,96,128]{2,1,0:T(8,128)(2,1)S(1)} %all_to_all.36.grads, bf16[4,72,1024]{2,1,0:T(8,128)(2,1)S(1)} %all_to_all.35.messages, f32[128,1]{1,0:T(8,128)S(1)} %copy.15.row_scale), custom_call_target="tpu_custom_call" | custom-call | flops 201326592 | bytes 1572864 | tf_op jit(solution)/shard_map/weight_grads/pallas_call | solution.py:403
  109.4 0.7 copy-done.9
  110.2 1.9 %collective-permute-start.4 = (bf16[2,96,1024]{2,1,0:T(8,128)(2,1)S(1)}, bf16[2,96,1024]{2,1,0:T(8,128)(2,1)S(1)}, u32[]{:S(2)}, u32[]{:S(2)}) collective-permute-start(bf16[2,96,1024]{2,1,0:T(8,128)(2,1)S(1)} %get-tuple-element.24), channel_id=1, source_target_pairs={{0,6},{2,0},{4,2},{6,4},{1,7},{3,1},{5,3},{7,5},{8,14},{10,8},{12,... | collective-permute-start | bytes 1179656 | tf_op jit(solution)/shard_map/ppermute | solution.py:45
  112.1 5.4 %collective-permute-start.5 = (bf16[2,96,1024]{2,1,0:T(8,128)(2,1)S(1)}, bf16[2,96,1024]{2,1,0:T(8,128)(2,1)S(1)}, u32[]{:S(2)}, u32[]{:S(2)}) collective-permute-start(bf16[2,96,1024]{2,1,0:T(8,128)(2,1)S(1)} %get-tuple-element.25), channel_id=1, source_target_pairs={{0,4},{2,6},{4,0},{6,2},{1,5},{3,7},{5,1},{7,3},{8,12},{10,14},{12... | collective-permute-start | bytes 1179656 | tf_op jit(solution)/shard_map/ppermute | solution.py:45
  117.5 3.1 %collective-permute-start.6 = (bf16[2,96,1024]{2,1,0:T(8,128)(2,1)S(1)}, bf16[2,96,1024]{2,1,0:T(8,128)(2,1)S(1)}, u32[]{:S(2)}, u32[]{:S(2)}) collective-permute-start(bf16[2,96,1024]{2,1,0:T(8,128)(2,1)S(1)} %get-tuple-element.26), channel_id=1, source_target_pairs={{0,2},{2,4},{4,6},{6,0},{1,3},{3,5},{5,7},{7,1},{8,10},{10,12},{12... | collective-permute-start | bytes 1179656 | tf_op jit(solution)/shard_map/ppermute | solution.py:45
  120.6 7.1 %all-to-all-done.5 = bf16[64,8,256]{2,1,0:T(8,128)(2,1)S(1)} async-done(((bf16[64,8,256]{2,1,0:T(8,128)(2,1)}), bf16[64,8,256]{2,1,0:T(8,128)(2,1)S(1)}, u32[]{:S(2)}, u32[]{:S(2)}) %all-to-all-start.5) | async-done | bytes 262176 | tf_op jit(solution)/shard_map/all_to_all | solution.py:37
  127.7 0.1 reduce_sum.41
  127.8 0.7 broadcast_in_dim.53
  128.5 8.0 %all-to-all-start.6 = ((bf16[64,8,256]{2,1,0:T(8,128)(2,1)}), bf16[64,8,256]{2,1,0:T(8,128)(2,1)S(1)}, u32[]{:S(2)}, u32[]{:S(2)}) async-start(bf16[64,8,256]{2,1,0:T(8,128)(2,1)} %broadcast_in_dim.53), calls=%async_computation.6 | async-start | bytes 524288 | tf_op jit(solution)/shard_map/all_to_all | solution.py:37
  136.6 0.7 copy-done.10
  137.4 0.2 copy-done.11
  137.5 0.1 copy-done.12
  137.7 2.2 %join_far.3 = bf16[4,96,1024]{2,1,0:T(8,128)(2,1)} custom-call(bf16[2,96,1024]{2,1,0:T(8,128)(2,1)} %copy-done.9, bf16[2,96,1024]{2,1,0:T(8,128)(2,1)} %copy-done.10, bf16[2,96,1024]{2,1,0:T(8,128)(2,1)} %copy-done.11, bf16[2,96,1024]{2,1,0:T(8,128)(2,1)} %copy-done.12), custom_call_target="tpu_custom_call" | custom-call | bytes 1572864 | tf_op jit(solution)/shard_map/join_far/pallas_call | solution.py:228
  139.8 1.9 %collective-permute-start.7 = (bf16[4,96,1024]{2,1,0:T(8,128)(2,1)}, bf16[4,96,1024]{2,1,0:T(8,128)(2,1)S(1)}, u32[]{:S(2)}, u32[]{:S(2)}) collective-permute-start(bf16[4,96,1024]{2,1,0:T(8,128)(2,1)} %join_far.3), channel_id=1, source_target_pairs={{0,1},{1,0},{2,3},{3,2},{4,5},{5,4},{6,7},{7,6},{8,9},{9,8},{10,11... | collective-permute-start | bytes 2359304 | tf_op jit(solution)/shard_map/ppermute | solution.py:49
  141.8 0.6 fusion.4
  142.4 0.6 iota_add_fusion
  143.1 0.0 copy-start.19
  143.1 0.6 copy-done.19
  143.7 0.1 select_reduce_fusion.1
  143.8 0.7 fusion.1.owner
  144.5 0.9 copy-done.16
  145.4 2.8 %unpack_grads.1 = (bf16[32,8192]{1,0:T(8,128)(2,1)}, bf16[32,8192]{1,0:T(8,128)(2,1)}, bf16[32,8192]{1,0:T(8,128)(2,1)}) custom-call(bf16[2,96,1024]{2,1,0:T(8,128)(2,1)} %copy-done.9, bf16[2,96,1024]{2,1,0:T(8,128)(2,1)} %copy-done.10, bf16[2,96,1024]{2,1,0:T(8,128)(2,1)} %copy-done.11, bf16[2,96,1024]{2,1,0:T(8,128)(2,1)} %copy-done.12, ...), custom_call_target="tpu_custom_call" | custom-call | bytes 3145728 | tf_op jit(solution)/shard_map/unpack_grads/pallas_call | solution.py:252
  148.2 7.7 %all-to-all-done.6.blocks = bf16[64,8,256]{2,1,0:T(8,128)(2,1)S(1)} async-done(((bf16[64,8,256]{2,1,0:T(8,128)(2,1)}), bf16[64,8,256]{2,1,0:T(8,128)(2,1)S(1)}, u32[]{:S(2)}, u32[]{:S(2)}) %all-to-all-start.6) | async-done | bytes 262176 | tf_op jit(solution)/shard_map/all_to_all | solution.py:37
  155.9 0.7 copy-done.14
  156.6 2.0 %finish.1 = (bf16[128,1024]{1,0:T(8,128)(2,1)}, f32[128,1024]{1,0:T(8,128)}) custom-call(bf16[64,8,256]{2,1,0:T(8,128)(2,1)} %copy-done.14, bf16[128,128]{1,0:T(8,128)(2,1)} %fusion.1.owner, bf16[128,1024]{1,0:T(8,128)(2,1)} %grad_out.3), custom_call_target="tpu_custom_call" | custom-call | flops 33554432 | bytes 1310720 | tf_op jit(solution)/shard_map/finish/pallas_call | solution.py:429
  (34 shorter events, 0.2 us)
Async XLA Ops:
  3.2 18.6 %all-to-all-start = ((bf16[4,16,1152]{2,1,0:T(8,128)(2,1)}), bf16[4,16,1152]{2,1,0:T(8,128)(2,1)S(1)}, u32[]{:S(2)}, u32[]{:S(2)}) async-start(bf16[4,16,1152]{2,1,0:T(8,128)(2,1)} %pick_rows.1._), calls=%async_computation | async-start | bytes 294912 | tf_op jit(solution)/shard_map/all_to_all | solution.py:37
  10.4 26.6 %collective-permute-start = (bf16[2,96,1024]{2,1,0:T(8,128)(2,1)}, bf16[2,96,1024]{2,1,0:T(8,128)(2,1)S(1)}, u32[]{:S(2)}, u32[]{:S(2)}) collective-permute-start(bf16[2,96,1024]{2,1,0:T(8,128)(2,1)} %get-tuple-element.19), channel_id=1, source_target_pairs={{0,2},{2,4},{4,6},{6,0},{1,3},{3,5},{5,7},{7,1},{8,10},{10,12},{12... | collective-permute-start | bytes 1179656 | tf_op jit(solution)/shard_map/ppermute | solution.py:45
  17.1 19.9 %collective-permute-start.1 = (bf16[2,96,1024]{2,1,0:T(8,128)(2,1)}, bf16[2,96,1024]{2,1,0:T(8,128)(2,1)S(1)}, u32[]{:S(2)}, u32[]{:S(2)}) collective-permute-start(bf16[2,96,1024]{2,1,0:T(8,128)(2,1)} %get-tuple-element.20), channel_id=1, source_target_pairs={{0,4},{2,6},{4,0},{6,2},{1,5},{3,7},{5,1},{7,3},{8,12},{10,14},{12... | collective-permute-start | bytes 1179656 | tf_op jit(solution)/shard_map/ppermute | solution.py:45
  19.0 18.0 %collective-permute-start.2 = (bf16[2,96,1024]{2,1,0:T(8,128)(2,1)}, bf16[2,96,1024]{2,1,0:T(8,128)(2,1)S(1)}, u32[]{:S(2)}, u32[]{:S(2)}) collective-permute-start(bf16[2,96,1024]{2,1,0:T(8,128)(2,1)} %get-tuple-element.21), channel_id=1, source_target_pairs={{0,6},{2,0},{4,2},{6,4},{1,7},{3,1},{5,3},{7,5},{8,14},{10,8},{12,... | collective-permute-start | bytes 1179656 | tf_op jit(solution)/shard_map/ppermute | solution.py:45
  21.8 0.7 copy-start.17
  24.5 31.6 %all-to-all-start.1 = ((bf16[16,8,1152]{2,1,0:T(8,128)(2,1)}), bf16[16,8,1152]{2,1,0:T(8,128)(2,1)S(1)}, u32[]{:S(2)}, u32[]{:S(2)}) async-start(bf16[16,8,1152]{2,1,0:T(8,128)(2,1)} %select_rows.1), calls=%async_computation.1 | async-start | bytes 589824 | tf_op jit(solution)/shard_map/all_to_all | solution.py:37
  37.0 0.7 copy-start.3
  37.0 0.9 copy-start.5
  37.0 1.0 copy-start.7
  40.2 4.4 %collective-permute-start.3 = (bf16[4,96,1024]{2,1,0:T(8,128)(2,1)}, bf16[4,96,1024]{2,1,0:T(8,128)(2,1)S(1)}, u32[]{:S(2)}, u32[]{:S(2)}) collective-permute-start(bf16[4,96,1024]{2,1,0:T(8,128)(2,1)} %join_far.2), channel_id=1, source_target_pairs={{0,1},{1,0},{2,3},{3,2},{4,5},{5,4},{6,7},{7,6},{8,9},{9,8},{10,11... | collective-permute-start | bytes 2359304 | tf_op jit(solution)/shard_map/ppermute | solution.py:49
  44.5 11.5 %copy-start = (bf16[4,96,1024]{2,1,0:T(8,128)(2,1)}, bf16[4,96,1024]{2,1,0:T(8,128)(2,1)S(1)}, u32[]{:S(2)}) copy-start(bf16[4,96,1024]{2,1,0:T(8,128)(2,1)S(1)} %collective-permute-done.3._.far) | copy-start | bytes 2359300
  56.0 0.7 copy-start.13
  56.8 15.6 %copy-start.4 = (bf16[2,96,1024]{2,1,0:T(8,128)(2,1)S(1)}, bf16[2,96,1024]{2,1,0:T(8,128)(2,1)}, u32[]{:S(2)}) copy-start(bf16[2,96,1024]{2,1,0:T(8,128)(2,1)} %copy-done.3) | copy-start | bytes 1179652
  56.8 15.6 %copy-start.6 = (bf16[2,96,1024]{2,1,0:T(8,128)(2,1)S(1)}, bf16[2,96,1024]{2,1,0:T(8,128)(2,1)}, u32[]{:S(2)}) copy-start(bf16[2,96,1024]{2,1,0:T(8,128)(2,1)} %copy-done.5) | copy-start | bytes 1179652
  56.8 15.6 %copy-start.8 = (bf16[2,96,1024]{2,1,0:T(8,128)(2,1)S(1)}, bf16[2,96,1024]{2,1,0:T(8,128)(2,1)}, u32[]{:S(2)}) copy-start(bf16[2,96,1024]{2,1,0:T(8,128)(2,1)} %copy-done.7) | copy-start | bytes 1179652
  59.1 13.2 %copy-start.1 = (bf16[4,96,1024]{2,1,0:T(8,128)(2,1)S(1)}, bf16[4,96,1024]{2,1,0:T(8,128)(2,1)}, u32[]{:S(2)}) copy-start(bf16[4,96,1024]{2,1,0:T(8,128)(2,1)} %copy-done) | copy-start | bytes 2359300
  59.1 13.2 %copy-start.2 = (bf16[2,96,1024]{2,1,0:T(8,128)(2,1)S(1)}, bf16[2,96,1024]{2,1,0:T(8,128)(2,1)}, u32[]{:S(2)}) copy-start(bf16[2,96,1024]{2,1,0:T(8,128)(2,1)} %get-tuple-element.18.refs_0_.w0) | copy-start | bytes 1179652
  74.4 11.0 %all-to-all-start.3 = ((bf16[8,96,128]{2,1,0:T(8,128)(2,1)}), bf16[8,96,128]{2,1,0:T(8,128)(2,1)S(1)}, u32[]{:S(2)}, u32[]{:S(2)}) async-start(bf16[8,96,128]{2,1,0:T(8,128)(2,1)} %forward.1), calls=%async_computation.3 | async-start | bytes 393216 | tf_op jit(solution)/shard_map/all_to_all | solution.py:37
  85.4 0.7 copy-start.15
  99.0 28.8 %all-to-all-start.5 = ((bf16[64,8,256]{2,1,0:T(8,128)(2,1)}), bf16[64,8,256]{2,1,0:T(8,128)(2,1)S(1)}, u32[]{:S(2)}, u32[]{:S(2)}) async-start(bf16[64,8,256]{2,1,0:T(8,128)(2,1)} %input_grad.1), calls=%async_computation.5 | async-start | bytes 524288 | tf_op jit(solution)/shard_map/all_to_all | solution.py:37
  107.0 0.7 copy-start.18
  109.4 0.8 copy-start.9
  110.2 26.4 %collective-permute-start.4 = (bf16[2,96,1024]{2,1,0:T(8,128)(2,1)S(1)}, bf16[2,96,1024]{2,1,0:T(8,128)(2,1)S(1)}, u32[]{:S(2)}, u32[]{:S(2)}) collective-permute-start(bf16[2,96,1024]{2,1,0:T(8,128)(2,1)S(1)} %get-tuple-element.24), channel_id=1, source_target_pairs={{0,6},{2,0},{4,2},{6,4},{1,7},{3,1},{5,3},{7,5},{8,14},{10,8},{12,... | collective-permute-start | bytes 1179656 | tf_op jit(solution)/shard_map/ppermute | solution.py:45
  112.1 24.5 %collective-permute-start.5 = (bf16[2,96,1024]{2,1,0:T(8,128)(2,1)S(1)}, bf16[2,96,1024]{2,1,0:T(8,128)(2,1)S(1)}, u32[]{:S(2)}, u32[]{:S(2)}) collective-permute-start(bf16[2,96,1024]{2,1,0:T(8,128)(2,1)S(1)} %get-tuple-element.25), channel_id=1, source_target_pairs={{0,4},{2,6},{4,0},{6,2},{1,5},{3,7},{5,1},{7,3},{8,12},{10,14},{12... | collective-permute-start | bytes 1179656 | tf_op jit(solution)/shard_map/ppermute | solution.py:45
  117.5 19.1 %collective-permute-start.6 = (bf16[2,96,1024]{2,1,0:T(8,128)(2,1)S(1)}, bf16[2,96,1024]{2,1,0:T(8,128)(2,1)S(1)}, u32[]{:S(2)}, u32[]{:S(2)}) collective-permute-start(bf16[2,96,1024]{2,1,0:T(8,128)(2,1)S(1)} %get-tuple-element.26), channel_id=1, source_target_pairs={{0,2},{2,4},{4,6},{6,0},{1,3},{3,5},{5,7},{7,1},{8,10},{10,12},{12... | collective-permute-start | bytes 1179656 | tf_op jit(solution)/shard_map/ppermute | solution.py:45
  128.5 27.4 %all-to-all-start.6 = ((bf16[64,8,256]{2,1,0:T(8,128)(2,1)}), bf16[64,8,256]{2,1,0:T(8,128)(2,1)S(1)}, u32[]{:S(2)}, u32[]{:S(2)}) async-start(bf16[64,8,256]{2,1,0:T(8,128)(2,1)} %broadcast_in_dim.53), calls=%async_computation.6 | async-start | bytes 524288 | tf_op jit(solution)/shard_map/all_to_all | solution.py:37
  136.6 0.8 copy-start.10
  136.6 0.9 copy-start.11
  136.6 1.0 copy-start.12
  139.8 4.7 %collective-permute-start.7 = (bf16[4,96,1024]{2,1,0:T(8,128)(2,1)}, bf16[4,96,1024]{2,1,0:T(8,128)(2,1)S(1)}, u32[]{:S(2)}, u32[]{:S(2)}) collective-permute-start(bf16[4,96,1024]{2,1,0:T(8,128)(2,1)} %join_far.3), channel_id=1, source_target_pairs={{0,1},{1,0},{2,3},{3,2},{4,5},{5,4},{6,7},{7,6},{8,9},{9,8},{10,11... | collective-permute-start | bytes 2359304 | tf_op jit(solution)/shard_map/ppermute | solution.py:49
  143.1 0.7 copy-start.19
  144.5 0.9 copy-start.16
  155.9 0.7 copy-start.14

commit v6 on v5

--- a/solution.py
+++ b/solution.py
@@ -327,31 +327,16 @@
     )(messages, *near, far)
 
 
-def hidden_kernel(pre, row_scale, out):
-    _, units3, _ = pre.shape
-    units = units3 // 3
-    total = jnp.sum(pre[...].astype(F32), axis=0)
+def hidden_grads(pre, row_scale):
+    units = pre.shape[1] // 3
+    total = jnp.sum(pre.astype(F32), axis=0)
     gate_pre, up_pre, back_proj = total[:units], total[units : 2 * units], total[2 * units :]
     sigmoid_gate = jax.nn.sigmoid(gate_pre)
     activated = gate_pre * sigmoid_gate
-    hidden_grad = row_scale[...] * back_proj
+    hidden_grad = row_scale * back_proj
     gate = hidden_grad * sigmoid_gate * (1.0 + gate_pre * (1.0 - sigmoid_gate)) * up_pre
-    up = hidden_grad * activated
-    hidden = activated * up_pre
-    both = jnp.concatenate([gate, up, hidden], axis=0).astype(BF)
-    for t in range(NT):
-        out[t] = both
-
-
-def hidden_grads(pre, row_scale):
-    return pl.pallas_call(
-        hidden_kernel,
-        in_specs=[VMEM] * 2,
-        out_specs=VMEM,
-        out_shape=jax.ShapeDtypeStruct(pre.shape, BF),
-        cost_estimate=cost(20 * pre.size, 6 * pre.size),
-        name="hidden_grads",
-    )(pre, row_scale)
+    both = jnp.concatenate([gate, hidden_grad * activated, activated * up_pre], axis=0)
+    return jnp.broadcast_to(both.astype(BF)[None], pre.shape)
 
 
 def input_grad_kernel(grads, w0, w1, w2, w3, far, out):

time: 161 us -> 157 us (0.975)
  Pallas kernels: 24.6 us -> 22.9 us
    pallas_call x1 -> x0, Pallas kernels: 1.65 us -> none  [hidden_grads(): pl.pallas_call(hidden_kernel, in_specs=[VMEM] * 2, out_specs=VMEM, out_sh...]
    unnamed x40 -> x36, local copies, waits for them, and re-layouts: 7.68 us -> 6.33 us
where the time goes in v6:
time: 157 us; the launch traced here: 155 us
  starting transfers between devices  64.2 us (41%)
  waiting for transfers between devices  33.9 us (22%)
  Pallas kernels  22.9 us (15%)
  blocking collectives  22.2 us (14%)
  local copies, waits for them, and re-layouts  7.49 us (5%)
  other arithmetic  2.61 us (2%)
  between operations  1.61 us (1%)
    all_to_all x5, starting transfers between devices, exchange(): return lax.all_to_all(pieces, axes, 0, 0, tiled=True)  38.6 us
    all_to_all x5, waiting for transfers between devices, exchange(): return lax.all_to_all(pieces, axes, 0, 0, tiled=True)  31.4 us
    all_to_all x2, blocking collectives, exchange(): return lax.all_to_all(pieces, axes, 0, 0, tiled=True)  22.2 us
    ppermute x6, starting transfers between devices, along_x(): return lax.ppermute(array, 'x', [(i, (i + s) % NX) for i in range(NX)])  21.8 us
    unnamed x36, local copies, waits for them, and re-layouts  6.33 us
    pallas_call x2, Pallas kernels, join_far(): pl.pallas_call(join_kernel, grid=(1,), in_specs=[pl.BlockSpec((1, units3,...  4.31 us
    ppermute x2, starting transfers between devices, other_core(): return lax.ppermute(array, 'core', [(0, 1), (1, 0)])  3.82 us
  transfers between devices with their start and end apart: 13, of which 5 were waited for; matrix products, arithmetic and copies ran while one was open for 2% of the time, Pallas kernels for 9%

profile of v6, /device:TPU:6, one launch (start us, length us, event | category | flops | bytes accessed | tf_op | source)
XLA Modules:
  0.0 154.9 jit_solution(3393108087451456029)
XLA Ops:
  1.3 1.9 %pick_rows.1._ = bf16[4,16,1152]{2,1,0:T(8,128)(2,1)} custom-call(s32[1]{0:T(128)} %copy.16.count, s32[1,6]{1,0:T(1,128)} %pos.1, bf16[1,6]{1,0:T(2,128)(2,1)} %router.1, bf16[128,1024]{1,0:T(8,128)(2,1)} %tokens.1, bf16[128,1024]{1,0:T(8,128)(2,1)} %grad_out.3), custom_call_target="tpu_custom_call" | custom-call | flops 4194304 | bytes 524288 | tf_op jit(solution)/shard_map/pick_rows/pallas_call | solution.py:77
  3.2 4.5 %all-to-all-start = ((bf16[4,16,1152]{2,1,0:T(8,128)(2,1)}), bf16[4,16,1152]{2,1,0:T(8,128)(2,1)S(1)}, u32[]{:S(2)}, u32[]{:S(2)}) async-start(bf16[4,16,1152]{2,1,0:T(8,128)(2,1)} %pick_rows.1._), calls=%async_computation | async-start | bytes 294912 | tf_op jit(solution)/shard_map/all_to_all | solution.py:37
  7.7 2.8 %pack_weights.1 = (bf16[2,96,1024]{2,1,0:T(8,128)(2,1)}, bf16[2,96,1024]{2,1,0:T(8,128)(2,1)}, bf16[2,96,1024]{2,1,0:T(8,128)(2,1)}, bf16[2,96,1024]{2,1,0:T(8,128)(2,1)}) custom-call(bf16[32,8192]{1,0:T(8,128)(2,1)} %gate_w.1, bf16[32,8192]{1,0:T(8,128)(2,1)} %up_w.1, bf16[32,8192]{1,0:T(8,128)(2,1)} %down_w.1, bf16[4,16,1152]{2,1,0:T(8,128)(2,1)} %pick_rows.1._), custom_call_target="tpu_custom_call" | custom-call | bytes 3145728 | tf_op jit(solution)/shard_map/pack_weights/pallas_call | solution.py:208
  10.4 6.7 %collective-permute-start = (bf16[2,96,1024]{2,1,0:T(8,128)(2,1)}, bf16[2,96,1024]{2,1,0:T(8,128)(2,1)S(1)}, u32[]{:S(2)}, u32[]{:S(2)}) collective-permute-start(bf16[2,96,1024]{2,1,0:T(8,128)(2,1)} %get-tuple-element.19), channel_id=1, source_target_pairs={{0,2},{2,4},{4,6},{6,0},{1,3},{3,5},{5,7},{7,1},{8,10},{10,12},{12... | collective-permute-start | bytes 1179656 | tf_op jit(solution)/shard_map/ppermute | solution.py:45
  17.1 1.9 %collective-permute-start.1 = (bf16[2,96,1024]{2,1,0:T(8,128)(2,1)}, bf16[2,96,1024]{2,1,0:T(8,128)(2,1)S(1)}, u32[]{:S(2)}, u32[]{:S(2)}) collective-permute-start(bf16[2,96,1024]{2,1,0:T(8,128)(2,1)} %get-tuple-element.20), channel_id=1, source_target_pairs={{0,4},{2,6},{4,0},{6,2},{1,5},{3,7},{5,1},{7,3},{8,12},{10,14},{12... | collective-permute-start | bytes 1179656 | tf_op jit(solution)/shard_map/ppermute | solution.py:45
  19.0 2.8 %collective-permute-start.2 = (bf16[2,96,1024]{2,1,0:T(8,128)(2,1)}, bf16[2,96,1024]{2,1,0:T(8,128)(2,1)S(1)}, u32[]{:S(2)}, u32[]{:S(2)}) collective-permute-start(bf16[2,96,1024]{2,1,0:T(8,128)(2,1)} %get-tuple-element.21), channel_id=1, source_target_pairs={{0,6},{2,0},{4,2},{6,4},{1,7},{3,1},{5,3},{7,5},{8,14},{10,8},{12,... | collective-permute-start | bytes 1179656 | tf_op jit(solution)/shard_map/ppermute | solution.py:45
  21.8 0.0 all-to-all-done.column
  21.8 0.0 copy-start.16
  21.8 0.7 copy-done.16
  22.5 2.0 %select_rows.1 = bf16[16,8,1152]{2,1,0:T(8,128)(2,1)} custom-call(bf16[4,16,1152]{2,1,0:T(8,128)(2,1)} %copy-done.16), custom_call_target="tpu_custom_call" | custom-call | flops 1179648 | bytes 589824 | tf_op jit(solution)/shard_map/select_rows/pallas_call | solution.py:127
  24.5 12.5 %all-to-all-start.1 = ((bf16[16,8,1152]{2,1,0:T(8,128)(2,1)}), bf16[16,8,1152]{2,1,0:T(8,128)(2,1)S(1)}, u32[]{:S(2)}, u32[]{:S(2)}) async-start(bf16[16,8,1152]{2,1,0:T(8,128)(2,1)} %select_rows.1), calls=%async_computation.1 | async-start | bytes 589824 | tf_op jit(solution)/shard_map/all_to_all | solution.py:37
  37.0 0.0 collective-permute-done.refs_1_.w1
  37.0 0.0 copy-start.3
  37.0 0.0 copy-start.5
  37.0 0.0 collective-permute-done.2.refs_3_.w3
  37.0 0.0 copy-start.7
  37.0 0.7 copy-done.3
  37.7 0.1 copy-done.5
  37.9 0.1 copy-done.7
  38.0 2.2 %join_far.2 = bf16[4,96,1024]{2,1,0:T(8,128)(2,1)} custom-call(bf16[2,96,1024]{2,1,0:T(8,128)(2,1)} %get-tuple-element.18.refs_0_.w0, bf16[2,96,1024]{2,1,0:T(8,128)(2,1)} %copy-done.3, bf16[2,96,1024]{2,1,0:T(8,128)(2,1)} %copy-done.5, bf16[2,96,1024]{2,1,0:T(8,128)(2,1)} %copy-done.7), custom_call_target="tpu_custom_call" | custom-call | bytes 1572864 | tf_op jit(solution)/shard_map/join_far/pallas_call | solution.py:228
  40.2 1.9 %collective-permute-start.3 = (bf16[4,96,1024]{2,1,0:T(8,128)(2,1)}, bf16[4,96,1024]{2,1,0:T(8,128)(2,1)S(1)}, u32[]{:S(2)}, u32[]{:S(2)}) collective-permute-start(bf16[4,96,1024]{2,1,0:T(8,128)(2,1)} %join_far.2), channel_id=1, source_target_pairs={{0,1},{1,0},{2,3},{3,2},{4,5},{5,4},{6,7},{7,6},{8,9},{9,8},{10,11... | collective-permute-start | bytes 2359304 | tf_op jit(solution)/shard_map/ppermute | solution.py:49
  42.1 2.5 %collective-permute-done.3._.far = bf16[4,96,1024]{2,1,0:T(8,128)(2,1)S(1)} collective-permute-done((bf16[4,96,1024]{2,1,0:T(8,128)(2,1)}, bf16[4,96,1024]{2,1,0:T(8,128)(2,1)S(1)}, u32[]{:S(2)}, u32[]{:S(2)}) %collective-permute-start.3) | collective-permute-done | bytes 786464 | tf_op jit(solution)/shard_map/ppermute | solution.py:49
  44.5 11.5 %all-to-all-done.1.plane = bf16[16,8,1152]{2,1,0:T(8,128)(2,1)S(1)} async-done(((bf16[16,8,1152]{2,1,0:T(8,128)(2,1)}), bf16[16,8,1152]{2,1,0:T(8,128)(2,1)S(1)}, u32[]{:S(2)}, u32[]{:S(2)}) %all-to-all-start.1) | async-done | bytes 294944 | tf_op jit(solution)/shard_map/all_to_all | solution.py:37
  56.1 0.7 copy-done.13
  56.8 2.3 %compact_rows.1 = bf16[4,72,1024]{2,1,0:T(8,128)(2,1)} custom-call(bf16[16,8,1152]{2,1,0:T(8,128)(2,1)} %copy-done.13, bf16[4,96,1024]{2,1,0:T(8,128)(2,1)} %copy-done), custom_call_target="tpu_custom_call" | custom-call | flops 37748736 | bytes 1179648 | tf_op jit(solution)/shard_map/compact_rows/pallas_call | solution.py:160
  59.1 12.9 %all_to_all.35.messages = bf16[4,72,1024]{2,1,0:T(8,128)(2,1)S(1)} all-to-all(bf16[4,72,1024]{2,1,0:T(8,128)(2,1)} %compact_rows.1), channel_id=1, replica_groups=mesh['y'=4,'z'=16,'x'=4,'core'=2] {'y'}, dimensions={0} | all-to-all | bytes 1179648 | tf_op jit(solution)/shard_map/all_to_all | solution.py:37
  72.2 0.1 gt.16
  72.3 0.1 add.35
  72.4 2.1 %forward.1 = bf16[8,96,128]{2,1,0:T(8,128)(2,1)} custom-call(bf16[4,72,1024]{2,1,0:T(8,128)(2,1)S(1)} %all_to_all.35.messages, bf16[2,96,1024]{2,1,0:T(8,128)(2,1)S(1)} %copy-done.2, bf16[2,96,1024]{2,1,0:T(8,128)(2,1)S(1)} %copy-done.4, bf16[2,96,1024]{2,1,0:T(8,128)(2,1)S(1)} %copy-done.6, bf16[2,96,1024]{2,1,0:T(8,128)(2,1)S(1)} %copy-done.8, ...), custom_call_target="tpu_custom_call" | custom-call | flops 201326592 | bytes 1572864 | tf_op jit(solution)/shard_map/forward/pallas_call | solution.py:318
  74.5 6.2 %all-to-all-start.3 = ((bf16[8,96,128]{2,1,0:T(8,128)(2,1)}), bf16[8,96,128]{2,1,0:T(8,128)(2,1)S(1)}, u32[]{:S(2)}, u32[]{:S(2)}) async-start(bf16[8,96,128]{2,1,0:T(8,128)(2,1)} %forward.1), calls=%async_computation.3 | async-start | bytes 393216 | tf_op jit(solution)/shard_map/all_to_all | solution.py:37
  80.7 0.2 convert_reduce_fusion.1
  80.9 0.1 broadcast_in_dim.28
  81.0 0.1 select_reduce_fusion
  81.1 4.3 %all-to-all-done.3 = bf16[8,96,128]{2,1,0:T(8,128)(2,1)S(1)} async-done(((bf16[8,96,128]{2,1,0:T(8,128)(2,1)}), bf16[8,96,128]{2,1,0:T(8,128)(2,1)S(1)}, u32[]{:S(2)}, u32[]{:S(2)}) %all-to-all-start.3) | async-done | bytes 196640 | tf_op jit(solution)/shard_map/all_to_all | solution.py:37
  85.6 9.2 %all_to_all.36.grads = bf16[8,96,128]{2,1,0:T(8,128)(2,1)S(1)} all-to-all(bf16[8,96,128]{2,1,0:T(8,128)(2,1)S(1)} %broadcast_in_dim.35), channel_id=1, replica_groups=mesh['y'=4,'z'=16,'x'=4,'core'=2] {'x','core'}, dimensions={0} | all-to-all | bytes 393216 | tf_op jit(solution)/shard_map/all_to_all | solution.py:37
  94.8 1.1 input_grad.1
  95.9 8.0 %all-to-all-start.5 = ((bf16[64,8,256]{2,1,0:T(8,128)(2,1)}), bf16[64,8,256]{2,1,0:T(8,128)(2,1)S(1)}, u32[]{:S(2)}, u32[]{:S(2)}) async-start(bf16[64,8,256]{2,1,0:T(8,128)(2,1)} %input_grad.1), calls=%async_computation.5 | async-start | bytes 524288 | tf_op jit(solution)/shard_map/all_to_all | solution.py:37
  103.9 0.1 copy.15.row_scale
  104.0 1.7 %weight_grads.1 = (bf16[2,96,1024]{2,1,0:T(8,128)(2,1)S(1)}, bf16[2,96,1024]{2,1,0:T(8,128)(2,1)S(1)}, bf16[2,96,1024]{2,1,0:T(8,128)(2,1)S(1)}, bf16[2,96,1024]{2,1,0:T(8,128)(2,1)S(1)}) custom-call(bf16[8,96,128]{2,1,0:T(8,128)(2,1)S(1)} %all_to_all.36.grads, bf16[4,72,1024]{2,1,0:T(8,128)(2,1)S(1)} %all_to_all.35.messages, f32[128,1]{1,0:T(8,128)S(1)} %copy.15.row_scale), custom_call_target="tpu_custom_call" | custom-call | flops 201326592 | bytes 1572864 | tf_op jit(solution)/shard_map/weight_grads/pallas_call | solution.py:388
  105.7 0.7 copy-done.9
  106.4 1.9 %collective-permute-start.4 = (bf16[2,96,1024]{2,1,0:T(8,128)(2,1)S(1)}, bf16[2,96,1024]{2,1,0:T(8,128)(2,1)S(1)}, u32[]{:S(2)}, u32[]{:S(2)}) collective-permute-start(bf16[2,96,1024]{2,1,0:T(8,128)(2,1)S(1)} %get-tuple-element.24), channel_id=1, source_target_pairs={{0,6},{2,0},{4,2},{6,4},{1,7},{3,1},{5,3},{7,5},{8,14},{10,8},{12,... | collective-permute-start | bytes 1179656 | tf_op jit(solution)/shard_map/ppermute | solution.py:45
  108.3 5.4 %collective-permute-start.5 = (bf16[2,96,1024]{2,1,0:T(8,128)(2,1)S(1)}, bf16[2,96,1024]{2,1,0:T(8,128)(2,1)S(1)}, u32[]{:S(2)}, u32[]{:S(2)}) collective-permute-start(bf16[2,96,1024]{2,1,0:T(8,128)(2,1)S(1)} %get-tuple-element.25), channel_id=1, source_target_pairs={{0,4},{2,6},{4,0},{6,2},{1,5},{3,7},{5,1},{7,3},{8,12},{10,14},{12... | collective-permute-start | bytes 1179656 | tf_op jit(solution)/shard_map/ppermute | solution.py:45
  113.8 3.1 %collective-permute-start.6 = (bf16[2,96,1024]{2,1,0:T(8,128)(2,1)S(1)}, bf16[2,96,1024]{2,1,0:T(8,128)(2,1)S(1)}, u32[]{:S(2)}, u32[]{:S(2)}) collective-permute-start(bf16[2,96,1024]{2,1,0:T(8,128)(2,1)S(1)} %get-tuple-element.26), channel_id=1, source_target_pairs={{0,2},{2,4},{4,6},{6,0},{1,3},{3,5},{5,7},{7,1},{8,10},{10,12},{12... | collective-permute-start | bytes 1179656 | tf_op jit(solution)/shard_map/ppermute | solution.py:45
  116.9 7.8 %all-to-all-done.5 = bf16[64,8,256]{2,1,0:T(8,128)(2,1)S(1)} async-done(((bf16[64,8,256]{2,1,0:T(8,128)(2,1)}), bf16[64,8,256]{2,1,0:T(8,128)(2,1)S(1)}, u32[]{:S(2)}, u32[]{:S(2)}) %all-to-all-start.5) | async-done | bytes 262176 | tf_op jit(solution)/shard_map/all_to_all | solution.py:37
  124.6 0.1 reduce_sum.51
  124.7 0.7 broadcast_in_dim.36
  125.4 7.4 %all-to-all-start.6 = ((bf16[64,8,256]{2,1,0:T(8,128)(2,1)}), bf16[64,8,256]{2,1,0:T(8,128)(2,1)S(1)}, u32[]{:S(2)}, u32[]{:S(2)}) async-start(bf16[64,8,256]{2,1,0:T(8,128)(2,1)} %broadcast_in_dim.36), calls=%async_computation.6 | async-start | bytes 524288 | tf_op jit(solution)/shard_map/all_to_all | solution.py:37
  132.8 0.0 collective-permute-done.4.refs_1_.in1
  132.9 0.7 copy-done.10
  133.6 0.2 copy-done.11
  133.7 0.1 copy-done.12
  133.9 2.2 %join_far.3 = bf16[4,96,1024]{2,1,0:T(8,128)(2,1)} custom-call(bf16[2,96,1024]{2,1,0:T(8,128)(2,1)} %copy-done.9, bf16[2,96,1024]{2,1,0:T(8,128)(2,1)} %copy-done.10, bf16[2,96,1024]{2,1,0:T(8,128)(2,1)} %copy-done.11, bf16[2,96,1024]{2,1,0:T(8,128)(2,1)} %copy-done.12), custom_call_target="tpu_custom_call" | custom-call | bytes 1572864 | tf_op jit(solution)/shard_map/join_far/pallas_call | solution.py:228
  136.0 1.9 %collective-permute-start.7 = (bf16[4,96,1024]{2,1,0:T(8,128)(2,1)}, bf16[4,96,1024]{2,1,0:T(8,128)(2,1)S(1)}, u32[]{:S(2)}, u32[]{:S(2)}) collective-permute-start(bf16[4,96,1024]{2,1,0:T(8,128)(2,1)} %join_far.3), channel_id=1, source_target_pairs={{0,1},{1,0},{2,3},{3,2},{4,5},{5,4},{6,7},{7,6},{8,9},{9,8},{10,11... | collective-permute-start | bytes 2359304 | tf_op jit(solution)/shard_map/ppermute | solution.py:49
  138.0 0.6 fusion.5
  138.6 0.6 iota_add_fusion
  139.3 0.0 copy-start.17
  139.3 0.6 copy-done.17
  139.9 0.1 select_reduce_fusion.1
  140.0 0.7 fusion.1.owner
  140.7 0.9 copy-done.15
  141.6 2.8 %unpack_grads.1 = (bf16[32,8192]{1,0:T(8,128)(2,1)}, bf16[32,8192]{1,0:T(8,128)(2,1)}, bf16[32,8192]{1,0:T(8,128)(2,1)}) custom-call(bf16[2,96,1024]{2,1,0:T(8,128)(2,1)} %copy-done.9, bf16[2,96,1024]{2,1,0:T(8,128)(2,1)} %copy-done.10, bf16[2,96,1024]{2,1,0:T(8,128)(2,1)} %copy-done.11, bf16[2,96,1024]{2,1,0:T(8,128)(2,1)} %copy-done.12, ...), custom_call_target="tpu_custom_call" | custom-call | bytes 3145728 | tf_op jit(solution)/shard_map/unpack_grads/pallas_call | solution.py:252
  144.4 7.8 %all-to-all-done.6.blocks = bf16[64,8,256]{2,1,0:T(8,128)(2,1)S(1)} async-done(((bf16[64,8,256]{2,1,0:T(8,128)(2,1)}), bf16[64,8,256]{2,1,0:T(8,128)(2,1)S(1)}, u32[]{:S(2)}, u32[]{:S(2)}) %all-to-all-start.6) | async-done | bytes 262176 | tf_op jit(solution)/shard_map/all_to_all | solution.py:37
  152.2 0.7 copy-done.14
  152.9 2.0 %finish.1 = (bf16[128,1024]{1,0:T(8,128)(2,1)}, f32[128,1024]{1,0:T(8,128)}) custom-call(bf16[64,8,256]{2,1,0:T(8,128)(2,1)} %copy-done.14, bf16[128,128]{1,0:T(8,128)(2,1)} %fusion.1.owner, bf16[128,1024]{1,0:T(8,128)(2,1)} %grad_out.3), custom_call_target="tpu_custom_call" | custom-call | flops 33554432 | bytes 1310720 | tf_op jit(solution)/shard_map/finish/pallas_call | solution.py:414
  (33 shorter events, 0.2 us)
Async XLA Ops:
  3.2 18.6 %all-to-all-start = ((bf16[4,16,1152]{2,1,0:T(8,128)(2,1)}), bf16[4,16,1152]{2,1,0:T(8,128)(2,1)S(1)}, u32[]{:S(2)}, u32[]{:S(2)}) async-start(bf16[4,16,1152]{2,1,0:T(8,128)(2,1)} %pick_rows.1._), calls=%async_computation | async-start | bytes 294912 | tf_op jit(solution)/shard_map/all_to_all | solution.py:37
  10.4 26.6 %collective-permute-start = (bf16[2,96,1024]{2,1,0:T(8,128)(2,1)}, bf16[2,96,1024]{2,1,0:T(8,128)(2,1)S(1)}, u32[]{:S(2)}, u32[]{:S(2)}) collective-permute-start(bf16[2,96,1024]{2,1,0:T(8,128)(2,1)} %get-tuple-element.19), channel_id=1, source_target_pairs={{0,2},{2,4},{4,6},{6,0},{1,3},{3,5},{5,7},{7,1},{8,10},{10,12},{12... | collective-permute-start | bytes 1179656 | tf_op jit(solution)/shard_map/ppermute | solution.py:45
  17.1 19.9 %collective-permute-start.1 = (bf16[2,96,1024]{2,1,0:T(8,128)(2,1)}, bf16[2,96,1024]{2,1,0:T(8,128)(2,1)S(1)}, u32[]{:S(2)}, u32[]{:S(2)}) collective-permute-start(bf16[2,96,1024]{2,1,0:T(8,128)(2,1)} %get-tuple-element.20), channel_id=1, source_target_pairs={{0,4},{2,6},{4,0},{6,2},{1,5},{3,7},{5,1},{7,3},{8,12},{10,14},{12... | collective-permute-start | bytes 1179656 | tf_op jit(solution)/shard_map/ppermute | solution.py:45
  19.0 18.0 %collective-permute-start.2 = (bf16[2,96,1024]{2,1,0:T(8,128)(2,1)}, bf16[2,96,1024]{2,1,0:T(8,128)(2,1)S(1)}, u32[]{:S(2)}, u32[]{:S(2)}) collective-permute-start(bf16[2,96,1024]{2,1,0:T(8,128)(2,1)} %get-tuple-element.21), channel_id=1, source_target_pairs={{0,6},{2,0},{4,2},{6,4},{1,7},{3,1},{5,3},{7,5},{8,14},{10,8},{12,... | collective-permute-start | bytes 1179656 | tf_op jit(solution)/shard_map/ppermute | solution.py:45
  21.8 0.7 copy-start.16
  24.5 31.6 %all-to-all-start.1 = ((bf16[16,8,1152]{2,1,0:T(8,128)(2,1)}), bf16[16,8,1152]{2,1,0:T(8,128)(2,1)S(1)}, u32[]{:S(2)}, u32[]{:S(2)}) async-start(bf16[16,8,1152]{2,1,0:T(8,128)(2,1)} %select_rows.1), calls=%async_computation.1 | async-start | bytes 589824 | tf_op jit(solution)/shard_map/all_to_all | solution.py:37
  37.0 0.7 copy-start.3
  37.0 0.9 copy-start.5
  37.0 1.0 copy-start.7
  40.2 4.4 %collective-permute-start.3 = (bf16[4,96,1024]{2,1,0:T(8,128)(2,1)}, bf16[4,96,1024]{2,1,0:T(8,128)(2,1)S(1)}, u32[]{:S(2)}, u32[]{:S(2)}) collective-permute-start(bf16[4,96,1024]{2,1,0:T(8,128)(2,1)} %join_far.2), channel_id=1, source_target_pairs={{0,1},{1,0},{2,3},{3,2},{4,5},{5,4},{6,7},{7,6},{8,9},{9,8},{10,11... | collective-permute-start | bytes 2359304 | tf_op jit(solution)/shard_map/ppermute | solution.py:49
  44.5 11.5 %copy-start = (bf16[4,96,1024]{2,1,0:T(8,128)(2,1)}, bf16[4,96,1024]{2,1,0:T(8,128)(2,1)S(1)}, u32[]{:S(2)}) copy-start(bf16[4,96,1024]{2,1,0:T(8,128)(2,1)S(1)} %collective-permute-done.3._.far) | copy-start | bytes 2359300
  56.1 0.7 copy-start.13
  56.8 15.6 %copy-start.4 = (bf16[2,96,1024]{2,1,0:T(8,128)(2,1)S(1)}, bf16[2,96,1024]{2,1,0:T(8,128)(2,1)}, u32[]{:S(2)}) copy-start(bf16[2,96,1024]{2,1,0:T(8,128)(2,1)} %copy-done.3) | copy-start | bytes 1179652
  56.8 15.6 %copy-start.6 = (bf16[2,96,1024]{2,1,0:T(8,128)(2,1)S(1)}, bf16[2,96,1024]{2,1,0:T(8,128)(2,1)}, u32[]{:S(2)}) copy-start(bf16[2,96,1024]{2,1,0:T(8,128)(2,1)} %copy-done.5) | copy-start | bytes 1179652
  56.8 15.6 %copy-start.8 = (bf16[2,96,1024]{2,1,0:T(8,128)(2,1)S(1)}, bf16[2,96,1024]{2,1,0:T(8,128)(2,1)}, u32[]{:S(2)}) copy-start(bf16[2,96,1024]{2,1,0:T(8,128)(2,1)} %copy-done.7) | copy-start | bytes 1179652
  59.1 13.2 %copy-start.1 = (bf16[4,96,1024]{2,1,0:T(8,128)(2,1)S(1)}, bf16[4,96,1024]{2,1,0:T(8,128)(2,1)}, u32[]{:S(2)}) copy-start(bf16[4,96,1024]{2,1,0:T(8,128)(2,1)} %copy-done) | copy-start | bytes 2359300
  59.1 13.2 %copy-start.2 = (bf16[2,96,1024]{2,1,0:T(8,128)(2,1)S(1)}, bf16[2,96,1024]{2,1,0:T(8,128)(2,1)}, u32[]{:S(2)}) copy-start(bf16[2,96,1024]{2,1,0:T(8,128)(2,1)} %get-tuple-element.18.refs_0_.w0) | copy-start | bytes 1179652
  74.5 11.0 %all-to-all-start.3 = ((bf16[8,96,128]{2,1,0:T(8,128)(2,1)}), bf16[8,96,128]{2,1,0:T(8,128)(2,1)S(1)}, u32[]{:S(2)}, u32[]{:S(2)}) async-start(bf16[8,96,128]{2,1,0:T(8,128)(2,1)} %forward.1), calls=%async_computation.3 | async-start | bytes 393216 | tf_op jit(solution)/shard_map/all_to_all | solution.py:37
  95.9 28.8 %all-to-all-start.5 = ((bf16[64,8,256]{2,1,0:T(8,128)(2,1)}), bf16[64,8,256]{2,1,0:T(8,128)(2,1)S(1)}, u32[]{:S(2)}, u32[]{:S(2)}) async-start(bf16[64,8,256]{2,1,0:T(8,128)(2,1)} %input_grad.1), calls=%async_computation.5 | async-start | bytes 524288 | tf_op jit(solution)/shard_map/all_to_all | solution.py:37
  105.7 0.8 copy-start.9
  106.4 26.4 %collective-permute-start.4 = (bf16[2,96,1024]{2,1,0:T(8,128)(2,1)S(1)}, bf16[2,96,1024]{2,1,0:T(8,128)(2,1)S(1)}, u32[]{:S(2)}, u32[]{:S(2)}) collective-permute-start(bf16[2,96,1024]{2,1,0:T(8,128)(2,1)S(1)} %get-tuple-element.24), channel_id=1, source_target_pairs={{0,6},{2,0},{4,2},{6,4},{1,7},{3,1},{5,3},{7,5},{8,14},{10,8},{12,... | collective-permute-start | bytes 1179656 | tf_op jit(solution)/shard_map/ppermute | solution.py:45
  108.3 24.5 %collective-permute-start.5 = (bf16[2,96,1024]{2,1,0:T(8,128)(2,1)S(1)}, bf16[2,96,1024]{2,1,0:T(8,128)(2,1)S(1)}, u32[]{:S(2)}, u32[]{:S(2)}) collective-permute-start(bf16[2,96,1024]{2,1,0:T(8,128)(2,1)S(1)} %get-tuple-element.25), channel_id=1, source_target_pairs={{0,4},{2,6},{4,0},{6,2},{1,5},{3,7},{5,1},{7,3},{8,12},{10,14},{12... | collective-permute-start | bytes 1179656 | tf_op jit(solution)/shard_map/ppermute | solution.py:45
  113.8 19.1 %collective-permute-start.6 = (bf16[2,96,1024]{2,1,0:T(8,128)(2,1)S(1)}, bf16[2,96,1024]{2,1,0:T(8,128)(2,1)S(1)}, u32[]{:S(2)}, u32[]{:S(2)}) collective-permute-start(bf16[2,96,1024]{2,1,0:T(8,128)(2,1)S(1)} %get-tuple-element.26), channel_id=1, source_target_pairs={{0,2},{2,4},{4,6},{6,0},{1,3},{3,5},{5,7},{7,1},{8,10},{10,12},{12... | collective-permute-start | bytes 1179656 | tf_op jit(solution)/shard_map/ppermute | solution.py:45
  125.4 26.8 %all-to-all-start.6 = ((bf16[64,8,256]{2,1,0:T(8,128)(2,1)}), bf16[64,8,256]{2,1,0:T(8,128)(2,1)S(1)}, u32[]{:S(2)}, u32[]{:S(2)}) async-start(bf16[64,8,256]{2,1,0:T(8,128)(2,1)} %broadcast_in_dim.36), calls=%async_computation.6 | async-start | bytes 524288 | tf_op jit(solution)/shard_map/all_to_all | solution.py:37
  132.8 0.8 copy-start.10
  132.9 0.9 copy-start.11
  132.9 1.0 copy-start.12
  136.0 4.7 %collective-permute-start.7 = (bf16[4,96,1024]{2,1,0:T(8,128)(2,1)}, bf16[4,96,1024]{2,1,0:T(8,128)(2,1)S(1)}, u32[]{:S(2)}, u32[]{:S(2)}) collective-permute-start(bf16[4,96,1024]{2,1,0:T(8,128)(2,1)} %join_far.3), channel_id=1, source_target_pairs={{0,1},{1,0},{2,3},{3,2},{4,5},{5,4},{6,7},{7,6},{8,9},{9,8},{10,11... | collective-permute-start | bytes 2359304 | tf_op jit(solution)/shard_map/ppermute | solution.py:49
  139.3 0.7 copy-start.17
  140.7 0.9 copy-start.15
  152.2 0.7 copy-start.14
